TPU v7x, 32 devices: a whole 2x2x4 slice. The times are simulated.
32 devices in a mesh: tile: 8 (over z, y), filt: 2 (over x), mc: 2 (over core).
Axes of the slice: x: 2, y: 2, z: 4, core: 2. Of those that a mesh axis runs over, the one named last changes fastest.
Arguments:
- sky_mean: float32 [8, 6, 256, 256], P('tile', 'filt'), may hold values from -6 to 6
- sky_log_scale: float32 [8, 6, 256, 256], P('tile', 'filt'), may hold values from -2.5 to -0.5
- noise_draw: bfloat16 [2, 8, 6, 256, 256], P('mc', 'tile', 'filt'), may hold values from -5 to 5
- observed: bfloat16 [8, 6, 256, 256], P('tile', 'filt'), may hold values from -6 to 6
- inv_var: bfloat16 [8, 6, 256, 256], P('tile', 'filt'), may hold values from 0.5 to 4
- intersections: int32 [8, 6, 3, 9], replicated, may hold values from -128 to 128, as said below
- counts: int32 [8, 6], replicated, may hold values from 1 to 3, as said below
- kernels: float32 [8, 2, 25], replicated, may hold values from 0 to 0.08
- psf_coeffs: bfloat16 [8, 6, 6, 3], replicated, may hold values from -0.5 to 1
- prior_prec: float32 [6, 6], replicated, as said below
Outputs:
- grad_mu: float32 [8, 6, 256, 256], P('tile', 'filt')
- grad_rho: float32 [8, 6, 256, 256], P('tile', 'filt')
Inputs may be any that keep to these rules, and one draw needn't show every extreme that they name: `intersections`: for tile t and filter f the first counts[t, f] slots name distinct exposures within 2 of t; later slots hold values in the same ranges and are not used. Offsets lie in -128 .. 128 and kernel indices in 0 .. 7. counts[t, f] never exceeds the number of exposures within 2 of tile t. `prior_prec`: Symmetric; each diagonal entry exceeds the sum of the magnitudes of the other entries of its row.
All inputs are finite; a program needn't handle non-finite values.
Results may differ from a plain program's by a relative error of at most 0.00086.
Values may be sent and summed in bfloat16 or wider, within the bound.
No kernel may reach another device: no remote copies, remote signals or barrier semaphores. Data moves between devices by JAX's collectives and lax.ppermute only.
A program may use at most 64 MiB of HBM per device.

v0:
```python
import functools

import jax
import jax.numpy as jnp
from jax import lax
from jax.experimental import pallas as pl
from jax.experimental.pallas import tpu as pltpu
from jax.sharding import PartitionSpec as P

NB = 6
K = 3
REACH = 2
HEAD = 3
VMEM_BYTES = 48 * 1024 * 1024
VMEM = pl.BlockSpec(memory_space=pltpu.VMEM)
SMEM = pl.BlockSpec(memory_space=pltpu.SMEM)


def shifted(x, axis, by):
    length = lax.axis_size(axis)
    pairs = [(i, i + by) for i in range(length) if 0 <= i + by < length]
    return lax.ppermute(x, axis, pairs)


def rotated(x, axis, by):
    length = lax.axis_size(axis)
    return lax.ppermute(x, axis, [(i, (i + by) % length) for i in range(length)])


def tap_rows(kernels, side, flip):
    half = (kernels.shape[1] - 1) // 2
    taps = kernels[:, ::-1] if flip else kernels
    zeros = jnp.zeros((kernels.shape[0], side - 2 * half - 1), kernels.dtype)
    return jnp.concatenate([taps[:, half:], zeros, taps[:, :half]], 1)


def build_basis(taps_ref, basis_ref, half):
    count, side = taps_ref.shape[0], taps_ref.shape[1]
    apart = lax.broadcasted_iota(jnp.int32, (side, side), 0) - lax.broadcasted_iota(
        jnp.int32, (side, side), 1
    )
    band = jnp.abs(apart) <= half

    def one(n, carry):
        rows = jnp.broadcast_to(taps_ref[pl.ds(n, 1), :], (side, side))
        turned = pltpu.roll(rows, 0, 1, stride=1, stride_axis=0)
        basis_ref[n] = jnp.where(band, turned, 0.0).astype(jnp.bfloat16)
        return carry

    lax.fori_loop(0, count, one, 0)


def find_slot(inter_ref, counts_ref, tile, expo, filt, sizes):
    tiles, filters, fields = sizes
    inside = (tile >= 0) & (tile < tiles) & (expo >= 0) & (expo < tiles)
    pair = jnp.clip(tile, 0, tiles - 1) * filters + filt
    live = counts_ref[pair]
    base = jnp.int32(0)
    found = jnp.int32(0)
    for q in range(K):
        here = (pair * K + q) * fields
        hit = (q < live) & (inter_ref[here] == expo) & inside
        base = jnp.where(hit, here, base)
        found = jnp.where(hit, 1, found)
    return found, base


def weight(coeff_ref, at, row_centred, col_centred):
    return (coeff_ref[at] + coeff_ref[at + 1] * row_centred) + coeff_ref[at + 2] * col_centred


def centred_axes(side, oy, ox):
    rows = lax.broadcasted_iota(jnp.int32, (side, 1), 0) + oy
    cols = lax.broadcasted_iota(jnp.int32, (1, side), 1) + ox
    return (
        (2 * rows + 1 - side).astype(jnp.float32) / side,
        (2 * cols + 1 - side).astype(jnp.float32) / side,
    )


def diagonal(side, by):
    apart = lax.broadcasted_iota(jnp.int32, (side, side), 1) - lax.broadcasted_iota(
        jnp.int32, (side, side), 0
    )
    return (apart == by).astype(jnp.float32).astype(jnp.bfloat16)


def dot(a, b):
    return jnp.dot(a, b, preferred_element_type=jnp.float32)


def add_contribution(inter_ref, coeff_ref, basis_ref, base, coeff_base, image, pred_ref, f):
    side = image.shape[0]
    kinds = basis_ref.shape[0] // 2
    oy, ox = inter_ref[base + 1], inter_ref[base + 2]
    row_centred, col_centred = centred_axes(side, oy, ox)
    total = jnp.zeros((side, side), jnp.float32)
    for b in range(NB):
        k = inter_ref[base + HEAD + b]
        half_blur = dot(basis_ref[k], image).astype(jnp.bfloat16)
        blurred = dot(half_blur, basis_ref[kinds + k])
        total = total + weight(coeff_ref, coeff_base + 3 * b, row_centred, col_centred) * blurred
    across = dot(total.astype(jnp.bfloat16), diagonal(side, ox)).astype(jnp.bfloat16)
    pred_ref[f] = pred_ref[f] + dot(diagonal(side, -oy), across)


def add_adjoint(inter_ref, coeff_ref, basis_ref, base, coeff_base, image, grad_ref, f):
    side = image.shape[0]
    kinds = basis_ref.shape[0] // 2
    oy, ox = inter_ref[base + 1], inter_ref[base + 2]
    row_centred, col_centred = centred_axes(side, oy, ox)
    across = dot(image, diagonal(side, -ox)).astype(jnp.bfloat16)
    moved = dot(diagonal(side, oy), across)
    total = jnp.zeros((side, side), jnp.float32)
    for b in range(NB):
        k = inter_ref[base + HEAD + b]
        w = weight(coeff_ref, coeff_base + 3 * b, row_centred, col_centred)
        back_half = dot(basis_ref[k], (w * moved).astype(jnp.bfloat16)).astype(jnp.bfloat16)
        total = total + dot(back_half, basis_ref[kinds + k])
    grad_ref[f] = grad_ref[f] + total


def source_of(own, move):
    distance, parity = move
    return own + jnp.where(lax.rem(own // distance, 2) == parity, distance, -distance)


def flipped(x, axis, move):
    distance, parity = move
    length = lax.axis_size(axis)
    firsts = [i for i in range(length - distance) if (i // distance) % 2 == parity]
    pairs = [(i, i + distance) for i in firsts] + [(i + distance, i) for i in firsts]
    return lax.ppermute(x, axis, pairs)


def forward_slots(sizes, move, inter_ref, counts_ref, coeff_ref, basis_ref, image_ref, pred_ref):
    tiles, filters, fields = sizes
    local = image_ref.shape[0]
    expo = lax.axis_index("tile")
    tile = expo if move is None else source_of(expo, move)
    first = lax.axis_index("filt") * local

    def one(f, carry):
        found, base = find_slot(inter_ref, counts_ref, tile, expo, first + f, sizes)

        @pl.when(found == 1)
        def _():
            coeff_base = (expo * filters + first + f) * NB * 3
            add_contribution(
                inter_ref, coeff_ref, basis_ref, base, coeff_base, image_ref[f], pred_ref, f
            )

        return carry

    lax.fori_loop(0, local, one, 0)


def backward_slots(sizes, move, inter_ref, counts_ref, coeff_ref, basis_ref, image_ref, grad_ref):
    tiles, filters, fields = sizes
    local = image_ref.shape[0]
    tile = lax.axis_index("tile")
    expo = tile if move is None else source_of(tile, move)
    first = lax.axis_index("filt") * local

    def one(f, carry):
        found, base = find_slot(inter_ref, counts_ref, tile, expo, first + f, sizes)

        @pl.when(found == 1)
        def _():
            coeff_base = (expo * filters + first + f) * NB * 3
            add_adjoint(
                inter_ref, coeff_ref, basis_ref, base, coeff_base, image_ref[f], grad_ref, f
            )

        return carry

    lax.fori_loop(0, local, one, 0)


def forward_own(sizes, half, inter_ref, counts_ref, coeff_ref, taps_ref, image_ref, *outs):
    pred_ref, basis_ref = outs
    build_basis(taps_ref, basis_ref, half)
    pred_ref[...] = jnp.zeros_like(pred_ref)
    forward_slots(sizes, None, inter_ref, counts_ref, coeff_ref, basis_ref, image_ref, pred_ref)


def forward_next(
    sizes, move, inter_ref, counts_ref, coeff_ref, basis_ref, image_ref, before_ref, pred_ref
):
    del before_ref
    forward_slots(sizes, move, inter_ref, counts_ref, coeff_ref, basis_ref, image_ref, pred_ref)


def forward_last(
    sizes,
    move,
    inter_ref,
    counts_ref,
    coeff_ref,
    basis_ref,
    image_ref,
    before_ref,
    observed_ref,
    inv_ref,
    pred_ref,
    resid_ref,
):
    del before_ref
    forward_slots(sizes, move, inter_ref, counts_ref, coeff_ref, basis_ref, image_ref, pred_ref)
    for f in range(observed_ref.shape[0]):
        gap = observed_ref[f].astype(jnp.float32) - pred_ref[f]
        resid_ref[f] = (inv_ref[f].astype(jnp.float32) * gap).astype(jnp.bfloat16)


def backward_own(
    sizes,
    half,
    samples,
    inter_ref,
    counts_ref,
    coeff_ref,
    prec_ref,
    taps_ref,
    image_ref,
    sample_ref,
    scale_ref,
    *refs,
):
    noises, refs = refs[:samples], refs[samples:]
    turns, refs = refs[-samples:], refs[:-samples]
    others, (grad_ref, basis_ref) = refs[:-2], refs[-2:]
    tiles, filters, fields = sizes
    local, side = sample_ref.shape[0], sample_ref.shape[1]
    part = lax.axis_index("filt")
    parts = filters // local
    first = part * local
    build_basis(taps_ref, basis_ref, half)
    for noise_ref, turn_ref in zip(noises, turns):
        turn_ref[...] = scale_ref[...] * noise_ref[...].astype(jnp.float32)
    for f in range(local):
        prior = jnp.zeros((side, side), jnp.float32)
        row = (first + f) * filters
        for g in range(local):
            prior = prior + prec_ref[row + first + g] * sample_ref[g]
        for r in range(1, parts):
            source = lax.rem(part + parts - r, parts) * local
            for g in range(local):
                prior = prior + prec_ref[row + source + g] * others[r - 1][g].astype(jnp.float32)
        grad_ref[f] = -prior
    backward_slots(sizes, None, inter_ref, counts_ref, coeff_ref, basis_ref, image_ref, grad_ref)


def backward_next(
    sizes, move, inter_ref, counts_ref, coeff_ref, basis_ref, image_ref, before_ref, grad_ref
):
    del before_ref
    backward_slots(sizes, move, inter_ref, counts_ref, coeff_ref, basis_ref, image_ref, grad_ref)


def body(
    sky_mean,
    sky_log_scale,
    noise_draw,
    observed,
    inv_var,
    intersections,
    counts,
    kernels,
    psf_coeffs,
    prior_prec,
):
    side = sky_mean.shape[2]
    local = sky_mean.shape[1]
    tiles, filters = counts.shape
    sizes = (tiles, filters, intersections.shape[3])
    half = (kernels.shape[2] - 1) // 2
    kinds = kernels.shape[0]
    started = [(d, parity) for d in range(1, REACH + 1) for parity in (0, 1)]
    used = [(1, 0)] + [m for m in started if m[0] > 1] + [(1, 1)]
    samples = lax.axis_size("mc")
    parts = lax.axis_size("filt")

    scale_map = jnp.exp(sky_log_scale[0])
    noise = noise_draw[0, 0]
    eps_float = noise.astype(jnp.float32)
    sample = sky_mean[0] + scale_map * eps_float
    sample_b = sample.astype(jnp.bfloat16)
    inter_flat = intersections.reshape(-1)
    counts_flat = counts.reshape(-1)
    coeff_flat = psf_coeffs.astype(jnp.float32).reshape(-1)
    prec_flat = prior_prec.reshape(-1)
    tables = (inter_flat, counts_flat, coeff_flat)
    rows_plain = tap_rows(kernels[:, 0], side, True)
    rows_trans = tap_rows(kernels[:, 0], side, False)
    cols_plain = tap_rows(kernels[:, 1], side, True)
    cols_trans = tap_rows(kernels[:, 1], side, False)
    taps_forward = jnp.concatenate([rows_plain, cols_trans], 0)
    taps_backward = jnp.concatenate([rows_trans, cols_plain], 0)

    image_f32 = jax.ShapeDtypeStruct((local, side, side), jnp.float32)
    image_b16 = jax.ShapeDtypeStruct((local, side, side), jnp.bfloat16)
    basis_type = jax.ShapeDtypeStruct((2 * kinds, side, side), jnp.bfloat16)
    cost = pl.CostEstimate(
        flops=2 * NB * 4 * side**3, bytes_accessed=8 * local * side * side, transcendentals=0
    )

    def call(kernel, name, outs, smem, vmem, aliases={}):
        return pl.pallas_call(
            kernel,
            out_shape=outs,
            in_specs=[SMEM] * len(smem) + [VMEM] * len(vmem),
            out_specs=[VMEM] * len(outs),
            input_output_aliases=aliases,
            compiler_params=pltpu.CompilerParams(vmem_limit_bytes=VMEM_BYTES),
            cost_estimate=cost,
            name=name,
        )(*smem, *vmem)

    near = {move: flipped(sample_b, "tile", move) for move in started}
    other_samples = [rotated(sample_b, "filt", r) for r in range(1, parts)]
    other_noise = [rotated(noise, "mc", r) for r in range(1, samples)]
    pred, basis = call(
        functools.partial(forward_own, sizes, half),
        "forward_own",
        [image_f32, basis_type],
        tables,
        (taps_forward, sample_b),
    )
    for move in used[:-1]:
        (pred,) = call(
            functools.partial(forward_next, sizes, move),
            f"forward_{move[0]}_{move[1]}",
            [image_f32],
            tables,
            (basis, near[move], pred),
            {len(tables) + 2: 0},
        )
    _, residual = call(
        functools.partial(forward_last, sizes, used[-1]),
        "forward_last",
        [image_f32, image_b16],
        tables,
        (basis, near[used[-1]], pred, observed[0], inv_var[0]),
        {len(tables) + 2: 0},
    )
    near_resid = {move: flipped(residual, "tile", move) for move in started}
    grad, basis, turn, *other_turns = call(
        functools.partial(backward_own, sizes, half, samples),
        "backward_own",
        [image_f32, basis_type] + [image_f32] * samples,
        tables + (prec_flat,),
        (taps_backward, residual, sample, scale_map, noise, *other_noise, *other_samples),
    )
    for move in used:
        (grad,) = call(
            functools.partial(backward_next, sizes, move),
            f"backward_{move[0]}_{move[1]}",
            [image_f32],
            tables,
            (basis, near_resid[move], grad),
            {len(tables) + 2: 0},
        )
    mean_sum = grad
    scale_sum = grad * turn
    for r in range(1, samples):
        other_grad = rotated(grad, "mc", r)
        mean_sum = mean_sum + other_grad
        scale_sum = scale_sum + other_grad * other_turns[r - 1]
    return ((mean_sum / samples)[None], (scale_sum / samples + 1.0)[None])

def solution(mesh):
    placed = (
        P("tile", "filt", None, None),
        P("tile", "filt", None, None),
        P("mc", "tile", "filt", None, None),
        P("tile", "filt", None, None),
        P("tile", "filt", None, None),
        P(),
        P(),
        P(),
        P(),
        P(),
    )
    return jax.shard_map(
        body,
        mesh=mesh,
        in_specs=placed,
        out_specs=(P("tile", "filt", None, None), P("tile", "filt", None, None)),
        check_vma=False,
    )
```

profile of v0, /device:TPU:17, one launch (start us, length us, event | category | flops | bytes accessed | tf_op | source)
XLA Modules:
  0.0 63.0 jit_solution(4947522296946111609)
XLA Ops:
  0.7 1.7 %fusion.6 = (bf16[3,256,256]{2,1,0:T(8,128)(2,1)S(1)}, f32[3,256,256]{2,1,0:T(8,128)S(1)}) fusion(bf16[1,1,3,256,256]{4,3,2,1,0:T(8,128)(2,1)} %param.12, f32[1,3,256,256]{3,2,1,0:T(8,128)} %param.11, f32[1,3,256,256]{3,2,1,0:T(8,128)} %param.10), kind=kLoop, calls=%fused_computation.14 | loop fusion | flops 786432 | bytes 3145728 | tf_op jit(solution)/shard_map/convert_element_type | solution.py:287
  2.4 1.3 %collective-permute-start.3 = (bf16[3,256,256]{2,1,0:T(8,128)(2,1)S(1)}, bf16[3,256,256]{2,1,0:T(8,128)(2,1)S(1)}, u32[]{:S(2)}, u32[]{:S(2)}) collective-permute-start(bf16[3,256,256]{2,1,0:T(8,128)(2,1)S(1)} %get-tuple-element.16.image_ref), channel_id=1, source_target_pairs={{0,4},{8,12},{16,20},{24,28},{4,0},{12,8},{20,16},{28,24},{1,5},{9... | collective-permute-start | bytes 1179656 | tf_op jit(solution)/shard_map/ppermute | solution.py:133
  3.7 1.3 %collective-permute-start.2 = (bf16[3,256,256]{2,1,0:T(8,128)(2,1)S(1)}, bf16[3,256,256]{2,1,0:T(8,128)(2,1)S(1)}, u32[]{:S(2)}, u32[]{:S(2)}) collective-permute-start(bf16[3,256,256]{2,1,0:T(8,128)(2,1)S(1)} %get-tuple-element.16.image_ref), channel_id=1, source_target_pairs={{0,8},{4,12},{16,24},{20,28},{8,0},{12,4},{24,16},{28,20},{1,9},{5... | collective-permute-start | bytes 1179656 | tf_op jit(solution)/shard_map/ppermute | solution.py:133
  5.0 1.9 %collective-permute-start.1 = (bf16[3,256,256]{2,1,0:T(8,128)(2,1)S(1)}, bf16[3,256,256]{2,1,0:T(8,128)(2,1)S(1)}, u32[]{:S(2)}, u32[]{:S(2)}) collective-permute-start(bf16[3,256,256]{2,1,0:T(8,128)(2,1)S(1)} %get-tuple-element.16.image_ref), channel_id=1, source_target_pairs={{8,16},{12,20},{16,8},{20,12},{9,17},{13,21},{17,9},{21,13},{10,18... | collective-permute-start | bytes 1179656 | tf_op jit(solution)/shard_map/ppermute | solution.py:133
  6.9 3.3 %collective-permute-start = (bf16[3,256,256]{2,1,0:T(8,128)(2,1)S(1)}, bf16[3,256,256]{2,1,0:T(8,128)(2,1)S(1)}, u32[]{:S(2)}, u32[]{:S(2)}) collective-permute-start(bf16[3,256,256]{2,1,0:T(8,128)(2,1)S(1)} %get-tuple-element.16.image_ref), channel_id=1, source_target_pairs={{4,8},{12,16},{20,24},{8,4},{16,12},{24,20},{5,9},{13,17},{21,25},... | collective-permute-start | bytes 1179656 | tf_op jit(solution)/shard_map/ppermute | solution.py:133
  10.2 1.3 %collective-permute-start.5 = (bf16[3,256,256]{2,1,0:T(8,128)(2,1)S(1)}, bf16[3,256,256]{2,1,0:T(8,128)(2,1)}, u32[]{:S(2)}, u32[]{:S(2)}) collective-permute-start(bf16[3,256,256]{2,1,0:T(8,128)(2,1)S(1)} %get-tuple-element.16.image_ref), channel_id=1, source_target_pairs={{0,2},{2,0},{1,3},{3,1},{4,6},{6,4},{5,7},{7,5},{8,10},{10,8},{9,1... | collective-permute-start | bytes 1179656 | tf_op jit(solution)/shard_map/ppermute | solution.py:27
  11.9 0.4 copy.23
  12.3 0.2 reshape.25.coeff_ref
  12.6 0.2 reshape.19.inter_ref
  12.9 0.7 %fusion.3 = (f32[16,256]{1,0:T(8,128)S(1)}, f32[16,256]{1,0:T(8,128)}) fusion(f32[8,231]{1,0:T(8,128)S(1)} %broadcast.8, f32[8,12]{1,0:T(8,128)S(1)} %get-tuple-element.35, f32[8,13]{1,0:T(8,128)S(1)} %get-tuple-element.33, f32[8,12]{1,0:T(8,128)S(1)} %slice.55, f32[8,13]{1,0:T(8,128)S(1)} %slice.53, f32[8,12]{1,0:T(8,128)S(1)} %slice.51, ...), kind=kLoop, calls=%fused_computation.11 | loop fusion | flops 40960 | bytes 43360 | tf_op jit(solution)/shard_map/concatenate | solution.py:297
  13.6 4.4 %forward_own.1 = (f32[3,256,256]{2,1,0:T(8,128)S(1)}, bf16[16,256,256]{2,1,0:T(8,128)(2,1)S(1)}) custom-call(s32[1296]{0:T(1024)S(1)} %reshape.19.inter_ref, s32[48]{0:T(128)S(1)} %reshape.20.counts_ref, f32[864]{0:T(1024)S(1)} %reshape.25.coeff_ref, f32[16,256]{1,0:T(8,128)S(1)} %get-tuple-element.20.taps_ref, ...), custom_call_target="tpu_custom_call" | custom-call | flops 805306368 | bytes 1572864 | tf_op jit(solution)/shard_map/forward_own/pallas_call | solution.py:308
  18.0 2.1 %collective-permute-start.4 = (bf16[3,256,256]{2,1,0:T(8,128)(2,1)S(1)}, bf16[3,256,256]{2,1,0:T(8,128)(2,1)}, u32[]{:S(2)}, u32[]{:S(2)}) collective-permute-start(bf16[3,256,256]{2,1,0:T(8,128)(2,1)S(1)} %bitcast.23), channel_id=1, source_target_pairs={{0,1},{1,0},{2,3},{3,2},{4,5},{5,4},{6,7},{7,6},{8,9},{9,8},{10,11... | collective-permute-start | bytes 1179656 | tf_op jit(solution)/shard_map/ppermute | solution.py:27
  20.1 1.8 %forward_1_0.1.before_ref = f32[3,256,256]{2,1,0:T(8,128)S(1)} custom-call(s32[1296]{0:T(1024)S(1)} %reshape.19.inter_ref, s32[48]{0:T(128)S(1)} %reshape.20.counts_ref, f32[864]{0:T(1024)S(1)} %reshape.25.coeff_ref, bf16[16,256,256]{2,1,0:T(8,128)(2,1)S(1)} %get-tuple-element.9.basis_ref, ...), custom_call_target="tpu_custom_call", output_to_operand_aliasing={{}: (5, {})} | custom-call | flops 805306368 | bytes 1572864 | tf_op jit(solution)/shard_map/forward_1_0/pallas_call | solution.py:308
  21.9 2.8 %forward_2_0.1.before_ref = f32[3,256,256]{2,1,0:T(8,128)S(1)} custom-call(s32[1296]{0:T(1024)S(1)} %reshape.19.inter_ref, s32[48]{0:T(128)S(1)} %reshape.20.counts_ref, f32[864]{0:T(1024)S(1)} %reshape.25.coeff_ref, bf16[16,256,256]{2,1,0:T(8,128)(2,1)S(1)} %get-tuple-element.9.basis_ref, ...), custom_call_target="tpu_custom_call", output_to_operand_aliasing={{}: (5, {})} | custom-call | flops 805306368 | bytes 1572864 | tf_op jit(solution)/shard_map/forward_2_0/pallas_call | solution.py:308
  24.7 2.8 %forward_2_1.1.before_ref = f32[3,256,256]{2,1,0:T(8,128)S(1)} custom-call(s32[1296]{0:T(1024)S(1)} %reshape.19.inter_ref, s32[48]{0:T(128)S(1)} %reshape.20.counts_ref, f32[864]{0:T(1024)S(1)} %reshape.25.coeff_ref, bf16[16,256,256]{2,1,0:T(8,128)(2,1)S(1)} %get-tuple-element.9.basis_ref, ...), custom_call_target="tpu_custom_call", output_to_operand_aliasing={{}: (5, {})} | custom-call | flops 805306368 | bytes 1572864 | tf_op jit(solution)/shard_map/forward_2_1/pallas_call | solution.py:308
  27.5 2.6 %forward_last.1 = (f32[3,256,256]{2,1,0:T(8,128)S(1)}, bf16[3,256,256]{2,1,0:T(8,128)(2,1)}) custom-call(s32[1296]{0:T(1024)S(1)} %reshape.19.inter_ref, s32[48]{0:T(128)S(1)} %reshape.20.counts_ref, f32[864]{0:T(1024)S(1)} %reshape.25.coeff_ref, bf16[16,256,256]{2,1,0:T(8,128)(2,1)S(1)} %get-tuple-element.9.basis_ref, ...), custom_call_target="tpu_custom_call", output_to_operand_aliasing={{0}: (5, {})} | custom-call | flops 805306368 | bytes 1572864 | tf_op jit(solution)/shard_map/forward_last/pallas_call | solution.py:308
  30.2 0.4 collective-permute-start.9
  30.6 1.9 %collective-permute-start.7 = (bf16[3,256,256]{2,1,0:T(8,128)(2,1)}, bf16[3,256,256]{2,1,0:T(8,128)(2,1)S(1)}, u32[]{:S(2)}, u32[]{:S(2)}) collective-permute-start(bf16[3,256,256]{2,1,0:T(8,128)(2,1)} %get-tuple-element.11.image_ref), channel_id=1, source_target_pairs={{8,16},{12,20},{16,8},{20,12},{9,17},{13,21},{17,9},{21,13},{10,18... | collective-permute-start | bytes 1179656 | tf_op jit(solution)/shard_map/ppermute | solution.py:133
  32.5 4.1 %collective-permute-start.6 = (bf16[3,256,256]{2,1,0:T(8,128)(2,1)}, bf16[3,256,256]{2,1,0:T(8,128)(2,1)S(1)}, u32[]{:S(2)}, u32[]{:S(2)}) collective-permute-start(bf16[3,256,256]{2,1,0:T(8,128)(2,1)} %get-tuple-element.11.image_ref), channel_id=1, source_target_pairs={{4,8},{12,16},{20,24},{8,4},{16,12},{24,20},{5,9},{13,17},{21,25},... | collective-permute-start | bytes 1179656 | tf_op jit(solution)/shard_map/ppermute | solution.py:133
  36.7 0.1 exponential_bitcast_fusion.scale_ref
  36.8 1.3 %reshape.23.prec_ref = f32[36]{0:T(128)} reshape(f32[6,6]{1,0:T(8,128)} %param.19) | data formatting | bytes 288 | tf_op jit(solution)/shard_map/reshape | solution.py:291
  38.1 0.7 %copy-done.4 = f32[16,256]{1,0:T(8,128)S(1)} copy-done((f32[16,256]{1,0:T(8,128)S(1)}, f32[16,256]{1,0:T(8,128)}, u32[]{:S(2)}) %copy-start.4) | copy-done | bytes 16408
  38.8 0.6 %copy-done.5 = f32[36]{0:T(128)S(1)} copy-done((f32[36]{0:T(128)S(1)}, f32[36]{0:T(128)}, u32[]{:S(2)}) %copy-start.5) | copy-done | bytes 168
  39.5 6.9 %backward_own.1 = (f32[3,256,256]{2,1,0:T(8,128)S(1)}, bf16[16,256,256]{2,1,0:T(8,128)(2,1)}, f32[3,256,256]{2,1,0:T(8,128)S(1)}, f32[3,256,256]{2,1,0:T(8,128)S(1)}) custom-call(s32[1296]{0:T(1024)S(1)} %reshape.19.inter_ref, s32[48]{0:T(128)S(1)} %reshape.20.counts_ref, f32[864]{0:T(1024)S(1)} %reshape.25.coeff_ref, f32[36]{0:T(128)S(1)} %copy-done.5, ...), custom_call_target="tpu_custom_call" | custom-call | flops 805306368 | bytes 1572864 | tf_op jit(solution)/shard_map/backward_own/pallas_call | solution.py:308
  46.4 1.6 %copy-done = bf16[16,256,256]{2,1,0:T(8,128)(2,1)S(1)} copy-done((bf16[16,256,256]{2,1,0:T(8,128)(2,1)S(1)}, bf16[16,256,256]{2,1,0:T(8,128)(2,1)}, u32[]{:S(2)}) %copy-start) | copy-done | bytes 2097176
  48.0 3.0 %backward_1_0.1.before_ref = f32[3,256,256]{2,1,0:T(8,128)S(1)} custom-call(s32[1296]{0:T(1024)S(1)} %reshape.19.inter_ref, s32[48]{0:T(128)S(1)} %reshape.20.counts_ref, f32[864]{0:T(1024)S(1)} %reshape.25.coeff_ref, bf16[16,256,256]{2,1,0:T(8,128)(2,1)S(1)} %copy-done, ...), custom_call_target="tpu_custom_call", output_to_operand_aliasing={{}: (5, {})} | custom-call | flops 805306368 | bytes 1572864 | tf_op jit(solution)/shard_map/backward_1_0/pallas_call | solution.py:308
  50.9 3.0 %backward_2_0.1.before_ref = f32[3,256,256]{2,1,0:T(8,128)S(1)} custom-call(s32[1296]{0:T(1024)S(1)} %reshape.19.inter_ref, s32[48]{0:T(128)S(1)} %reshape.20.counts_ref, f32[864]{0:T(1024)S(1)} %reshape.25.coeff_ref, bf16[16,256,256]{2,1,0:T(8,128)(2,1)S(1)} %copy-done, ...), custom_call_target="tpu_custom_call", output_to_operand_aliasing={{}: (5, {})} | custom-call | flops 805306368 | bytes 1572864 | tf_op jit(solution)/shard_map/backward_2_0/pallas_call | solution.py:308
  53.9 1.9 %backward_2_1.1.before_ref = f32[3,256,256]{2,1,0:T(8,128)S(1)} custom-call(s32[1296]{0:T(1024)S(1)} %reshape.19.inter_ref, s32[48]{0:T(128)S(1)} %reshape.20.counts_ref, f32[864]{0:T(1024)S(1)} %reshape.25.coeff_ref, bf16[16,256,256]{2,1,0:T(8,128)(2,1)S(1)} %copy-done, ...), custom_call_target="tpu_custom_call", output_to_operand_aliasing={{}: (5, {})} | custom-call | flops 805306368 | bytes 1572864 | tf_op jit(solution)/shard_map/backward_2_1/pallas_call | solution.py:308
  55.8 3.0 %backward_1_1.1 = f32[3,256,256]{2,1,0:T(8,128)S(1)} custom-call(s32[1296]{0:T(1024)S(1)} %reshape.19.inter_ref, s32[48]{0:T(128)S(1)} %reshape.20.counts_ref, f32[864]{0:T(1024)S(1)} %reshape.25.coeff_ref, bf16[16,256,256]{2,1,0:T(8,128)(2,1)S(1)} %copy-done, ...), custom_call_target="tpu_custom_call", output_to_operand_aliasing={{}: (5, {})} | custom-call | flops 805306368 | bytes 1572864 | tf_op jit(solution)/shard_map/backward_1_1/pallas_call | solution.py:308
  58.8 0.9 %collective-permute-start.10 = (f32[3,256,256]{2,1,0:T(8,128)S(1)}, f32[3,256,256]{2,1,0:T(8,128)S(1)}, u32[]{:S(2)}, u32[]{:S(2)}) collective-permute-start(f32[3,256,256]{2,1,0:T(8,128)S(1)} %backward_1_1.1), channel_id=1, source_target_pairs={{0,1},{1,0},{2,3},{3,2},{4,5},{5,4},{6,7},{7,6},{8,9},{9,8},{10,11... | collective-permute-start | bytes 2359304 | tf_op jit(solution)/shard_map/ppermute | solution.py:27
  59.7 1.9 %collective-permute-done.10 = f32[3,256,256]{2,1,0:T(8,128)S(1)} collective-permute-done((f32[3,256,256]{2,1,0:T(8,128)S(1)}, f32[3,256,256]{2,1,0:T(8,128)S(1)}, u32[]{:S(2)}, u32[]{:S(2)}) %collective-permute-start.10) | collective-permute-done | bytes 786464 | tf_op jit(solution)/shard_map/ppermute | solution.py:27
  61.6 1.4 %add_bitcast_fusion = (f32[1,3,256,256]{3,2,1,0:T(8,128)}, f32[1,3,256,256]{3,2,1,0:T(8,128)}) fusion(f32[3,256,256]{2,1,0:T(8,128)S(1)} %collective-permute-done.10, f32[3,256,256]{2,1,0:T(8,128)S(1)} %get-tuple-element.15, f32[3,256,256]{2,1,0:T(8,128)S(1)} %backward_1_1.1, f32[3,256,256]{2,1,0:T(8,128)S(1)} %get-tuple-element.14), kind=kLoop, calls=%fused_computation.1 | loop fusion | flops 1376256 | bytes 4718592 | tf_op jit(solution)/shard_map/broadcast_in_dim | solution.py:369
  (40 shorter events, 0.6 us)
Async XLA Ops:
  0.6 10.8 %copy-start.9 = (f32[8,2,25]{2,1,0:T(2,128)S(1)}, f32[8,2,25]{2,1,0:T(2,128)}, u32[]{:S(2)}) copy-start(f32[8,2,25]{2,1,0:T(2,128)} %param.17) | copy-start | bytes 4804
  0.6 11.3 %copy-start.8 = (bf16[8,6,6,3]{2,0,3,1:T(8,128)(2,1)S(1)}, bf16[8,6,6,3]{2,0,3,1:T(8,128)(2,1)}, u32[]{:S(2)}) copy-start(bf16[8,6,6,3]{2,0,3,1:T(8,128)(2,1)} %param.18) | copy-start | bytes 5188
  0.7 11.9 %copy-start.7 = (s32[8,6,3,9]{3,0,2,1:T(8,128)S(1)}, s32[8,6,3,9]{3,0,2,1:T(8,128)}, u32[]{:S(2)}) copy-start(s32[8,6,3,9]{3,0,2,1:T(8,128)} %param.15) | copy-start | bytes 15556
  0.7 12.1 %copy-start.10 = (s32[8,6]{1,0:T(8,128)S(1)}, s32[8,6]{1,0:T(8,128)}, u32[]{:S(2)}) copy-start(s32[8,6]{1,0:T(8,128)} %param.16) | copy-start | bytes 580
  2.4 15.6 %copy-start.1 = (bf16[1,1,3,256,256]{4,3,2,1,0:T(8,128)(2,1)S(1)}, bf16[1,1,3,256,256]{4,3,2,1,0:T(8,128)(2,1)}, u32[]{:S(2)}) copy-start(bf16[1,1,3,256,256]{4,3,2,1,0:T(8,128)(2,1)} %param.12) | copy-start | bytes 1179652
  2.4 15.6 %collective-permute-start.3 = (bf16[3,256,256]{2,1,0:T(8,128)(2,1)S(1)}, bf16[3,256,256]{2,1,0:T(8,128)(2,1)S(1)}, u32[]{:S(2)}, u32[]{:S(2)}) collective-permute-start(bf16[3,256,256]{2,1,0:T(8,128)(2,1)S(1)} %get-tuple-element.16.image_ref), channel_id=1, source_target_pairs={{0,4},{8,12},{16,20},{24,28},{4,0},{12,8},{20,16},{28,24},{1,5},{9... | collective-permute-start | bytes 1179656 | tf_op jit(solution)/shard_map/ppermute | solution.py:133
  3.7 18.2 %collective-permute-start.2 = (bf16[3,256,256]{2,1,0:T(8,128)(2,1)S(1)}, bf16[3,256,256]{2,1,0:T(8,128)(2,1)S(1)}, u32[]{:S(2)}, u32[]{:S(2)}) collective-permute-start(bf16[3,256,256]{2,1,0:T(8,128)(2,1)S(1)} %get-tuple-element.16.image_ref), channel_id=1, source_target_pairs={{0,8},{4,12},{16,24},{20,28},{8,0},{12,4},{24,16},{28,20},{1,9},{5... | collective-permute-start | bytes 1179656 | tf_op jit(solution)/shard_map/ppermute | solution.py:133
  5.0 19.8 %collective-permute-start.1 = (bf16[3,256,256]{2,1,0:T(8,128)(2,1)S(1)}, bf16[3,256,256]{2,1,0:T(8,128)(2,1)S(1)}, u32[]{:S(2)}, u32[]{:S(2)}) collective-permute-start(bf16[3,256,256]{2,1,0:T(8,128)(2,1)S(1)} %get-tuple-element.16.image_ref), channel_id=1, source_target_pairs={{8,16},{12,20},{16,8},{20,12},{9,17},{13,21},{17,9},{21,13},{10,18... | collective-permute-start | bytes 1179656 | tf_op jit(solution)/shard_map/ppermute | solution.py:133
  6.9 20.6 %collective-permute-start = (bf16[3,256,256]{2,1,0:T(8,128)(2,1)S(1)}, bf16[3,256,256]{2,1,0:T(8,128)(2,1)S(1)}, u32[]{:S(2)}, u32[]{:S(2)}) collective-permute-start(bf16[3,256,256]{2,1,0:T(8,128)(2,1)S(1)} %get-tuple-element.16.image_ref), channel_id=1, source_target_pairs={{4,8},{12,16},{20,24},{8,4},{16,12},{24,20},{5,9},{13,17},{21,25},... | collective-permute-start | bytes 1179656 | tf_op jit(solution)/shard_map/ppermute | solution.py:133
  10.2 22.3 %collective-permute-start.5 = (bf16[3,256,256]{2,1,0:T(8,128)(2,1)S(1)}, bf16[3,256,256]{2,1,0:T(8,128)(2,1)}, u32[]{:S(2)}, u32[]{:S(2)}) collective-permute-start(bf16[3,256,256]{2,1,0:T(8,128)(2,1)S(1)} %get-tuple-element.16.image_ref), channel_id=1, source_target_pairs={{0,2},{2,0},{1,3},{3,1},{4,6},{6,4},{5,7},{7,5},{8,10},{10,8},{9,1... | collective-permute-start | bytes 1179656 | tf_op jit(solution)/shard_map/ppermute | solution.py:27
  18.0 20.1 %collective-permute-start.4 = (bf16[3,256,256]{2,1,0:T(8,128)(2,1)S(1)}, bf16[3,256,256]{2,1,0:T(8,128)(2,1)}, u32[]{:S(2)}, u32[]{:S(2)}) collective-permute-start(bf16[3,256,256]{2,1,0:T(8,128)(2,1)S(1)} %bitcast.23), channel_id=1, source_target_pairs={{0,1},{1,0},{2,3},{3,2},{4,5},{5,4},{6,7},{7,6},{8,9},{9,8},{10,11... | collective-permute-start | bytes 1179656 | tf_op jit(solution)/shard_map/ppermute | solution.py:27
  24.7 2.8 %copy-start.2 = (bf16[1,3,256,256]{3,2,1,0:T(8,128)(2,1)S(1)}, bf16[1,3,256,256]{3,2,1,0:T(8,128)(2,1)}, u32[]{:S(2)}) copy-start(bf16[1,3,256,256]{3,2,1,0:T(8,128)(2,1)} %param.13) | copy-start | bytes 1179652
  24.7 2.8 %copy-start.3 = (bf16[1,3,256,256]{3,2,1,0:T(8,128)(2,1)S(1)}, bf16[1,3,256,256]{3,2,1,0:T(8,128)(2,1)}, u32[]{:S(2)}) copy-start(bf16[1,3,256,256]{3,2,1,0:T(8,128)(2,1)} %param.14) | copy-start | bytes 1179652
  27.5 9.2 %copy-start.6 = (f32[1,3,256,256]{3,2,1,0:T(8,128)S(1)}, f32[1,3,256,256]{3,2,1,0:T(8,128)}, u32[]{:S(2)}) copy-start(f32[1,3,256,256]{3,2,1,0:T(8,128)} %param.11) | copy-start | bytes 2359300
  30.2 16.2 %collective-permute-start.9 = (bf16[3,256,256]{2,1,0:T(8,128)(2,1)}, bf16[3,256,256]{2,1,0:T(8,128)(2,1)S(1)}, u32[]{:S(2)}, u32[]{:S(2)}) collective-permute-start(bf16[3,256,256]{2,1,0:T(8,128)(2,1)} %get-tuple-element.11.image_ref), channel_id=1, source_target_pairs={{0,4},{8,12},{16,20},{24,28},{4,0},{12,8},{20,16},{28,24},{1,5},{9... | collective-permute-start | bytes 1179656 | tf_op jit(solution)/shard_map/ppermute | solution.py:133
  30.6 20.3 %collective-permute-start.8 = (bf16[3,256,256]{2,1,0:T(8,128)(2,1)}, bf16[3,256,256]{2,1,0:T(8,128)(2,1)S(1)}, u32[]{:S(2)}, u32[]{:S(2)}) collective-permute-start(bf16[3,256,256]{2,1,0:T(8,128)(2,1)} %get-tuple-element.11.image_ref), channel_id=1, source_target_pairs={{0,8},{4,12},{16,24},{20,28},{8,0},{12,4},{24,16},{28,20},{1,9},{5... | collective-permute-start | bytes 1179656 | tf_op jit(solution)/shard_map/ppermute | solution.py:133
  30.6 23.3 %collective-permute-start.7 = (bf16[3,256,256]{2,1,0:T(8,128)(2,1)}, bf16[3,256,256]{2,1,0:T(8,128)(2,1)S(1)}, u32[]{:S(2)}, u32[]{:S(2)}) collective-permute-start(bf16[3,256,256]{2,1,0:T(8,128)(2,1)} %get-tuple-element.11.image_ref), channel_id=1, source_target_pairs={{8,16},{12,20},{16,8},{20,12},{9,17},{13,21},{17,9},{21,13},{10,18... | collective-permute-start | bytes 1179656 | tf_op jit(solution)/shard_map/ppermute | solution.py:133
  32.5 23.3 %collective-permute-start.6 = (bf16[3,256,256]{2,1,0:T(8,128)(2,1)}, bf16[3,256,256]{2,1,0:T(8,128)(2,1)S(1)}, u32[]{:S(2)}, u32[]{:S(2)}) collective-permute-start(bf16[3,256,256]{2,1,0:T(8,128)(2,1)} %get-tuple-element.11.image_ref), channel_id=1, source_target_pairs={{4,8},{12,16},{20,24},{8,4},{16,12},{24,20},{5,9},{13,17},{21,25},... | collective-permute-start | bytes 1179656 | tf_op jit(solution)/shard_map/ppermute | solution.py:133
  38.1 0.7 %copy-start.4 = (f32[16,256]{1,0:T(8,128)S(1)}, f32[16,256]{1,0:T(8,128)}, u32[]{:S(2)}) copy-start(f32[16,256]{1,0:T(8,128)} %get-tuple-element.21.taps_ref) | copy-start | bytes 49156
  38.8 0.6 %copy-start.5 = (f32[36]{0:T(128)S(1)}, f32[36]{0:T(128)}, u32[]{:S(2)}) copy-start(f32[36]{0:T(128)} %reshape.23.prec_ref) | copy-start | bytes 436
  46.4 1.6 %copy-start = (bf16[16,256,256]{2,1,0:T(8,128)(2,1)S(1)}, bf16[16,256,256]{2,1,0:T(8,128)(2,1)}, u32[]{:S(2)}) copy-start(bf16[16,256,256]{2,1,0:T(8,128)(2,1)} %get-tuple-element.12.basis_ref) | copy-start | bytes 6291460
  58.8 2.8 %collective-permute-start.10 = (f32[3,256,256]{2,1,0:T(8,128)S(1)}, f32[3,256,256]{2,1,0:T(8,128)S(1)}, u32[]{:S(2)}, u32[]{:S(2)}) collective-permute-start(f32[3,256,256]{2,1,0:T(8,128)S(1)} %backward_1_1.1), channel_id=1, source_target_pairs={{0,1},{1,0},{2,3},{3,2},{4,5},{5,4},{6,7},{7,6},{8,9},{9,8},{10,11... | collective-permute-start | bytes 2359304 | tf_op jit(solution)/shard_map/ppermute | solution.py:27
where the time goes:
time: 62.4 us; the launch traced here: 63 us
  Pallas kernels  32 us (51%)
  starting transfers between devices  18.6 us (30%)
  local copies, waits for them, and re-layouts  5.78 us (9%)
  other arithmetic  3.72 us (6%)
  waiting for transfers between devices  1.94 us (3%)
  between operations  0.95 us (2%)
    pallas_call x10, Pallas kernels, call(): pl.pallas_call(kernel, out_shape=outs, in_specs=[SMEM] * len(smem) + [VME...  32 us
    ppermute x8, starting transfers between devices, flipped(): return lax.ppermute(x, axis, pairs)  14.3 us
    ppermute x3, starting transfers between devices, rotated(): lax.ppermute(x, axis, [(i, (i + by) % length) for i in range(length)])  4.34 us
    unnamed x23, local copies, waits for them, and re-layouts  3.02 us
    ppermute x3, waiting for transfers between devices, rotated(): lax.ppermute(x, axis, [(i, (i + by) % length) for i in range(length)])  1.92 us
    convert_element_type x1, other arithmetic, body(): sample_b = sample.astype(jnp.bfloat16)  1.68 us
    broadcast_in_dim x1, other arithmetic, body(): return ((mean_sum / samples)[None], (scale_sum / samples + 1.0)[None])  1.35 us
    reshape x1, local copies, waits for them, and re-layouts, body(): prec_flat = prior_prec.reshape(-1)  1.31 us
  transfers between devices with their start and end apart: 11, of which 1 were waited for; matrix products, arithmetic and copies ran while one was open for 6% of the time, Pallas kernels for 46%

commit v1 on v0

v1 whole, which is shorter than its diff:
```python
import functools

import jax
import jax.numpy as jnp
from jax import lax
from jax.experimental import pallas as pl
from jax.experimental.pallas import tpu as pltpu
from jax.sharding import PartitionSpec as P

NB = 6
K = 3
REACH = 2
HEAD = 3
VMEM_BYTES = 16 * 1024 * 1024
VMEM = pl.BlockSpec(memory_space=pltpu.VMEM)
SMEM = pl.BlockSpec(memory_space=pltpu.SMEM)


def shifted(x, axis, by):
    length = lax.axis_size(axis)
    pairs = [(i, i + by) for i in range(length) if 0 <= i + by < length]
    return lax.ppermute(x, axis, pairs)


def rotated(x, axis, by):
    length = lax.axis_size(axis)
    return lax.ppermute(x, axis, [(i, (i + by) % length) for i in range(length)])


def build_basis(taps_ref, lines_ref, basis_ref, adjoint):
    kinds, side = basis_ref.shape[0] // 2, basis_ref.shape[1]
    count = taps_ref.shape[1]
    half = (count - 1) // 2
    taps = taps_ref[...].astype(jnp.bfloat16)
    tap = lax.broadcasted_iota(jnp.int32, (count, side), 0)
    lane = lax.broadcasted_iota(jnp.int32, (count, side), 1)
    lane = jnp.where(lane < side // 2, lane, lane - side)
    plain = (lane == half - tap).astype(jnp.float32).astype(jnp.bfloat16)
    turned = (lane == tap - half).astype(jnp.float32).astype(jnp.bfloat16)
    lines_ref[0] = dot(taps, turned if adjoint else plain)
    lines_ref[1] = dot(taps, plain if adjoint else turned)
    apart = lax.broadcasted_iota(jnp.int32, (side, side), 0) - lax.broadcasted_iota(
        jnp.int32, (side, side), 1
    )
    band = jnp.abs(apart) <= half

    def one(k, carry):
        for c in range(2):
            line = jnp.broadcast_to(lines_ref[c, pl.ds(2 * k + c, 1), :], (side, side))
            rows = pltpu.roll(line, 0, 1, stride=1, stride_axis=0)
            basis_ref[c * kinds + k] = jnp.where(band, rows, 0.0).astype(jnp.bfloat16)
        return carry

    lax.fori_loop(0, kinds, one, 0)


def find_slot(inter_ref, counts_ref, tile, expo, filt, sizes):
    tiles, filters, fields = sizes
    inside = (tile >= 0) & (tile < tiles) & (expo >= 0) & (expo < tiles)
    pair = jnp.clip(tile, 0, tiles - 1) * filters + filt
    live = counts_ref[pair]
    base = jnp.int32(0)
    found = jnp.int32(0)
    for q in range(K):
        here = (pair * K + q) * fields
        hit = (q < live) & (inter_ref[here] == expo) & inside
        base = jnp.where(hit, here, base)
        found = jnp.where(hit, 1, found)
    return found, base


def weight(coeff_ref, at, row_centred, col_centred):
    return (coeff_ref[at] + coeff_ref[at + 1] * row_centred) + coeff_ref[at + 2] * col_centred


def centred_axes(side, oy, ox):
    rows = lax.broadcasted_iota(jnp.int32, (side, 1), 0) + oy
    cols = lax.broadcasted_iota(jnp.int32, (1, side), 1) + ox
    return (
        (2 * rows + 1 - side).astype(jnp.float32) / side,
        (2 * cols + 1 - side).astype(jnp.float32) / side,
    )


def diagonal(side, by):
    apart = lax.broadcasted_iota(jnp.int32, (side, side), 1) - lax.broadcasted_iota(
        jnp.int32, (side, side), 0
    )
    return (apart == by).astype(jnp.float32).astype(jnp.bfloat16)


def dot(a, b):
    return jnp.dot(a, b, preferred_element_type=jnp.float32)


def settle_contribution(image, oy, ox, pred_ref, f):
    side = image.shape[0]
    across = dot(image, diagonal(side, ox)).astype(jnp.bfloat16)
    pred_ref[f] = pred_ref[f] + dot(diagonal(side, -oy), across)


def contribution(inter_ref, coeff_ref, basis_ref, base, coeff_base, image):
    side = image.shape[0]
    kinds = basis_ref.shape[0] // 2
    row_centred, col_centred = centred_axes(side, inter_ref[base + 1], inter_ref[base + 2])
    total = jnp.zeros((side, side), jnp.float32)
    for b in range(NB):
        k = inter_ref[base + HEAD + b]
        half_blur = dot(basis_ref[k], image).astype(jnp.bfloat16)
        blurred = dot(half_blur, basis_ref[kinds + k])
        total = total + weight(coeff_ref, coeff_base + 3 * b, row_centred, col_centred) * blurred
    return total.astype(jnp.bfloat16)


def bring_residual(image, oy, ox):
    side = image.shape[0]
    across = dot(image, diagonal(side, -ox)).astype(jnp.bfloat16)
    return dot(diagonal(side, oy), across)


def adjoint_term(inter_ref, coeff_ref, basis_ref, base, coeff_base, moved):
    side = moved.shape[0]
    kinds = basis_ref.shape[0] // 2
    row_centred, col_centred = centred_axes(side, inter_ref[base + 1], inter_ref[base + 2])
    total = jnp.zeros((side, side), jnp.float32)
    for b in range(NB):
        k = inter_ref[base + HEAD + b]
        w = weight(coeff_ref, coeff_base + 3 * b, row_centred, col_centred)
        back_half = dot(basis_ref[k], (w * moved).astype(jnp.bfloat16)).astype(jnp.bfloat16)
        total = total + dot(back_half, basis_ref[kinds + k])
    return total


def source_of(own, move):
    distance, parity = move
    return own + jnp.where(lax.rem(own // distance, 2) == parity, distance, -distance)


def flipped(x, axis, move):
    distance, parity = move
    length = lax.axis_size(axis)
    firsts = [i for i in range(length - distance) if (i // distance) % 2 == parity]
    pairs = [(i, i + distance) for i in firsts] + [(i + distance, i) for i in firsts]
    return lax.ppermute(x, axis, pairs)


def gather_live(sizes, moves, backward, inter_ref, counts_ref, images, list_ref, held_ref):
    tiles, filters, fields = sizes
    local = images[0].shape[0]
    own = lax.axis_index("tile")
    first = lax.axis_index("filt") * local
    live = jnp.int32(0)
    for move, image_ref in zip(moves, images):
        far = own if move is None else source_of(own, move)
        tile, expo = (own, far) if backward else (far, own)
        for f in range(local):
            found, base = find_slot(inter_ref, counts_ref, tile, expo, first + f, sizes)

            @pl.when(found == 1)
            def _():
                list_ref[0, live] = f
                list_ref[1, live] = base
                list_ref[2, live] = (expo * filters + first + f) * NB * 3
                held_ref[live] = image_ref[f]

            live = live + found
    return live


def forward_slots(
    sizes, moves, inter_ref, counts_ref, coeff_ref, basis_ref, images, pred_ref, scratch
):
    list_ref, held_ref, ready_ref = scratch
    live = gather_live(
        sizes, moves, False, inter_ref, counts_ref, images, list_ref, held_ref
    )

    @pl.when(live > 0)
    def _():
        def blur(n):
            ready_ref[...] = contribution(
                inter_ref, coeff_ref, basis_ref, list_ref[1, n], list_ref[2, n], held_ref[n]
            )

        def settle(n):
            base = list_ref[1, n]
            settle_contribution(
                ready_ref[...], inter_ref[base + 1], inter_ref[base + 2], pred_ref, list_ref[0, n]
            )

        def one(n, carry):
            settle(n - 1)
            blur(n)
            return carry

        blur(0)
        lax.fori_loop(1, live, one, 0)
        settle(live - 1)


def backward_slots(
    sizes, moves, inter_ref, counts_ref, coeff_ref, basis_ref, images, grad_ref, scratch
):
    list_ref, held_ref, ready_ref = scratch
    live = gather_live(
        sizes, moves, True, inter_ref, counts_ref, images, list_ref, held_ref
    )

    @pl.when(live > 0)
    def _():
        def bring(n):
            base = list_ref[1, n]
            return bring_residual(held_ref[n], inter_ref[base + 1], inter_ref[base + 2])

        def take(n):
            f = list_ref[0, n]
            grad_ref[f] = grad_ref[f] + adjoint_term(
                inter_ref, coeff_ref, basis_ref, list_ref[1, n], list_ref[2, n], ready_ref[...]
            )

        def one(n, carry):
            following = bring(n)
            take(n - 1)
            ready_ref[...] = following
            return carry

        ready_ref[...] = bring(0)
        lax.fori_loop(1, live, one, 0)
        take(live - 1)


def forward_own(sizes, inter_ref, counts_ref, coeff_ref, taps_ref, image_ref, *refs):
    pred_ref, basis_ref, lines_ref, *scratch = refs
    build_basis(taps_ref, lines_ref, basis_ref, False)
    pred_ref[...] = jnp.zeros_like(pred_ref)
    forward_slots(
        sizes, [None], inter_ref, counts_ref, coeff_ref, basis_ref, [image_ref], pred_ref, scratch
    )


def forward_next(sizes, moves, inter_ref, counts_ref, coeff_ref, basis_ref, *refs):
    images, (before_ref, pred_ref, *scratch) = refs[: len(moves)], refs[len(moves) :]
    del before_ref
    forward_slots(
        sizes, moves, inter_ref, counts_ref, coeff_ref, basis_ref, images, pred_ref, scratch
    )


def forward_last(sizes, moves, inter_ref, counts_ref, coeff_ref, basis_ref, *refs):
    images, refs = refs[: len(moves)], refs[len(moves) :]
    before_ref, observed_ref, inv_ref, pred_ref, resid_ref, *scratch = refs
    del before_ref
    forward_slots(
        sizes, moves, inter_ref, counts_ref, coeff_ref, basis_ref, images, pred_ref, scratch
    )
    for f in range(observed_ref.shape[0]):
        gap = observed_ref[f].astype(jnp.float32) - pred_ref[f]
        resid_ref[f] = (inv_ref[f].astype(jnp.float32) * gap).astype(jnp.bfloat16)


def backward_own(
    sizes,
    samples,
    inter_ref,
    counts_ref,
    coeff_ref,
    prec_ref,
    taps_ref,
    image_ref,
    sample_ref,
    scale_ref,
    *refs,
):
    tiles, filters, fields = sizes
    local, side = sample_ref.shape[0], sample_ref.shape[1]
    part = lax.axis_index("filt")
    parts = filters // local
    first = part * local
    noises, refs = refs[:samples], refs[samples:]
    others, refs = refs[: parts - 1], refs[parts - 1 :]
    grad_ref, basis_ref, *refs = refs
    turns, (lines_ref, *scratch) = refs[:samples], refs[samples:]
    build_basis(taps_ref, lines_ref, basis_ref, True)
    for noise_ref, turn_ref in zip(noises, turns):
        turn_ref[...] = scale_ref[...] * noise_ref[...].astype(jnp.float32)
    for f in range(local):
        prior = jnp.zeros((side, side), jnp.float32)
        for g in range(local):
            prior = prior + prec_ref[first + f, first + g] * sample_ref[g]
        for r in range(1, parts):
            source = lax.rem(part + parts - r, parts) * local
            for g in range(local):
                far = others[r - 1][g].astype(jnp.float32)
                prior = prior + prec_ref[first + f, source + g] * far
        grad_ref[f] = -prior
    backward_slots(
        sizes, [None], inter_ref, counts_ref, coeff_ref, basis_ref, [image_ref], grad_ref, scratch
    )


def backward_next(sizes, moves, inter_ref, counts_ref, coeff_ref, basis_ref, *refs):
    images, (before_ref, grad_ref, *scratch) = refs[: len(moves)], refs[len(moves) :]
    del before_ref
    backward_slots(
        sizes, moves, inter_ref, counts_ref, coeff_ref, basis_ref, images, grad_ref, scratch
    )


def body(
    sky_mean,
    sky_log_scale,
    noise_draw,
    observed,
    inv_var,
    intersections,
    counts,
    kernels,
    psf_coeffs,
    prior_prec,
):
    side = sky_mean.shape[2]
    local = sky_mean.shape[1]
    tiles, filters = counts.shape
    sizes = (tiles, filters, intersections.shape[3])
    kinds = kernels.shape[0]
    started = [(d, parity) for d in range(1, REACH + 1) for parity in (0, 1)]
    last = (1, 1)
    early = [move for move in started if move != last]
    samples = lax.axis_size("mc")
    parts = lax.axis_size("filt")

    scale_map = jnp.exp(sky_log_scale[0])
    noise = noise_draw[0, 0]
    eps_float = noise.astype(jnp.float32)
    sample = sky_mean[0] + scale_map * eps_float
    sample_b = sample.astype(jnp.bfloat16)
    inter_flat = intersections.reshape(-1)
    counts_flat = counts.reshape(-1)
    coeff_flat = psf_coeffs.astype(jnp.float32).reshape(-1)
    tables = (inter_flat, counts_flat, coeff_flat)
    taps = kernels.reshape(2 * kinds, kernels.shape[2])

    image_f32 = jax.ShapeDtypeStruct((local, side, side), jnp.float32)
    image_b16 = jax.ShapeDtypeStruct((local, side, side), jnp.bfloat16)
    basis_type = jax.ShapeDtypeStruct((2 * kinds, side, side), jnp.bfloat16)
    cost = pl.CostEstimate(
        flops=2 * NB * 4 * side**3, bytes_accessed=8 * local * side * side, transcendentals=0
    )

    lines = pltpu.VMEM((2, 2 * kinds, side), jnp.float32)

    def slot_scratch(groups, ready):
        return [
            pltpu.SMEM((3, groups * local), jnp.int32),
            pltpu.VMEM((groups * local, side, side), jnp.bfloat16),
            pltpu.VMEM((side, side), ready),
        ]

    def call(kernel, name, outs, smem, vmem, scratch, aliases={}):
        return pl.pallas_call(
            kernel,
            out_shape=outs,
            in_specs=[SMEM] * len(smem) + [VMEM] * len(vmem),
            out_specs=[VMEM] * len(outs),
            scratch_shapes=scratch,
            input_output_aliases=aliases,
            compiler_params=pltpu.CompilerParams(vmem_limit_bytes=VMEM_BYTES),
            cost_estimate=cost,
            name=name,
        )(*smem, *vmem)

    near = {move: flipped(sample_b, "tile", move) for move in started}
    other_samples = [rotated(sample_b, "filt", r) for r in range(1, parts)]
    other_noise = [rotated(noise, "mc", r) for r in range(1, samples)]
    pred, basis = call(
        functools.partial(forward_own, sizes),
        "forward_own",
        [image_f32, basis_type],
        tables,
        (taps, sample_b),
        [lines] + slot_scratch(1, jnp.bfloat16),
    )
    (pred,) = call(
        functools.partial(forward_next, sizes, early),
        "forward_next",
        [image_f32],
        tables,
        (basis, *[near[move] for move in early], pred),
        slot_scratch(len(early), jnp.bfloat16),
        {len(tables) + 1 + len(early): 0},
    )
    _, residual = call(
        functools.partial(forward_last, sizes, [last]),
        "forward_last",
        [image_f32, image_b16],
        tables,
        (basis, near[last], pred, observed[0], inv_var[0]),
        slot_scratch(1, jnp.bfloat16),
        {len(tables) + 2: 0},
    )
    near_resid = {move: flipped(residual, "tile", move) for move in started}
    grad, basis, turn, *other_turns = call(
        functools.partial(backward_own, sizes, samples),
        "backward_own",
        [image_f32, basis_type] + [image_f32] * samples,
        tables + (prior_prec,),
        (taps, residual, sample, scale_map, noise, *other_noise, *other_samples),
        [lines] + slot_scratch(1, jnp.float32),
    )
    (grad,) = call(
        functools.partial(backward_next, sizes, early),
        "backward_next",
        [image_f32],
        tables,
        (basis, *[near_resid[move] for move in early], grad),
        slot_scratch(len(early), jnp.float32),
        {len(tables) + 1 + len(early): 0},
    )
    (grad,) = call(
        functools.partial(backward_next, sizes, [last]),
        "backward_last",
        [image_f32],
        tables,
        (basis, near_resid[last], grad),
        slot_scratch(1, jnp.float32),
        {len(tables) + 2: 0},
    )
    mean_sum = grad
    scale_sum = grad * turn
    for r in range(1, samples):
        other_grad = rotated(grad, "mc", r)
        mean_sum = mean_sum + other_grad
        scale_sum = scale_sum + other_grad * other_turns[r - 1]
    return ((mean_sum / samples)[None], (scale_sum / samples + 1.0)[None])

def solution(mesh):
    placed = (
        P("tile", "filt", None, None),
        P("tile", "filt", None, None),
        P("mc", "tile", "filt", None, None),
        P("tile", "filt", None, None),
        P("tile", "filt", None, None),
        P(),
        P(),
        P(),
        P(),
        P(),
    )
    return jax.shard_map(
        body,
        mesh=mesh,
        in_specs=placed,
        out_specs=(P("tile", "filt", None, None), P("tile", "filt", None, None)),
        check_vma=False,
    )
```

time: 62.4 us -> 60.1 us (0.963); the launches traced: 63 us -> 59.7 us
  Pallas kernels: 32 us -> 23.1 us
  waiting for transfers between devices: 1.94 us -> 6.6 us
  local copies, waits for them, and re-layouts: 5.78 us -> 7.22 us
  other arithmetic: 3.72 us -> 2.98 us
    pallas_call x10 -> x6, Pallas kernels: 32 us -> 23.1 us  [call(): pl.pallas_call(kernel, out_shape=outs, in_specs=[SMEM] * len(smem) + [VME...]
    ppermute x8, waiting for transfers between devices: 0.02 us -> 4.68 us  [flipped(): return lax.ppermute(x, axis, pairs)]
    reshape x2, local copies, waits for them, and re-layouts: 0.62 us -> 2.96 us  [body(): coeff_flat = psf_coeffs.astype(jnp.float32).reshape(-1)]
    reshape x1 -> x0, local copies, waits for them, and re-layouts: 1.31 us -> none  [body(): prec_flat = prior_prec.reshape(-1)]
    reshape x1, local copies, waits for them, and re-layouts: 0.21 us -> 1.1 us  [body(): inter_flat = intersections.reshape(-1)]
    unnamed x23 -> x13, local copies, waits for them, and re-layouts: 3.02 us -> 2.28 us
    concatenate x1 -> x0, other arithmetic: 0.69 us -> none  [body(): taps_forward = jnp.concatenate([rows_plain, cols_trans], 0)]
    reshape x1, local copies, waits for them, and re-layouts: 0.08 us -> 0.77 us  [body(): counts_flat = counts.reshape(-1)]
  transfers between devices with their start and end apart: 11 -> 11, of which waited for: 1 -> 5; matrix products, arithmetic and copies ran while one was open for 6% -> 11% of each run, Pallas kernels for 46% -> 35%
where the time goes in v1:
time: 60.1 us; the launch traced here: 59.7 us
  Pallas kernels  23.1 us (38%)
  starting transfers between devices  18.9 us (31%)
  local copies, waits for them, and re-layouts  7.22 us (12%)
  waiting for transfers between devices  6.6 us (11%)
  other arithmetic  2.98 us (5%)
  between operations  0.86 us (1%)
    pallas_call x6, Pallas kernels, call(): pl.pallas_call(kernel, out_shape=outs, in_specs=[SMEM] * len(smem) + [VME...  23.1 us
    ppermute x8, starting transfers between devices, flipped(): return lax.ppermute(x, axis, pairs)  14.4 us
    ppermute x8, waiting for transfers between devices, flipped(): return lax.ppermute(x, axis, pairs)  4.68 us
    ppermute x3, starting transfers between devices, rotated(): lax.ppermute(x, axis, [(i, (i + by) % length) for i in range(length)])  4.54 us
    reshape x2, local copies, waits for them, and re-layouts, body(): coeff_flat = psf_coeffs.astype(jnp.float32).reshape(-1)  2.96 us
    unnamed x13, local copies, waits for them, and re-layouts  2.28 us
    ppermute x3, waiting for transfers between devices, rotated(): lax.ppermute(x, axis, [(i, (i + by) % length) for i in range(length)])  1.92 us
    convert_element_type x1, other arithmetic, body(): sample_b = sample.astype(jnp.bfloat16)  1.64 us
  transfers between devices with their start and end apart: 11, of which 5 were waited for; matrix products, arithmetic and copies ran while one was open for 11% of the time, Pallas kernels for 35%

profile of v1, /device:TPU:17, one launch (start us, length us, event | category | flops | bytes accessed | tf_op | source)
XLA Modules:
  0.0 59.7 jit_solution(1720032798660796207)
XLA Ops:
  0.6 1.6 %fusion = (bf16[3,256,256]{2,1,0:T(8,128)(2,1)S(1)}, f32[3,256,256]{2,1,0:T(8,128)S(1)}) fusion(bf16[1,1,3,256,256]{4,3,2,1,0:T(8,128)(2,1)} %param.12, f32[1,3,256,256]{3,2,1,0:T(8,128)} %param.11, f32[1,3,256,256]{3,2,1,0:T(8,128)} %param.10), kind=kLoop, calls=%fused_computation.4 | loop fusion | flops 786432 | bytes 3145728 | tf_op jit(solution)/shard_map/convert_element_type | solution.py:336
  2.3 0.0 copy-start
  2.3 1.3 %collective-permute-start.1 = (bf16[3,256,256]{2,1,0:T(8,128)(2,1)S(1)}, bf16[3,256,256]{2,1,0:T(8,128)(2,1)S(1)}, u32[]{:S(2)}, u32[]{:S(2)}) collective-permute-start(bf16[3,256,256]{2,1,0:T(8,128)(2,1)S(1)} %get-tuple-element.16.image_ref), channel_id=1, source_target_pairs={{0,4},{8,12},{16,20},{24,28},{4,0},{12,8},{20,16},{28,24},{1,5},{9... | collective-permute-start | bytes 1179656 | tf_op jit(solution)/shard_map/ppermute | solution.py:144
  3.6 1.3 %collective-permute-start.2 = (bf16[3,256,256]{2,1,0:T(8,128)(2,1)S(1)}, bf16[3,256,256]{2,1,0:T(8,128)(2,1)S(1)}, u32[]{:S(2)}, u32[]{:S(2)}) collective-permute-start(bf16[3,256,256]{2,1,0:T(8,128)(2,1)S(1)} %get-tuple-element.16.image_ref), channel_id=1, source_target_pairs={{0,8},{4,12},{16,24},{20,28},{8,0},{12,4},{24,16},{28,20},{1,9},{5... | collective-permute-start | bytes 1179656 | tf_op jit(solution)/shard_map/ppermute | solution.py:144
  4.9 1.9 %collective-permute-start.3 = (bf16[3,256,256]{2,1,0:T(8,128)(2,1)S(1)}, bf16[3,256,256]{2,1,0:T(8,128)(2,1)S(1)}, u32[]{:S(2)}, u32[]{:S(2)}) collective-permute-start(bf16[3,256,256]{2,1,0:T(8,128)(2,1)S(1)} %get-tuple-element.16.image_ref), channel_id=1, source_target_pairs={{8,16},{12,20},{16,8},{20,12},{9,17},{13,21},{17,9},{21,13},{10,18... | collective-permute-start | bytes 1179656 | tf_op jit(solution)/shard_map/ppermute | solution.py:144
  6.8 3.3 %collective-permute-start = (bf16[3,256,256]{2,1,0:T(8,128)(2,1)S(1)}, bf16[3,256,256]{2,1,0:T(8,128)(2,1)S(1)}, u32[]{:S(2)}, u32[]{:S(2)}) collective-permute-start(bf16[3,256,256]{2,1,0:T(8,128)(2,1)S(1)} %get-tuple-element.16.image_ref), channel_id=1, source_target_pairs={{4,8},{12,16},{20,24},{8,4},{16,12},{24,20},{5,9},{13,17},{21,25},... | collective-permute-start | bytes 1179656 | tf_op jit(solution)/shard_map/ppermute | solution.py:144
  10.1 1.3 %collective-permute-start.5 = (bf16[3,256,256]{2,1,0:T(8,128)(2,1)S(1)}, bf16[3,256,256]{2,1,0:T(8,128)(2,1)S(1)}, u32[]{:S(2)}, u32[]{:S(2)}) collective-permute-start(bf16[3,256,256]{2,1,0:T(8,128)(2,1)S(1)} %get-tuple-element.16.image_ref), channel_id=1, source_target_pairs={{0,2},{2,0},{1,3},{3,1},{4,6},{6,4},{5,7},{7,5},{8,10},{10,8},{9,1... | collective-permute-start | bytes 1179656 | tf_op jit(solution)/shard_map/ppermute | solution.py:27
  11.4 1.8 %copy.17 = f32[8,6,6,3]{3,2,1,0:T(8,128)} copy(bf16[8,6,6,3]{2,0,3,1:T(8,128)(2,1)} %param.18) | data formatting | bytes 5184 | tf_op jit(solution)/shard_map/reshape | solution.py:339
  13.2 1.1 %reshape.25.coeff_ref = f32[864]{0:T(1024)S(1)} reshape(f32[8,6,6,3]{3,2,1,0:T(8,128)} %copy.17) | data formatting | bytes 6912 | tf_op jit(solution)/shard_map/reshape | solution.py:339
  14.4 1.6 %copy.16 = s32[8,6,3,9]{3,2,1,0:T(4,128)} copy(s32[8,6,3,9]{3,0,2,1:T(8,128)} %param.15) | data formatting | bytes 10368 | tf_op args[5]
  15.9 1.1 %reshape.19.inter_ref = s32[1296]{0:T(1024)S(1)} reshape(s32[8,6,3,9]{3,2,1,0:T(4,128)} %copy.16) | data formatting | bytes 10368 | tf_op jit(solution)/shard_map/reshape | solution.py:337
  17.0 0.8 %reshape.20.counts_ref = s32[48]{0:T(128)S(1)} reshape(s32[8,6]{1,0:T(8,128)} %param.16) | data formatting | bytes 384 | tf_op jit(solution)/shard_map/reshape | solution.py:338
  17.8 0.7 %copy-done.3 = f32[8,2,25]{2,1,0:T(2,128)S(1)} copy-done((f32[8,2,25]{2,1,0:T(2,128)S(1)}, f32[8,2,25]{2,1,0:T(2,128)}, u32[]{:S(2)}) %copy-start.3) | copy-done | bytes 1624
  18.5 3.0 %forward_own.1 = (f32[3,256,256]{2,1,0:T(8,128)S(1)}, bf16[16,256,256]{2,1,0:T(8,128)(2,1)S(1)}) custom-call(s32[1296]{0:T(1024)S(1)} %reshape.19.inter_ref, s32[48]{0:T(128)S(1)} %reshape.20.counts_ref, f32[864]{0:T(1024)S(1)} %reshape.25.coeff_ref, f32[16,25]{1,0:T(8,128)S(1)} %bitcast.22, bf16[3,256,256]{2,1,0:T(8,128)(2,1)S(1)} %get-tuple-element.16.image_ref), custom_call_target="tpu_custom_call" | custom-call | flops 805306368 | bytes 1572864 | tf_op jit(solution)/shard_map/forward_own/pallas_call | solution.py:360
  21.5 2.1 %collective-permute-start.4 = (bf16[3,256,256]{2,1,0:T(8,128)(2,1)S(1)}, bf16[3,256,256]{2,1,0:T(8,128)(2,1)S(1)}, u32[]{:S(2)}, u32[]{:S(2)}) collective-permute-start(bf16[3,256,256]{2,1,0:T(8,128)(2,1)S(1)} %bitcast.18), channel_id=1, source_target_pairs={{0,1},{1,0},{2,3},{3,2},{4,5},{5,4},{6,7},{7,6},{8,9},{9,8},{10,11... | collective-permute-start | bytes 1179656 | tf_op jit(solution)/shard_map/ppermute | solution.py:27
  23.7 5.5 %forward_next.1.refs_1_ = f32[3,256,256]{2,1,0:T(8,128)S(1)} custom-call(s32[1296]{0:T(1024)S(1)} %reshape.19.inter_ref, s32[48]{0:T(128)S(1)} %reshape.20.counts_ref, f32[864]{0:T(1024)S(1)} %reshape.25.coeff_ref, bf16[16,256,256]{2,1,0:T(8,128)(2,1)S(1)} %get-tuple-element.9.basis_ref, ...), custom_call_target="tpu_custom_call", output_to_operand_aliasing={{}: (7, {})} | custom-call | flops 805306368 | bytes 1572864 | tf_op jit(solution)/shard_map/forward_next/pallas_call | solution.py:360
  29.2 2.0 %forward_last.1 = (f32[3,256,256]{2,1,0:T(8,128)S(1)}, bf16[3,256,256]{2,1,0:T(8,128)(2,1)S(1)}) custom-call(s32[1296]{0:T(1024)S(1)} %reshape.19.inter_ref, s32[48]{0:T(128)S(1)} %reshape.20.counts_ref, f32[864]{0:T(1024)S(1)} %reshape.25.coeff_ref, bf16[16,256,256]{2,1,0:T(8,128)(2,1)S(1)} %get-tuple-element.9.basis_ref, ...), custom_call_target="tpu_custom_call", output_to_operand_aliasing={{0}: (5, {})} | custom-call | flops 805306368 | bytes 1572864 | tf_op jit(solution)/shard_map/forward_last/pallas_call | solution.py:360
  31.2 0.1 collective-permute-start.7
  31.3 0.1 collective-permute-start.8
  31.4 3.6 %collective-permute-start.9 = (bf16[3,256,256]{2,1,0:T(8,128)(2,1)S(1)}, bf16[3,256,256]{2,1,0:T(8,128)(2,1)S(1)}, u32[]{:S(2)}, u32[]{:S(2)}) collective-permute-start(bf16[3,256,256]{2,1,0:T(8,128)(2,1)S(1)} %get-tuple-element.11.image_ref), channel_id=1, source_target_pairs={{8,16},{12,20},{16,8},{20,12},{9,17},{13,21},{17,9},{21,13},{10,18... | collective-permute-start | bytes 1179656 | tf_op jit(solution)/shard_map/ppermute | solution.py:144
  35.1 2.8 %collective-permute-start.6 = (bf16[3,256,256]{2,1,0:T(8,128)(2,1)S(1)}, bf16[3,256,256]{2,1,0:T(8,128)(2,1)S(1)}, u32[]{:S(2)}, u32[]{:S(2)}) collective-permute-start(bf16[3,256,256]{2,1,0:T(8,128)(2,1)S(1)} %get-tuple-element.11.image_ref), channel_id=1, source_target_pairs={{4,8},{12,16},{20,24},{8,4},{16,12},{24,20},{5,9},{13,17},{21,25},... | collective-permute-start | bytes 1179656 | tf_op jit(solution)/shard_map/ppermute | solution.py:144
  37.9 0.1 exponential_bitcast_fusion.scale_ref
  38.0 3.7 %backward_own.1 = (f32[3,256,256]{2,1,0:T(8,128)S(1)}, bf16[16,256,256]{2,1,0:T(8,128)(2,1)S(1)}, f32[3,256,256]{2,1,0:T(8,128)S(1)}, f32[3,256,256]{2,1,0:T(8,128)S(1)}) custom-call(s32[1296]{0:T(1024)S(1)} %reshape.19.inter_ref, s32[48]{0:T(128)S(1)} %reshape.20.counts_ref, f32[864]{0:T(1024)S(1)} %reshape.25.coeff_ref, f32[6,6]{1,0:T(8,128)S(1)} %copy-done.4, ...), custom_call_target="tpu_custom_call" | custom-call | flops 805306368 | bytes 1572864 | tf_op jit(solution)/shard_map/backward_own/pallas_call | solution.py:360
  41.7 0.3 collective-permute-done.7.refs_0_
  42.0 0.1 collective-permute-done.8.refs_1_
  42.1 2.2 %collective-permute-done.9.refs_2_ = bf16[3,256,256]{2,1,0:T(8,128)(2,1)S(1)} collective-permute-done((bf16[3,256,256]{2,1,0:T(8,128)(2,1)S(1)}, bf16[3,256,256]{2,1,0:T(8,128)(2,1)S(1)}, u32[]{:S(2)}, u32[]{:S(2)}) %collective-permute-start.9) | collective-permute-done | bytes 393248 | tf_op jit(solution)/shard_map/ppermute | solution.py:144
  44.3 7.0 %backward_next.1.refs_1_ = f32[3,256,256]{2,1,0:T(8,128)S(1)} custom-call(s32[1296]{0:T(1024)S(1)} %reshape.19.inter_ref, s32[48]{0:T(128)S(1)} %reshape.20.counts_ref, f32[864]{0:T(1024)S(1)} %reshape.25.coeff_ref, bf16[16,256,256]{2,1,0:T(8,128)(2,1)S(1)} %get-tuple-element.12.basis_ref, ...), custom_call_target="tpu_custom_call", output_to_operand_aliasing={{}: (7, {})} | custom-call | flops 805306368 | bytes 1572864 | tf_op jit(solution)/shard_map/backward_next/pallas_call | solution.py:360
  51.2 2.1 %collective-permute-done.6.refs_0_ = bf16[3,256,256]{2,1,0:T(8,128)(2,1)S(1)} collective-permute-done((bf16[3,256,256]{2,1,0:T(8,128)(2,1)S(1)}, bf16[3,256,256]{2,1,0:T(8,128)(2,1)S(1)}, u32[]{:S(2)}, u32[]{:S(2)}) %collective-permute-start.6) | collective-permute-done | bytes 393248 | tf_op jit(solution)/shard_map/ppermute | solution.py:144
  53.3 2.0 %backward_last.1 = f32[3,256,256]{2,1,0:T(8,128)S(1)} custom-call(s32[1296]{0:T(1024)S(1)} %reshape.19.inter_ref, s32[48]{0:T(128)S(1)} %reshape.20.counts_ref, f32[864]{0:T(1024)S(1)} %reshape.25.coeff_ref, bf16[16,256,256]{2,1,0:T(8,128)(2,1)S(1)} %get-tuple-element.12.basis_ref, ...), custom_call_target="tpu_custom_call", output_to_operand_aliasing={{}: (5, {})} | custom-call | flops 805306368 | bytes 1572864 | tf_op jit(solution)/shard_map/backward_last/pallas_call | solution.py:360
  55.3 1.1 %collective-permute-start.10 = (f32[3,256,256]{2,1,0:T(8,128)S(1)}, f32[3,256,256]{2,1,0:T(8,128)S(1)}, u32[]{:S(2)}, u32[]{:S(2)}) collective-permute-start(f32[3,256,256]{2,1,0:T(8,128)S(1)} %backward_last.1), channel_id=1, source_target_pairs={{0,1},{1,0},{2,3},{3,2},{4,5},{5,4},{6,7},{7,6},{8,9},{9,8},{10,11... | collective-permute-start | bytes 2359304 | tf_op jit(solution)/shard_map/ppermute | solution.py:27
  56.4 1.9 %collective-permute-done.10 = f32[3,256,256]{2,1,0:T(8,128)S(1)} collective-permute-done((f32[3,256,256]{2,1,0:T(8,128)S(1)}, f32[3,256,256]{2,1,0:T(8,128)S(1)}, u32[]{:S(2)}, u32[]{:S(2)}) %collective-permute-start.10) | collective-permute-done | bytes 786464 | tf_op jit(solution)/shard_map/ppermute | solution.py:27
  58.3 1.3 %add_bitcast_fusion = (f32[1,3,256,256]{3,2,1,0:T(8,128)}, f32[1,3,256,256]{3,2,1,0:T(8,128)}) fusion(f32[3,256,256]{2,1,0:T(8,128)S(1)} %collective-permute-done.10, f32[3,256,256]{2,1,0:T(8,128)S(1)} %get-tuple-element.15, f32[3,256,256]{2,1,0:T(8,128)S(1)} %backward_last.1, f32[3,256,256]{2,1,0:T(8,128)S(1)} %get-tuple-element.14), kind=kLoop, calls=%fused_computation.1 | loop fusion | flops 1376256 | bytes 4718592 | tf_op jit(solution)/shard_map/broadcast_in_dim | solution.py:434
  (16 shorter events, 0.0 us)
Async XLA Ops:
  2.3 19.2 %copy-start = (bf16[1,1,3,256,256]{4,3,2,1,0:T(8,128)(2,1)S(1)}, bf16[1,1,3,256,256]{4,3,2,1,0:T(8,128)(2,1)}, u32[]{:S(2)}) copy-start(bf16[1,1,3,256,256]{4,3,2,1,0:T(8,128)(2,1)} %param.12) | copy-start | bytes 1179652
  2.3 19.2 %collective-permute-start.1 = (bf16[3,256,256]{2,1,0:T(8,128)(2,1)S(1)}, bf16[3,256,256]{2,1,0:T(8,128)(2,1)S(1)}, u32[]{:S(2)}, u32[]{:S(2)}) collective-permute-start(bf16[3,256,256]{2,1,0:T(8,128)(2,1)S(1)} %get-tuple-element.16.image_ref), channel_id=1, source_target_pairs={{0,4},{8,12},{16,20},{24,28},{4,0},{12,8},{20,16},{28,24},{1,5},{9... | collective-permute-start | bytes 1179656 | tf_op jit(solution)/shard_map/ppermute | solution.py:144
  3.6 20.1 %collective-permute-start.2 = (bf16[3,256,256]{2,1,0:T(8,128)(2,1)S(1)}, bf16[3,256,256]{2,1,0:T(8,128)(2,1)S(1)}, u32[]{:S(2)}, u32[]{:S(2)}) collective-permute-start(bf16[3,256,256]{2,1,0:T(8,128)(2,1)S(1)} %get-tuple-element.16.image_ref), channel_id=1, source_target_pairs={{0,8},{4,12},{16,24},{20,28},{8,0},{12,4},{24,16},{28,20},{1,9},{5... | collective-permute-start | bytes 1179656 | tf_op jit(solution)/shard_map/ppermute | solution.py:144
  4.9 18.8 %collective-permute-start.3 = (bf16[3,256,256]{2,1,0:T(8,128)(2,1)S(1)}, bf16[3,256,256]{2,1,0:T(8,128)(2,1)S(1)}, u32[]{:S(2)}, u32[]{:S(2)}) collective-permute-start(bf16[3,256,256]{2,1,0:T(8,128)(2,1)S(1)} %get-tuple-element.16.image_ref), channel_id=1, source_target_pairs={{8,16},{12,20},{16,8},{20,12},{9,17},{13,21},{17,9},{21,13},{10,18... | collective-permute-start | bytes 1179656 | tf_op jit(solution)/shard_map/ppermute | solution.py:144
  6.8 22.4 %collective-permute-start = (bf16[3,256,256]{2,1,0:T(8,128)(2,1)S(1)}, bf16[3,256,256]{2,1,0:T(8,128)(2,1)S(1)}, u32[]{:S(2)}, u32[]{:S(2)}) collective-permute-start(bf16[3,256,256]{2,1,0:T(8,128)(2,1)S(1)} %get-tuple-element.16.image_ref), channel_id=1, source_target_pairs={{4,8},{12,16},{20,24},{8,4},{16,12},{24,20},{5,9},{13,17},{21,25},... | collective-permute-start | bytes 1179656 | tf_op jit(solution)/shard_map/ppermute | solution.py:144
  10.1 24.9 %collective-permute-start.5 = (bf16[3,256,256]{2,1,0:T(8,128)(2,1)S(1)}, bf16[3,256,256]{2,1,0:T(8,128)(2,1)S(1)}, u32[]{:S(2)}, u32[]{:S(2)}) collective-permute-start(bf16[3,256,256]{2,1,0:T(8,128)(2,1)S(1)} %get-tuple-element.16.image_ref), channel_id=1, source_target_pairs={{0,2},{2,0},{1,3},{3,1},{4,6},{6,4},{5,7},{7,5},{8,10},{10,8},{9,1... | collective-permute-start | bytes 1179656 | tf_op jit(solution)/shard_map/ppermute | solution.py:27
  17.8 0.7 %copy-start.3 = (f32[8,2,25]{2,1,0:T(2,128)S(1)}, f32[8,2,25]{2,1,0:T(2,128)}, u32[]{:S(2)}) copy-start(f32[8,2,25]{2,1,0:T(2,128)} %param.17) | copy-start | bytes 4804
  21.5 16.5 %collective-permute-start.4 = (bf16[3,256,256]{2,1,0:T(8,128)(2,1)S(1)}, bf16[3,256,256]{2,1,0:T(8,128)(2,1)S(1)}, u32[]{:S(2)}, u32[]{:S(2)}) collective-permute-start(bf16[3,256,256]{2,1,0:T(8,128)(2,1)S(1)} %bitcast.18), channel_id=1, source_target_pairs={{0,1},{1,0},{2,3},{3,2},{4,5},{5,4},{6,7},{7,6},{8,9},{9,8},{10,11... | collective-permute-start | bytes 1179656 | tf_op jit(solution)/shard_map/ppermute | solution.py:27
  23.7 5.5 %copy-start.1 = (bf16[1,3,256,256]{3,2,1,0:T(8,128)(2,1)S(1)}, bf16[1,3,256,256]{3,2,1,0:T(8,128)(2,1)}, u32[]{:S(2)}) copy-start(bf16[1,3,256,256]{3,2,1,0:T(8,128)(2,1)} %param.13) | copy-start | bytes 1179652
  23.7 5.5 %copy-start.2 = (bf16[1,3,256,256]{3,2,1,0:T(8,128)(2,1)S(1)}, bf16[1,3,256,256]{3,2,1,0:T(8,128)(2,1)}, u32[]{:S(2)}) copy-start(bf16[1,3,256,256]{3,2,1,0:T(8,128)(2,1)} %param.14) | copy-start | bytes 1179652
  29.2 8.7 %copy-start.5 = (f32[1,3,256,256]{3,2,1,0:T(8,128)S(1)}, f32[1,3,256,256]{3,2,1,0:T(8,128)}, u32[]{:S(2)}) copy-start(f32[1,3,256,256]{3,2,1,0:T(8,128)} %param.11) | copy-start | bytes 2359300
  29.2 8.8 %copy-start.4 = (f32[6,6]{1,0:T(8,128)S(1)}, f32[6,6]{1,0:T(8,128)}, u32[]{:S(2)}) copy-start(f32[6,6]{1,0:T(8,128)} %prec_ref.1) | copy-start | bytes 436
  31.2 10.8 %collective-permute-start.7 = (bf16[3,256,256]{2,1,0:T(8,128)(2,1)S(1)}, bf16[3,256,256]{2,1,0:T(8,128)(2,1)S(1)}, u32[]{:S(2)}, u32[]{:S(2)}) collective-permute-start(bf16[3,256,256]{2,1,0:T(8,128)(2,1)S(1)} %get-tuple-element.11.image_ref), channel_id=1, source_target_pairs={{0,4},{8,12},{16,20},{24,28},{4,0},{12,8},{20,16},{28,24},{1,5},{9... | collective-permute-start | bytes 1179656 | tf_op jit(solution)/shard_map/ppermute | solution.py:144
  31.3 10.8 %collective-permute-start.8 = (bf16[3,256,256]{2,1,0:T(8,128)(2,1)S(1)}, bf16[3,256,256]{2,1,0:T(8,128)(2,1)S(1)}, u32[]{:S(2)}, u32[]{:S(2)}) collective-permute-start(bf16[3,256,256]{2,1,0:T(8,128)(2,1)S(1)} %get-tuple-element.11.image_ref), channel_id=1, source_target_pairs={{0,8},{4,12},{16,24},{20,28},{8,0},{12,4},{24,16},{28,20},{1,9},{5... | collective-permute-start | bytes 1179656 | tf_op jit(solution)/shard_map/ppermute | solution.py:144
  31.4 12.9 %collective-permute-start.9 = (bf16[3,256,256]{2,1,0:T(8,128)(2,1)S(1)}, bf16[3,256,256]{2,1,0:T(8,128)(2,1)S(1)}, u32[]{:S(2)}, u32[]{:S(2)}) collective-permute-start(bf16[3,256,256]{2,1,0:T(8,128)(2,1)S(1)} %get-tuple-element.11.image_ref), channel_id=1, source_target_pairs={{8,16},{12,20},{16,8},{20,12},{9,17},{13,21},{17,9},{21,13},{10,18... | collective-permute-start | bytes 1179656 | tf_op jit(solution)/shard_map/ppermute | solution.py:144
  35.1 18.3 %collective-permute-start.6 = (bf16[3,256,256]{2,1,0:T(8,128)(2,1)S(1)}, bf16[3,256,256]{2,1,0:T(8,128)(2,1)S(1)}, u32[]{:S(2)}, u32[]{:S(2)}) collective-permute-start(bf16[3,256,256]{2,1,0:T(8,128)(2,1)S(1)} %get-tuple-element.11.image_ref), channel_id=1, source_target_pairs={{4,8},{12,16},{20,24},{8,4},{16,12},{24,20},{5,9},{13,17},{21,25},... | collective-permute-start | bytes 1179656 | tf_op jit(solution)/shard_map/ppermute | solution.py:144
  55.3 3.0 %collective-permute-start.10 = (f32[3,256,256]{2,1,0:T(8,128)S(1)}, f32[3,256,256]{2,1,0:T(8,128)S(1)}, u32[]{:S(2)}, u32[]{:S(2)}) collective-permute-start(f32[3,256,256]{2,1,0:T(8,128)S(1)} %backward_last.1), channel_id=1, source_target_pairs={{0,1},{1,0},{2,3},{3,2},{4,5},{5,4},{6,7},{7,6},{8,9},{9,8},{10,11... | collective-permute-start | bytes 2359304 | tf_op jit(solution)/shard_map/ppermute | solution.py:27

commit v2 on v1

v2 whole, which is shorter than its diff:
```python
import functools

import jax
import jax.numpy as jnp
from jax import lax
from jax.experimental import pallas as pl
from jax.experimental.pallas import tpu as pltpu
from jax.sharding import PartitionSpec as P

NB = 6
K = 3
REACH = 2
HEAD = 3
STEP = 16
LANES = 128
VMEM_BYTES = 16 * 1024 * 1024
VMEM = pl.BlockSpec(memory_space=pltpu.VMEM)
SMEM = pl.BlockSpec(memory_space=pltpu.SMEM)


def shifted(x, axis, by):
    length = lax.axis_size(axis)
    pairs = [(i, i + by) for i in range(length) if 0 <= i + by < length]
    return lax.ppermute(x, axis, pairs)


def rotated(x, axis, by):
    length = lax.axis_size(axis)
    return lax.ppermute(x, axis, [(i, (i + by) % length) for i in range(length)])


def build_basis(taps_ref, lines_ref, basis_ref, adjoint):
    kinds, side = basis_ref.shape[0] // 2, basis_ref.shape[1]
    count = taps_ref.shape[1]
    half = (count - 1) // 2
    taps = taps_ref[...].astype(jnp.bfloat16)
    tap = lax.broadcasted_iota(jnp.int32, (count, side), 0)
    lane = lax.broadcasted_iota(jnp.int32, (count, side), 1)
    lane = jnp.where(lane < side // 2, lane, lane - side)
    plain = (lane == half - tap).astype(jnp.float32).astype(jnp.bfloat16)
    turned = (lane == tap - half).astype(jnp.float32).astype(jnp.bfloat16)
    lines_ref[0] = dot(taps, turned if adjoint else plain)
    lines_ref[1] = dot(taps, plain if adjoint else turned)
    apart = lax.broadcasted_iota(jnp.int32, (side, side), 0) - lax.broadcasted_iota(
        jnp.int32, (side, side), 1
    )
    band = jnp.abs(apart) <= half

    def one(k, carry):
        for c in range(2):
            line = jnp.broadcast_to(lines_ref[c, pl.ds(2 * k + c, 1), :], (side, side))
            rows = pltpu.roll(line, 0, 1, stride=1, stride_axis=0)
            basis_ref[c * kinds + k] = jnp.where(band, rows, 0.0).astype(jnp.bfloat16)
        return carry

    lax.fori_loop(0, kinds, one, 0)


def fill_tables(sizes, inter_ref, counts_ref, coeff_ref, slots_ref, weights_ref):
    tiles, filters, local = sizes
    fields = inter_ref.shape[3]
    own = lax.axis_index("tile")
    first = lax.axis_index("filt") * local
    row_id = lax.broadcasted_iota(jnp.int32, (tiles, NB), 0)
    lane_id = lax.broadcasted_iota(jnp.int32, (1, filters), 1)
    for w in range(2 * REACH + 1):
        tile = jnp.clip(own + w - REACH, 0, tiles - 1)
        live = counts_ref[pl.ds(tile, 1), :]
        for f in range(local):
            row = w * local + f
            for q in range(K):
                entry = inter_ref[first + f, q, pl.ds(tile, 1), :]
                slots_ref[row : row + 1, STEP * q : STEP * q + fields] = entry
            count = jnp.sum(jnp.where(lane_id == first + f, live, 0).astype(jnp.float32), 1, keepdims=True)
            slots_ref[row : row + 1, STEP * K : STEP * K + 1] = count.astype(jnp.int32)
            for c in range(3):
                block = coeff_ref[first + f, c].astype(jnp.float32)
                picked = jnp.sum(jnp.where(row_id == tile, block, 0.0), 0, keepdims=True)
                weights_ref[row : row + 1, STEP * c : STEP * c + NB] = picked


def find_slot(slots_ref, row, expo):
    live = slots_ref[row, STEP * K]
    base = jnp.int32(0)
    found = jnp.int32(0)
    for q in range(K):
        hit = (q < live) & (slots_ref[row, STEP * q] == expo)
        base = jnp.where(hit, STEP * q, base)
        found = jnp.where(hit, 1, found)
    return found, base


def weight(weights_ref, row, b, row_centred, col_centred):
    flat = weights_ref[row, b] + weights_ref[row, STEP + b] * row_centred
    return flat + weights_ref[row, 2 * STEP + b] * col_centred


def centred_axes(side, oy, ox):
    rows = lax.broadcasted_iota(jnp.int32, (side, 1), 0) + oy
    cols = lax.broadcasted_iota(jnp.int32, (1, side), 1) + ox
    return (
        (2 * rows + 1 - side).astype(jnp.float32) / side,
        (2 * cols + 1 - side).astype(jnp.float32) / side,
    )


def diagonal(side, by):
    apart = lax.broadcasted_iota(jnp.int32, (side, side), 1) - lax.broadcasted_iota(
        jnp.int32, (side, side), 0
    )
    return (apart == by).astype(jnp.float32).astype(jnp.bfloat16)


def dot(a, b):
    half = a.shape[0] // 2
    return jnp.concatenate(
        [
            jnp.dot(a[:half], b, preferred_element_type=jnp.float32),
            jnp.dot(a[half:], b, preferred_element_type=jnp.float32),
        ],
        0,
    )


def settle_contribution(image, oy, ox, pred_ref, f):
    side = image.shape[0]
    across = dot(image, diagonal(side, ox)).astype(jnp.bfloat16)
    pred_ref[f] = pred_ref[f] + dot(diagonal(side, -oy), across)


def contribution(slots_ref, weights_ref, basis_ref, row, base, place, image):
    side = image.shape[0]
    kinds = basis_ref.shape[0] // 2
    row_centred, col_centred = centred_axes(
        side, slots_ref[row, base + 1], slots_ref[row, base + 2]
    )
    total = jnp.zeros((side, side), jnp.float32)
    for b in range(NB):
        k = slots_ref[row, base + HEAD + b]
        half_blur = dot(basis_ref[k], image).astype(jnp.bfloat16)
        blurred = dot(half_blur, basis_ref[kinds + k])
        total = total + weight(weights_ref, place, b, row_centred, col_centred) * blurred
    return total.astype(jnp.bfloat16)


def bring_residual(image, oy, ox):
    side = image.shape[0]
    across = dot(image, diagonal(side, -ox)).astype(jnp.bfloat16)
    return dot(diagonal(side, oy), across)


def adjoint_term(slots_ref, weights_ref, basis_ref, row, base, place, moved):
    side = moved.shape[0]
    kinds = basis_ref.shape[0] // 2
    row_centred, col_centred = centred_axes(
        side, slots_ref[row, base + 1], slots_ref[row, base + 2]
    )
    total = jnp.zeros((side, side), jnp.float32)
    for b in range(NB):
        k = slots_ref[row, base + HEAD + b]
        w = weight(weights_ref, place, b, row_centred, col_centred)
        back_half = dot(basis_ref[k], (w * moved).astype(jnp.bfloat16)).astype(jnp.bfloat16)
        total = total + dot(back_half, basis_ref[kinds + k])
    return total


def source_of(own, move):
    distance, parity = move
    return own + jnp.where(lax.rem(own // distance, 2) == parity, distance, -distance)


def flipped(x, axis, move):
    distance, parity = move
    length = lax.axis_size(axis)
    firsts = [i for i in range(length - distance) if (i // distance) % 2 == parity]
    pairs = [(i, i + distance) for i in firsts] + [(i + distance, i) for i in firsts]
    return lax.ppermute(x, axis, pairs)


def gather_live(sizes, moves, backward, slots_ref, images, list_ref, held_ref):
    tiles, filters, local = sizes
    own = lax.axis_index("tile")
    live = jnp.int32(0)
    for move, image_ref in zip(moves, images):
        far = own if move is None else source_of(own, move)
        inside = jnp.where((far >= 0) & (far < tiles), 1, 0)
        here, there = REACH * local, jnp.clip(far - own + REACH, 0, 2 * REACH) * local
        tile_at, expo_at = (here, there) if backward else (there, here)
        expo = far if backward else own
        for f in range(local):
            found, base = find_slot(slots_ref, tile_at + f, expo)
            found = found * inside

            @pl.when(found == 1)
            def _():
                list_ref[0, live] = f
                list_ref[1, live] = tile_at + f
                list_ref[2, live] = base
                list_ref[3, live] = expo_at + f
                held_ref[live] = image_ref[f]

            live = live + found
    return live


def forward_slots(sizes, moves, slots_ref, weights_ref, basis_ref, images, pred_ref, scratch):
    list_ref, held_ref, ready_ref = scratch
    live = gather_live(sizes, moves, False, slots_ref, images, list_ref, held_ref)

    @pl.when(live > 0)
    def _():
        def blur(n):
            ready_ref[...] = contribution(
                slots_ref,
                weights_ref,
                basis_ref,
                list_ref[1, n],
                list_ref[2, n],
                list_ref[3, n],
                held_ref[n],
            )

        def settle(n):
            row, base = list_ref[1, n], list_ref[2, n]
            oy, ox = slots_ref[row, base + 1], slots_ref[row, base + 2]
            settle_contribution(ready_ref[...], oy, ox, pred_ref, list_ref[0, n])

        def one(n, carry):
            settle(n - 1)
            blur(n)
            return carry

        blur(0)
        lax.fori_loop(1, live, one, 0)
        settle(live - 1)


def backward_slots(sizes, moves, slots_ref, weights_ref, basis_ref, images, grad_ref, scratch):
    list_ref, held_ref, ready_ref = scratch
    live = gather_live(sizes, moves, True, slots_ref, images, list_ref, held_ref)

    @pl.when(live > 0)
    def _():
        def bring(n):
            row, base = list_ref[1, n], list_ref[2, n]
            return bring_residual(held_ref[n], slots_ref[row, base + 1], slots_ref[row, base + 2])

        def take(n):
            f = list_ref[0, n]
            grad_ref[f] = grad_ref[f] + adjoint_term(
                slots_ref,
                weights_ref,
                basis_ref,
                list_ref[1, n],
                list_ref[2, n],
                list_ref[3, n],
                ready_ref[...],
            )

        def one(n, carry):
            following = bring(n)
            take(n - 1)
            ready_ref[...] = following
            return carry

        ready_ref[...] = bring(0)
        lax.fori_loop(1, live, one, 0)
        take(live - 1)


def prepare(sizes, inter_ref, counts_ref, coeff_ref, taps_ref, *refs):
    slots_ref, weights_ref, forth_ref, back_ref, lines_ref = refs
    fill_tables(sizes, inter_ref, counts_ref, coeff_ref, slots_ref, weights_ref)
    build_basis(taps_ref, lines_ref, forth_ref, False)
    build_basis(taps_ref, lines_ref, back_ref, True)


def forward_own(sizes, slots_ref, weights_ref, basis_ref, image_ref, *refs):
    pred_ref, *scratch = refs
    pred_ref[...] = jnp.zeros_like(pred_ref)
    forward_slots(sizes, [None], slots_ref, weights_ref, basis_ref, [image_ref], pred_ref, scratch)


def forward_next(sizes, moves, slots_ref, weights_ref, basis_ref, *refs):
    images, (before_ref, pred_ref, *scratch) = refs[: len(moves)], refs[len(moves) :]
    del before_ref
    forward_slots(sizes, moves, slots_ref, weights_ref, basis_ref, images, pred_ref, scratch)


def forward_last(sizes, moves, slots_ref, weights_ref, basis_ref, *refs):
    images, refs = refs[: len(moves)], refs[len(moves) :]
    before_ref, observed_ref, inv_ref, pred_ref, resid_ref, *scratch = refs
    del before_ref
    forward_slots(sizes, moves, slots_ref, weights_ref, basis_ref, images, pred_ref, scratch)
    for f in range(observed_ref.shape[0]):
        gap = observed_ref[f].astype(jnp.float32) - pred_ref[f]
        resid_ref[f] = (inv_ref[f].astype(jnp.float32) * gap).astype(jnp.bfloat16)


def backward_own(
    sizes, samples, slots_ref, weights_ref, prec_ref, basis_ref, image_ref, *refs
):
    sample_ref, scale_ref, *refs = refs
    tiles, filters, local = sizes
    side = sample_ref.shape[1]
    part = lax.axis_index("filt")
    parts = filters // local
    first = part * local
    noises, refs = refs[:samples], refs[samples:]
    others, refs = refs[: parts - 1], refs[parts - 1 :]
    grad_ref, *refs = refs
    turns, scratch = refs[:samples], refs[samples:]
    for noise_ref, turn_ref in zip(noises, turns):
        turn_ref[...] = scale_ref[...] * noise_ref[...].astype(jnp.float32)
    for f in range(local):
        prior = jnp.zeros((side, side), jnp.float32)
        for g in range(local):
            prior = prior + prec_ref[first + f, first + g] * sample_ref[g]
        for r in range(1, parts):
            source = lax.rem(part + parts - r, parts) * local
            for g in range(local):
                far = others[r - 1][g].astype(jnp.float32)
                prior = prior + prec_ref[first + f, source + g] * far
        grad_ref[f] = -prior
    backward_slots(
        sizes, [None], slots_ref, weights_ref, basis_ref, [image_ref], grad_ref, scratch
    )


def backward_next(sizes, moves, slots_ref, weights_ref, basis_ref, *refs):
    images, (before_ref, grad_ref, *scratch) = refs[: len(moves)], refs[len(moves) :]
    del before_ref
    backward_slots(sizes, moves, slots_ref, weights_ref, basis_ref, images, grad_ref, scratch)


def body(
    sky_mean,
    sky_log_scale,
    noise_draw,
    observed,
    inv_var,
    intersections,
    counts,
    kernels,
    psf_coeffs,
    prior_prec,
):
    side = sky_mean.shape[2]
    local = sky_mean.shape[1]
    tiles, filters = counts.shape
    sizes = (tiles, filters, local)
    kinds = kernels.shape[0]
    started = [(d, parity) for d in range(1, REACH + 1) for parity in (0, 1)]
    last = (1, 1)
    early = [move for move in started if move != last]
    samples = lax.axis_size("mc")
    parts = lax.axis_size("filt")

    scale_map = jnp.exp(sky_log_scale[0])
    noise = noise_draw[0, 0]
    eps_float = noise.astype(jnp.float32)
    sample = sky_mean[0] + scale_map * eps_float
    sample_b = sample.astype(jnp.bfloat16)
    taps = kernels.reshape(2 * kinds, kernels.shape[2])

    image_f32 = jax.ShapeDtypeStruct((local, side, side), jnp.float32)
    image_b16 = jax.ShapeDtypeStruct((local, side, side), jnp.bfloat16)
    basis_type = jax.ShapeDtypeStruct((2 * kinds, side, side), jnp.bfloat16)
    cost = pl.CostEstimate(
        flops=2 * NB * 4 * side**3, bytes_accessed=8 * local * side * side, transcendentals=0
    )

    lines = pltpu.VMEM((2, 2 * kinds, side), jnp.float32)

    def slot_scratch(groups, ready):
        return [
            pltpu.SMEM((4, groups * local), jnp.int32),
            pltpu.VMEM((groups * local, side, side), jnp.bfloat16),
            pltpu.VMEM((side, side), ready),
        ]

    def call(kernel, name, outs, smem, vmem, scratch, aliases={}):
        return pl.pallas_call(
            kernel,
            out_shape=outs,
            in_specs=[SMEM] * len(smem) + [VMEM] * len(vmem),
            out_specs=[VMEM] * len(outs),
            scratch_shapes=scratch,
            input_output_aliases=aliases,
            compiler_params=pltpu.CompilerParams(vmem_limit_bytes=VMEM_BYTES),
            cost_estimate=cost,
            name=name,
        )(*smem, *vmem)

    near = {move: flipped(sample_b, "tile", move) for move in started}
    other_samples = [rotated(sample_b, "filt", r) for r in range(1, parts)]
    other_noise = [rotated(noise, "mc", r) for r in range(1, samples)]
    rows = -(-(2 * REACH + 1) * local // 8) * 8
    slots, weights, forth, back = call(
        functools.partial(prepare, sizes),
        "prepare",
        [
            jax.ShapeDtypeStruct((rows, LANES), jnp.int32),
            jax.ShapeDtypeStruct((rows, LANES), jnp.float32),
            basis_type,
            basis_type,
        ],
        (),
        (intersections.transpose(1, 2, 0, 3), counts, psf_coeffs.transpose(1, 3, 0, 2), taps),
        [lines],
    )
    tables = (slots, weights)
    (pred,) = call(
        functools.partial(forward_own, sizes),
        "forward_own",
        [image_f32],
        tables,
        (forth, sample_b),
        slot_scratch(1, jnp.bfloat16),
    )
    (pred,) = call(
        functools.partial(forward_next, sizes, early),
        "forward_next",
        [image_f32],
        tables,
        (forth, *[near[move] for move in early], pred),
        slot_scratch(len(early), jnp.bfloat16),
        {len(tables) + 1 + len(early): 0},
    )
    _, residual = call(
        functools.partial(forward_last, sizes, [last]),
        "forward_last",
        [image_f32, image_b16],
        tables,
        (forth, near[last], pred, observed[0], inv_var[0]),
        slot_scratch(1, jnp.bfloat16),
        {len(tables) + 2: 0},
    )
    near_resid = {move: flipped(residual, "tile", move) for move in started}
    grad, turn, *other_turns = call(
        functools.partial(backward_own, sizes, samples),
        "backward_own",
        [image_f32] * (1 + samples),
        tables + (prior_prec,),
        (back, residual, sample, scale_map, noise, *other_noise, *other_samples),
        slot_scratch(1, jnp.float32),
    )
    (grad,) = call(
        functools.partial(backward_next, sizes, early),
        "backward_next",
        [image_f32],
        tables,
        (back, *[near_resid[move] for move in early], grad),
        slot_scratch(len(early), jnp.float32),
        {len(tables) + 1 + len(early): 0},
    )
    (grad,) = call(
        functools.partial(backward_next, sizes, [last]),
        "backward_last",
        [image_f32],
        tables,
        (back, near_resid[last], grad),
        slot_scratch(1, jnp.float32),
        {len(tables) + 2: 0},
    )
    mean_sum = grad
    scale_sum = grad * turn
    for r in range(1, samples):
        other_grad = rotated(grad, "mc", r)
        mean_sum = mean_sum + other_grad
        scale_sum = scale_sum + other_grad * other_turns[r - 1]
    return ((mean_sum / samples)[None], (scale_sum / samples + 1.0)[None])

def solution(mesh):
    placed = (
        P("tile", "filt", None, None),
        P("tile", "filt", None, None),
        P("mc", "tile", "filt", None, None),
        P("tile", "filt", None, None),
        P("tile", "filt", None, None),
        P(),
        P(),
        P(),
        P(),
        P(),
    )
    return jax.shard_map(
        body,
        mesh=mesh,
        in_specs=placed,
        out_specs=(P("tile", "filt", None, None), P("tile", "filt", None, None)),
        check_vma=False,
    )
```

time: 60.1 us -> 62 us (1.032); the launches traced: 59.7 us -> 60.8 us
  Pallas kernels: 23.1 us -> 31.8 us
  local copies, waits for them, and re-layouts: 7.22 us -> 0.16 us
  waiting for transfers between devices: 6.6 us -> 4.63 us
  starting transfers between devices: 18.9 us -> 20.2 us
    pallas_call x6 -> x7, Pallas kernels: 23.1 us -> 31.8 us  [call(): pl.pallas_call(kernel, out_shape=outs, in_specs=[SMEM] * len(smem) + [VME...]
    reshape x4 -> x0, local copies, waits for them, and re-layouts: 4.82 us -> none  [the longest x2 2.96 us: body(): coeff_flat = psf_coeffs.astype(jnp.float32).reshape(-1)]
    unnamed x13 -> x18, local copies, waits for them, and re-layouts: 2.28 us -> 0.05 us
    ppermute x8, waiting for transfers between devices: 4.68 us -> 2.71 us  [flipped(): return lax.ppermute(x, axis, pairs)]
    ppermute x8, starting transfers between devices: 14.4 us -> 15.6 us  [flipped(): return lax.ppermute(x, axis, pairs)]
  transfers between devices with their start and end apart: 11 -> 11, of which waited for: 5 -> 2; matrix products, arithmetic and copies ran while one was open for 11% -> 0% of each run, Pallas kernels for 35% -> 48%
where the time goes in v2:
time: 62 us; the launch traced here: 60.8 us
  Pallas kernels  31.8 us (51%)
  starting transfers between devices  20.2 us (33%)
  waiting for transfers between devices  4.63 us (7%)
  other arithmetic  3.08 us (5%)
  between operations  0.91 us (1%)
    pallas_call x7, Pallas kernels, call(): pl.pallas_call(kernel, out_shape=outs, in_specs=[SMEM] * len(smem) + [VME...  31.8 us
    ppermute x8, starting transfers between devices, flipped(): return lax.ppermute(x, axis, pairs)  15.6 us
    ppermute x3, starting transfers between devices, rotated(): lax.ppermute(x, axis, [(i, (i + by) % length) for i in range(length)])  4.62 us
    ppermute x8, waiting for transfers between devices, flipped(): return lax.ppermute(x, axis, pairs)  2.71 us
    ppermute x3, waiting for transfers between devices, rotated(): lax.ppermute(x, axis, [(i, (i + by) % length) for i in range(length)])  1.92 us
    convert_element_type x1, other arithmetic, body(): sample_b = sample.astype(jnp.bfloat16)  1.68 us
    broadcast_in_dim x1, other arithmetic, body(): return ((mean_sum / samples)[None], (scale_sum / samples + 1.0)[None])  1.39 us
  transfers between devices with their start and end apart: 11, of which 2 were waited for; matrix products, arithmetic and copies ran while one was open for 0% of the time, Pallas kernels for 48%

profile of v2, /device:TPU:17, one launch (start us, length us, event | category | flops | bytes accessed | tf_op | source)
XLA Modules:
  0.0 60.8 jit_solution(12893889812001226410)
XLA Ops:
  0.7 1.7 %fusion = (bf16[3,256,256]{2,1,0:T(8,128)(2,1)S(1)}, f32[3,256,256]{2,1,0:T(8,128)S(1)}) fusion(bf16[1,1,3,256,256]{4,3,2,1,0:T(8,128)(2,1)} %param.12, f32[1,3,256,256]{3,2,1,0:T(8,128)} %param.11, f32[1,3,256,256]{3,2,1,0:T(8,128)} %param.10), kind=kLoop, calls=%fused_computation.4 | loop fusion | flops 786432 | bytes 3145728 | tf_op jit(solution)/shard_map/convert_element_type | solution.py:363
  2.4 1.3 %collective-permute-start.1 = (bf16[3,256,256]{2,1,0:T(8,128)(2,1)S(1)}, bf16[3,256,256]{2,1,0:T(8,128)(2,1)S(1)}, u32[]{:S(2)}, u32[]{:S(2)}) collective-permute-start(bf16[3,256,256]{2,1,0:T(8,128)(2,1)S(1)} %get-tuple-element.18.image_ref), channel_id=1, source_target_pairs={{0,4},{8,12},{16,20},{24,28},{4,0},{12,8},{20,16},{28,24},{1,5},{9... | collective-permute-start | bytes 1179656 | tf_op jit(solution)/shard_map/ppermute | solution.py:177
  3.7 1.3 %collective-permute-start.2 = (bf16[3,256,256]{2,1,0:T(8,128)(2,1)S(1)}, bf16[3,256,256]{2,1,0:T(8,128)(2,1)S(1)}, u32[]{:S(2)}, u32[]{:S(2)}) collective-permute-start(bf16[3,256,256]{2,1,0:T(8,128)(2,1)S(1)} %get-tuple-element.18.image_ref), channel_id=1, source_target_pairs={{0,8},{4,12},{16,24},{20,28},{8,0},{12,4},{24,16},{28,20},{1,9},{5... | collective-permute-start | bytes 1179656 | tf_op jit(solution)/shard_map/ppermute | solution.py:177
  5.0 1.9 %collective-permute-start.3 = (bf16[3,256,256]{2,1,0:T(8,128)(2,1)S(1)}, bf16[3,256,256]{2,1,0:T(8,128)(2,1)S(1)}, u32[]{:S(2)}, u32[]{:S(2)}) collective-permute-start(bf16[3,256,256]{2,1,0:T(8,128)(2,1)S(1)} %get-tuple-element.18.image_ref), channel_id=1, source_target_pairs={{8,16},{12,20},{16,8},{20,12},{9,17},{13,21},{17,9},{21,13},{10,18... | collective-permute-start | bytes 1179656 | tf_op jit(solution)/shard_map/ppermute | solution.py:177
  6.9 3.3 %collective-permute-start = (bf16[3,256,256]{2,1,0:T(8,128)(2,1)S(1)}, bf16[3,256,256]{2,1,0:T(8,128)(2,1)S(1)}, u32[]{:S(2)}, u32[]{:S(2)}) collective-permute-start(bf16[3,256,256]{2,1,0:T(8,128)(2,1)S(1)} %get-tuple-element.18.image_ref), channel_id=1, source_target_pairs={{4,8},{12,16},{20,24},{8,4},{16,12},{24,20},{5,9},{13,17},{21,25},... | collective-permute-start | bytes 1179656 | tf_op jit(solution)/shard_map/ppermute | solution.py:177
  10.2 1.3 %collective-permute-start.9 = (bf16[3,256,256]{2,1,0:T(8,128)(2,1)S(1)}, bf16[3,256,256]{2,1,0:T(8,128)(2,1)S(1)}, u32[]{:S(2)}, u32[]{:S(2)}) collective-permute-start(bf16[3,256,256]{2,1,0:T(8,128)(2,1)S(1)} %get-tuple-element.18.image_ref), channel_id=1, source_target_pairs={{0,2},{2,0},{1,3},{3,1},{4,6},{6,4},{5,7},{7,5},{8,10},{10,8},{9,1... | collective-permute-start | bytes 1179656 | tf_op jit(solution)/shard_map/ppermute | solution.py:29
  11.5 2.4 %prepare.1 = (s32[16,128]{1,0:T(8,128)S(1)}, f32[16,128]{1,0:T(8,128)S(1)}, bf16[16,256,256]{2,1,0:T(8,128)(2,1)S(1)}, bf16[16,256,256]{2,1,0:T(8,128)(2,1)S(1)}) custom-call(s32[6,3,8,9]{3,2,1,0:T(8,128)S(1)} %bitcast.24, s32[8,6]{1,0:T(8,128)S(1)} %copy-done.7, bf16[6,3,8,6]{3,2,1,0:T(8,128)(2,1)S(1)} %bitcast.25, f32[16,25]{1,0:T(8,128)S(1)} %bitcast.26), custom_call_target="tpu_custom_call" | custom-call | flops 805306368 | bytes 1572864 | tf_op jit(solution)/shard_map/prepare/pallas_call | solution.py:383
  13.9 0.0 copy-start
  13.9 2.4 %forward_own.1.refs_3_ = f32[3,256,256]{2,1,0:T(8,128)S(1)} custom-call(s32[16,128]{1,0:T(8,128)S(1)} %get-tuple-element.10.slots_ref, f32[16,128]{1,0:T(8,128)S(1)} %get-tuple-element.11.weights_ref, bf16[16,256,256]{2,1,0:T(8,128)(2,1)S(1)} %get-tuple-element.13.basis_ref, bf16[3,256,256]{2,1,0:T(8,128)(2,1)S(1)} %get-tuple-element.18.image_ref), custom_call_target="tpu_custom_call" | custom-call | flops 805306368 | bytes 1572864 | tf_op jit(solution)/shard_map/forward_own/pallas_call | solution.py:383
  16.3 0.0 collective-permute-done.1.refs_0_
  16.3 0.0 copy-start.1
  16.4 0.0 copy-start.2
  16.4 2.1 %collective-permute-start.8 = (bf16[3,256,256]{2,1,0:T(8,128)(2,1)S(1)}, bf16[3,256,256]{2,1,0:T(8,128)(2,1)S(1)}, u32[]{:S(2)}, u32[]{:S(2)}) collective-permute-start(bf16[3,256,256]{2,1,0:T(8,128)(2,1)S(1)} %bitcast.20), channel_id=1, source_target_pairs={{0,1},{1,0},{2,3},{3,2},{4,5},{5,4},{6,7},{7,6},{8,9},{9,8},{10,11... | collective-permute-start | bytes 1179656 | tf_op jit(solution)/shard_map/ppermute | solution.py:29
  18.5 11.0 %forward_next.1.refs_1_ = f32[3,256,256]{2,1,0:T(8,128)S(1)} custom-call(s32[16,128]{1,0:T(8,128)S(1)} %get-tuple-element.10.slots_ref, f32[16,128]{1,0:T(8,128)S(1)} %get-tuple-element.11.weights_ref, bf16[16,256,256]{2,1,0:T(8,128)(2,1)S(1)} %get-tuple-element.13.basis_ref, ...), custom_call_target="tpu_custom_call", output_to_operand_aliasing={{}: (6, {})} | custom-call | flops 805306368 | bytes 1572864 | tf_op jit(solution)/shard_map/forward_next/pallas_call | solution.py:383
  29.5 0.0 copy-start.8
  29.5 0.0 collective-permute-done.refs_0_
  29.6 0.0 copy-start.3
  29.6 1.0 %forward_last.1 = (f32[3,256,256]{2,1,0:T(8,128)S(1)}, bf16[3,256,256]{2,1,0:T(8,128)(2,1)S(1)}) custom-call(s32[16,128]{1,0:T(8,128)S(1)} %get-tuple-element.10.slots_ref, f32[16,128]{1,0:T(8,128)S(1)} %get-tuple-element.11.weights_ref, bf16[16,256,256]{2,1,0:T(8,128)(2,1)S(1)} %get-tuple-element.13.basis_ref, ...), custom_call_target="tpu_custom_call", output_to_operand_aliasing={{0}: (4, {})} | custom-call | flops 805306368 | bytes 1572864 | tf_op jit(solution)/shard_map/forward_last/pallas_call | solution.py:383
  30.6 0.1 collective-permute-start.5
  30.7 1.3 %collective-permute-start.6 = (bf16[3,256,256]{2,1,0:T(8,128)(2,1)S(1)}, bf16[3,256,256]{2,1,0:T(8,128)(2,1)S(1)}, u32[]{:S(2)}, u32[]{:S(2)}) collective-permute-start(bf16[3,256,256]{2,1,0:T(8,128)(2,1)S(1)} %get-tuple-element.14.image_ref), channel_id=1, source_target_pairs={{0,8},{4,12},{16,24},{20,28},{8,0},{12,4},{24,16},{28,20},{1,9},{5... | collective-permute-start | bytes 1179656 | tf_op jit(solution)/shard_map/ppermute | solution.py:177
  32.0 1.9 %collective-permute-start.7 = (bf16[3,256,256]{2,1,0:T(8,128)(2,1)S(1)}, bf16[3,256,256]{2,1,0:T(8,128)(2,1)S(1)}, u32[]{:S(2)}, u32[]{:S(2)}) collective-permute-start(bf16[3,256,256]{2,1,0:T(8,128)(2,1)S(1)} %get-tuple-element.14.image_ref), channel_id=1, source_target_pairs={{8,16},{12,20},{16,8},{20,12},{9,17},{13,21},{17,9},{21,13},{10,18... | collective-permute-start | bytes 1179656 | tf_op jit(solution)/shard_map/ppermute | solution.py:177
  33.9 0.0 collective-permute-done.9.refs_4_
  33.9 4.5 %collective-permute-start.4 = (bf16[3,256,256]{2,1,0:T(8,128)(2,1)S(1)}, bf16[3,256,256]{2,1,0:T(8,128)(2,1)S(1)}, u32[]{:S(2)}, u32[]{:S(2)}) collective-permute-start(bf16[3,256,256]{2,1,0:T(8,128)(2,1)S(1)} %get-tuple-element.14.image_ref), channel_id=1, source_target_pairs={{4,8},{12,16},{20,24},{8,4},{16,12},{24,20},{5,9},{13,17},{21,25},... | collective-permute-start | bytes 1179656 | tf_op jit(solution)/shard_map/ppermute | solution.py:177
  38.4 0.1 exponential_bitcast_fusion.refs_1_
  38.5 3.0 %backward_own.1 = (f32[3,256,256]{2,1,0:T(8,128)S(1)}, f32[3,256,256]{2,1,0:T(8,128)S(1)}, f32[3,256,256]{2,1,0:T(8,128)S(1)}) custom-call(s32[16,128]{1,0:T(8,128)S(1)} %get-tuple-element.10.slots_ref, f32[16,128]{1,0:T(8,128)S(1)} %get-tuple-element.11.weights_ref, f32[6,6]{1,0:T(8,128)S(1)} %copy-done.3, ...), custom_call_target="tpu_custom_call" | custom-call | flops 805306368 | bytes 1572864 | tf_op jit(solution)/shard_map/backward_own/pallas_call | solution.py:383
  41.6 0.0 collective-permute-done.6.refs_1_
  41.6 2.7 %collective-permute-done.7.refs_2_ = bf16[3,256,256]{2,1,0:T(8,128)(2,1)S(1)} collective-permute-done((bf16[3,256,256]{2,1,0:T(8,128)(2,1)S(1)}, bf16[3,256,256]{2,1,0:T(8,128)(2,1)S(1)}, u32[]{:S(2)}, u32[]{:S(2)}) %collective-permute-start.7) | collective-permute-done | bytes 393248 | tf_op jit(solution)/shard_map/ppermute | solution.py:177
  44.3 9.6 %backward_next.1.refs_1_ = f32[3,256,256]{2,1,0:T(8,128)S(1)} custom-call(s32[16,128]{1,0:T(8,128)S(1)} %get-tuple-element.10.slots_ref, f32[16,128]{1,0:T(8,128)S(1)} %get-tuple-element.11.weights_ref, bf16[16,256,256]{2,1,0:T(8,128)(2,1)S(1)} %get-tuple-element.12.basis_ref, ...), custom_call_target="tpu_custom_call", output_to_operand_aliasing={{}: (6, {})} | custom-call | flops 805306368 | bytes 1572864 | tf_op jit(solution)/shard_map/backward_next/pallas_call | solution.py:383
  53.9 2.4 %backward_last.1 = f32[3,256,256]{2,1,0:T(8,128)S(1)} custom-call(s32[16,128]{1,0:T(8,128)S(1)} %get-tuple-element.10.slots_ref, f32[16,128]{1,0:T(8,128)S(1)} %get-tuple-element.11.weights_ref, bf16[16,256,256]{2,1,0:T(8,128)(2,1)S(1)} %get-tuple-element.12.basis_ref, ...), custom_call_target="tpu_custom_call", output_to_operand_aliasing={{}: (4, {})} | custom-call | flops 805306368 | bytes 1572864 | tf_op jit(solution)/shard_map/backward_last/pallas_call | solution.py:383
  56.3 1.2 %collective-permute-start.10 = (f32[3,256,256]{2,1,0:T(8,128)S(1)}, f32[3,256,256]{2,1,0:T(8,128)S(1)}, u32[]{:S(2)}, u32[]{:S(2)}) collective-permute-start(f32[3,256,256]{2,1,0:T(8,128)S(1)} %backward_last.1), channel_id=1, source_target_pairs={{0,1},{1,0},{2,3},{3,2},{4,5},{5,4},{6,7},{7,6},{8,9},{9,8},{10,11... | collective-permute-start | bytes 2359304 | tf_op jit(solution)/shard_map/ppermute | solution.py:29
  57.5 1.9 %collective-permute-done.10 = f32[3,256,256]{2,1,0:T(8,128)S(1)} collective-permute-done((f32[3,256,256]{2,1,0:T(8,128)S(1)}, f32[3,256,256]{2,1,0:T(8,128)S(1)}, u32[]{:S(2)}, u32[]{:S(2)}) %collective-permute-start.10) | collective-permute-done | bytes 786464 | tf_op jit(solution)/shard_map/ppermute | solution.py:29
  59.4 1.4 %add_bitcast_fusion = (f32[1,3,256,256]{3,2,1,0:T(8,128)}, f32[1,3,256,256]{3,2,1,0:T(8,128)}) fusion(f32[3,256,256]{2,1,0:T(8,128)S(1)} %collective-permute-done.10, f32[3,256,256]{2,1,0:T(8,128)S(1)} %get-tuple-element.17, f32[3,256,256]{2,1,0:T(8,128)S(1)} %backward_last.1, f32[3,256,256]{2,1,0:T(8,128)S(1)} %get-tuple-element.16), kind=kLoop, calls=%fused_computation.1 | loop fusion | flops 1376256 | bytes 4718592 | tf_op jit(solution)/shard_map/broadcast_in_dim | solution.py:472
  (18 shorter events, 0.0 us)
Async XLA Ops:
  0.6 10.8 %copy-start.4 = (s32[8,6,3,9]{3,0,2,1:T(8,128)S(1)}, s32[8,6,3,9]{3,0,2,1:T(8,128)}, u32[]{:S(2)}) copy-start(s32[8,6,3,9]{3,0,2,1:T(8,128)} %param.15) | copy-start | bytes 15556
  0.6 10.8 %copy-start.5 = (bf16[8,6,6,3]{2,0,3,1:T(8,128)(2,1)S(1)}, bf16[8,6,6,3]{2,0,3,1:T(8,128)(2,1)}, u32[]{:S(2)}) copy-start(bf16[8,6,6,3]{2,0,3,1:T(8,128)(2,1)} %param.18) | copy-start | bytes 5188
  0.7 10.8 %copy-start.6 = (f32[8,2,25]{2,1,0:T(2,128)S(1)}, f32[8,2,25]{2,1,0:T(2,128)}, u32[]{:S(2)}) copy-start(f32[8,2,25]{2,1,0:T(2,128)} %param.17) | copy-start | bytes 4804
  0.7 10.8 %copy-start.7 = (s32[8,6]{1,0:T(8,128)S(1)}, s32[8,6]{1,0:T(8,128)}, u32[]{:S(2)}) copy-start(s32[8,6]{1,0:T(8,128)} %counts_ref.1) | copy-start | bytes 580
  2.4 14.0 %collective-permute-start.1 = (bf16[3,256,256]{2,1,0:T(8,128)(2,1)S(1)}, bf16[3,256,256]{2,1,0:T(8,128)(2,1)S(1)}, u32[]{:S(2)}, u32[]{:S(2)}) collective-permute-start(bf16[3,256,256]{2,1,0:T(8,128)(2,1)S(1)} %get-tuple-element.18.image_ref), channel_id=1, source_target_pairs={{0,4},{8,12},{16,20},{24,28},{4,0},{12,8},{20,16},{28,24},{1,5},{9... | collective-permute-start | bytes 1179656 | tf_op jit(solution)/shard_map/ppermute | solution.py:177
  3.7 14.8 %collective-permute-start.2 = (bf16[3,256,256]{2,1,0:T(8,128)(2,1)S(1)}, bf16[3,256,256]{2,1,0:T(8,128)(2,1)S(1)}, u32[]{:S(2)}, u32[]{:S(2)}) collective-permute-start(bf16[3,256,256]{2,1,0:T(8,128)(2,1)S(1)} %get-tuple-element.18.image_ref), channel_id=1, source_target_pairs={{0,8},{4,12},{16,24},{20,28},{8,0},{12,4},{24,16},{28,20},{1,9},{5... | collective-permute-start | bytes 1179656 | tf_op jit(solution)/shard_map/ppermute | solution.py:177
  5.0 13.6 %collective-permute-start.3 = (bf16[3,256,256]{2,1,0:T(8,128)(2,1)S(1)}, bf16[3,256,256]{2,1,0:T(8,128)(2,1)S(1)}, u32[]{:S(2)}, u32[]{:S(2)}) collective-permute-start(bf16[3,256,256]{2,1,0:T(8,128)(2,1)S(1)} %get-tuple-element.18.image_ref), channel_id=1, source_target_pairs={{8,16},{12,20},{16,8},{20,12},{9,17},{13,21},{17,9},{21,13},{10,18... | collective-permute-start | bytes 1179656 | tf_op jit(solution)/shard_map/ppermute | solution.py:177
  6.9 22.7 %collective-permute-start = (bf16[3,256,256]{2,1,0:T(8,128)(2,1)S(1)}, bf16[3,256,256]{2,1,0:T(8,128)(2,1)S(1)}, u32[]{:S(2)}, u32[]{:S(2)}) collective-permute-start(bf16[3,256,256]{2,1,0:T(8,128)(2,1)S(1)} %get-tuple-element.18.image_ref), channel_id=1, source_target_pairs={{4,8},{12,16},{20,24},{8,4},{16,12},{24,20},{5,9},{13,17},{21,25},... | collective-permute-start | bytes 1179656 | tf_op jit(solution)/shard_map/ppermute | solution.py:177
  10.2 23.7 %collective-permute-start.9 = (bf16[3,256,256]{2,1,0:T(8,128)(2,1)S(1)}, bf16[3,256,256]{2,1,0:T(8,128)(2,1)S(1)}, u32[]{:S(2)}, u32[]{:S(2)}) collective-permute-start(bf16[3,256,256]{2,1,0:T(8,128)(2,1)S(1)} %get-tuple-element.18.image_ref), channel_id=1, source_target_pairs={{0,2},{2,0},{1,3},{3,1},{4,6},{6,4},{5,7},{7,5},{8,10},{10,8},{9,1... | collective-permute-start | bytes 1179656 | tf_op jit(solution)/shard_map/ppermute | solution.py:29
  13.9 2.5 %copy-start = (bf16[1,1,3,256,256]{4,3,2,1,0:T(8,128)(2,1)S(1)}, bf16[1,1,3,256,256]{4,3,2,1,0:T(8,128)(2,1)}, u32[]{:S(2)}) copy-start(bf16[1,1,3,256,256]{4,3,2,1,0:T(8,128)(2,1)} %param.12) | copy-start | bytes 1179652
  16.3 13.2 %copy-start.1 = (bf16[1,3,256,256]{3,2,1,0:T(8,128)(2,1)S(1)}, bf16[1,3,256,256]{3,2,1,0:T(8,128)(2,1)}, u32[]{:S(2)}) copy-start(bf16[1,3,256,256]{3,2,1,0:T(8,128)(2,1)} %param.13) | copy-start | bytes 1179652
  16.4 13.2 %copy-start.2 = (bf16[1,3,256,256]{3,2,1,0:T(8,128)(2,1)S(1)}, bf16[1,3,256,256]{3,2,1,0:T(8,128)(2,1)}, u32[]{:S(2)}) copy-start(bf16[1,3,256,256]{3,2,1,0:T(8,128)(2,1)} %param.14) | copy-start | bytes 1179652
  16.4 22.2 %collective-permute-start.8 = (bf16[3,256,256]{2,1,0:T(8,128)(2,1)S(1)}, bf16[3,256,256]{2,1,0:T(8,128)(2,1)S(1)}, u32[]{:S(2)}, u32[]{:S(2)}) collective-permute-start(bf16[3,256,256]{2,1,0:T(8,128)(2,1)S(1)} %bitcast.20), channel_id=1, source_target_pairs={{0,1},{1,0},{2,3},{3,2},{4,5},{5,4},{6,7},{7,6},{8,9},{9,8},{10,11... | collective-permute-start | bytes 1179656 | tf_op jit(solution)/shard_map/ppermute | solution.py:29
  29.5 8.9 %copy-start.8 = (f32[1,3,256,256]{3,2,1,0:T(8,128)S(1)}, f32[1,3,256,256]{3,2,1,0:T(8,128)}, u32[]{:S(2)}) copy-start(f32[1,3,256,256]{3,2,1,0:T(8,128)} %param.11) | copy-start | bytes 2359300
  29.6 9.0 %copy-start.3 = (f32[6,6]{1,0:T(8,128)S(1)}, f32[6,6]{1,0:T(8,128)}, u32[]{:S(2)}) copy-start(f32[6,6]{1,0:T(8,128)} %prec_ref.1) | copy-start | bytes 436
  30.6 11.0 %collective-permute-start.5 = (bf16[3,256,256]{2,1,0:T(8,128)(2,1)S(1)}, bf16[3,256,256]{2,1,0:T(8,128)(2,1)S(1)}, u32[]{:S(2)}, u32[]{:S(2)}) collective-permute-start(bf16[3,256,256]{2,1,0:T(8,128)(2,1)S(1)} %get-tuple-element.14.image_ref), channel_id=1, source_target_pairs={{0,4},{8,12},{16,20},{24,28},{4,0},{12,8},{20,16},{28,24},{1,5},{9... | collective-permute-start | bytes 1179656 | tf_op jit(solution)/shard_map/ppermute | solution.py:177
  30.7 10.9 %collective-permute-start.6 = (bf16[3,256,256]{2,1,0:T(8,128)(2,1)S(1)}, bf16[3,256,256]{2,1,0:T(8,128)(2,1)S(1)}, u32[]{:S(2)}, u32[]{:S(2)}) collective-permute-start(bf16[3,256,256]{2,1,0:T(8,128)(2,1)S(1)} %get-tuple-element.14.image_ref), channel_id=1, source_target_pairs={{0,8},{4,12},{16,24},{20,28},{8,0},{12,4},{24,16},{28,20},{1,9},{5... | collective-permute-start | bytes 1179656 | tf_op jit(solution)/shard_map/ppermute | solution.py:177
  32.0 12.3 %collective-permute-start.7 = (bf16[3,256,256]{2,1,0:T(8,128)(2,1)S(1)}, bf16[3,256,256]{2,1,0:T(8,128)(2,1)S(1)}, u32[]{:S(2)}, u32[]{:S(2)}) collective-permute-start(bf16[3,256,256]{2,1,0:T(8,128)(2,1)S(1)} %get-tuple-element.14.image_ref), channel_id=1, source_target_pairs={{8,16},{12,20},{16,8},{20,12},{9,17},{13,21},{17,9},{21,13},{10,18... | collective-permute-start | bytes 1179656 | tf_op jit(solution)/shard_map/ppermute | solution.py:177
  33.9 20.0 %collective-permute-start.4 = (bf16[3,256,256]{2,1,0:T(8,128)(2,1)S(1)}, bf16[3,256,256]{2,1,0:T(8,128)(2,1)S(1)}, u32[]{:S(2)}, u32[]{:S(2)}) collective-permute-start(bf16[3,256,256]{2,1,0:T(8,128)(2,1)S(1)} %get-tuple-element.14.image_ref), channel_id=1, source_target_pairs={{4,8},{12,16},{20,24},{8,4},{16,12},{24,20},{5,9},{13,17},{21,25},... | collective-permute-start | bytes 1179656 | tf_op jit(solution)/shard_map/ppermute | solution.py:177
  56.3 3.1 %collective-permute-start.10 = (f32[3,256,256]{2,1,0:T(8,128)S(1)}, f32[3,256,256]{2,1,0:T(8,128)S(1)}, u32[]{:S(2)}, u32[]{:S(2)}) collective-permute-start(f32[3,256,256]{2,1,0:T(8,128)S(1)} %backward_last.1), channel_id=1, source_target_pairs={{0,1},{1,0},{2,3},{3,2},{4,5},{5,4},{6,7},{7,6},{8,9},{9,8},{10,11... | collective-permute-start | bytes 2359304 | tf_op jit(solution)/shard_map/ppermute | solution.py:29

commit v3 on v2

--- a/solution.py
+++ b/solution.py
@@ -112,14 +112,7 @@
 
 
 def dot(a, b):
-    half = a.shape[0] // 2
-    return jnp.concatenate(
-        [
-            jnp.dot(a[:half], b, preferred_element_type=jnp.float32),
-            jnp.dot(a[half:], b, preferred_element_type=jnp.float32),
-        ],
-        0,
-    )
+    return jnp.dot(a, b, preferred_element_type=jnp.float32)
 
 
 def settle_contribution(image, oy, ox, pred_ref, f):
@@ -135,10 +128,10 @@
         side, slots_ref[row, base + 1], slots_ref[row, base + 2]
     )
     total = jnp.zeros((side, side), jnp.float32)
+    chosen = [slots_ref[row, base + HEAD + b] for b in range(NB)]
+    half_blurs = dot(jnp.concatenate([basis_ref[k] for k in chosen], 0), image).astype(jnp.bfloat16)
     for b in range(NB):
-        k = slots_ref[row, base + HEAD + b]
-        half_blur = dot(basis_ref[k], image).astype(jnp.bfloat16)
-        blurred = dot(half_blur, basis_ref[kinds + k])
+        blurred = dot(half_blurs[b * side : (b + 1) * side], basis_ref[kinds + chosen[b]])
         total = total + weight(weights_ref, place, b, row_centred, col_centred) * blurred
     return total.astype(jnp.bfloat16)
 
@@ -297,34 +290,39 @@
         resid_ref[f] = (inv_ref[f].astype(jnp.float32) * gap).astype(jnp.bfloat16)
 
 
-def backward_own(
-    sizes, samples, slots_ref, weights_ref, prec_ref, basis_ref, image_ref, *refs
-):
-    sample_ref, scale_ref, *refs = refs
+def subtract_prior(sizes, prec_ref, sample_ref, others, grad_ref):
     tiles, filters, local = sizes
-    side = sample_ref.shape[1]
     part = lax.axis_index("filt")
     parts = filters // local
     first = part * local
-    noises, refs = refs[:samples], refs[samples:]
-    others, refs = refs[: parts - 1], refs[parts - 1 :]
-    grad_ref, *refs = refs
-    turns, scratch = refs[:samples], refs[samples:]
-    for noise_ref, turn_ref in zip(noises, turns):
-        turn_ref[...] = scale_ref[...] * noise_ref[...].astype(jnp.float32)
     for f in range(local):
-        prior = jnp.zeros((side, side), jnp.float32)
+        grad = grad_ref[f]
         for g in range(local):
-            prior = prior + prec_ref[first + f, first + g] * sample_ref[g]
+            grad = grad - prec_ref[first + f, first + g] * sample_ref[g]
         for r in range(1, parts):
             source = lax.rem(part + parts - r, parts) * local
             for g in range(local):
                 far = others[r - 1][g].astype(jnp.float32)
-                prior = prior + prec_ref[first + f, source + g] * far
-        grad_ref[f] = -prior
+                grad = grad - prec_ref[first + f, source + g] * far
+        grad_ref[f] = grad
+
+
+def backward_own(sizes, samples, slots_ref, weights_ref, basis_ref, image_ref, *refs):
+    scale_ref, *refs = refs
+    noises, (grad_ref, *refs) = refs[:samples], refs[samples:]
+    turns, scratch = refs[:samples], refs[samples:]
+    for noise_ref, turn_ref in zip(noises, turns):
+        turn_ref[...] = scale_ref[...] * noise_ref[...].astype(jnp.float32)
+    grad_ref[...] = jnp.zeros_like(grad_ref)
     backward_slots(
         sizes, [None], slots_ref, weights_ref, basis_ref, [image_ref], grad_ref, scratch
     )
+
+
+def backward_prior(sizes, prec_ref, before_ref, sample_ref, *refs):
+    others, (grad_ref,) = refs[:-1], refs[-1:]
+    del before_ref
+    subtract_prior(sizes, prec_ref, sample_ref, others, grad_ref)
 
 
 def backward_next(sizes, moves, slots_ref, weights_ref, basis_ref, *refs):
@@ -393,7 +391,6 @@
         )(*smem, *vmem)
 
     near = {move: flipped(sample_b, "tile", move) for move in started}
-    other_samples = [rotated(sample_b, "filt", r) for r in range(1, parts)]
     other_noise = [rotated(noise, "mc", r) for r in range(1, samples)]
     rows = -(-(2 * REACH + 1) * local // 8) * 8
     slots, weights, forth, back = call(
@@ -441,10 +438,12 @@
         functools.partial(backward_own, sizes, samples),
         "backward_own",
         [image_f32] * (1 + samples),
-        tables + (prior_prec,),
-        (back, residual, sample, scale_map, noise, *other_noise, *other_samples),
+        tables,
+        (back, residual, scale_map, noise, *other_noise),
         slot_scratch(1, jnp.float32),
     )
+    late_b, grad = lax.optimization_barrier((sample_b, grad))
+    other_samples = [rotated(late_b, "filt", r) for r in range(1, parts)]
     (grad,) = call(
         functools.partial(backward_next, sizes, early),
         "backward_next",
@@ -453,6 +452,15 @@
         (back, *[near_resid[move] for move in early], grad),
         slot_scratch(len(early), jnp.float32),
         {len(tables) + 1 + len(early): 0},
+    )
+    (grad,) = call(
+        functools.partial(backward_prior, sizes),
+        "backward_prior",
+        [image_f32],
+        (prior_prec,),
+        (grad, sample, *other_samples),
+        [],
+        {1: 0},
     )
     (grad,) = call(
         functools.partial(backward_next, sizes, [last]),

time: 62 us -> 56.2 us (0.906); the launches traced: 60.8 us -> 56 us
  Pallas kernels: 31.8 us -> 26.7 us
  waiting for transfers between devices: 4.63 us -> 7.7 us
  starting transfers between devices: 20.2 us -> 17.5 us
    pallas_call x7 -> x8, Pallas kernels: 31.8 us -> 26.7 us  [call(): pl.pallas_call(kernel, out_shape=outs, in_specs=[SMEM] * len(smem) + [VME...]
    ppermute x8, waiting for transfers between devices: 2.71 us -> 5.79 us  [flipped(): return lax.ppermute(x, axis, pairs)]
    ppermute x8, starting transfers between devices: 15.6 us -> 13.4 us  [flipped(): return lax.ppermute(x, axis, pairs)]
  transfers between devices with their start and end apart: 11 -> 11, of which waited for: 2 -> 4; matrix products, arithmetic and copies ran while one was open for 0% -> 0% of each run, Pallas kernels for 48% -> 44%
where the time goes in v3:
time: 56.2 us; the launch traced here: 56 us
  Pallas kernels  26.7 us (48%)
  starting transfers between devices  17.5 us (31%)
  waiting for transfers between devices  7.7 us (14%)
  other arithmetic  3.03 us (5%)
  between operations  0.91 us (2%)
    pallas_call x8, Pallas kernels, call(): pl.pallas_call(kernel, out_shape=outs, in_specs=[SMEM] * len(smem) + [VME...  26.7 us
    ppermute x8, starting transfers between devices, flipped(): return lax.ppermute(x, axis, pairs)  13.4 us
    ppermute x8, waiting for transfers between devices, flipped(): return lax.ppermute(x, axis, pairs)  5.79 us
    ppermute x3, starting transfers between devices, rotated(): lax.ppermute(x, axis, [(i, (i + by) % length) for i in range(length)])  4.15 us
    ppermute x3, waiting for transfers between devices, rotated(): lax.ppermute(x, axis, [(i, (i + by) % length) for i in range(length)])  1.92 us
    convert_element_type x1, other arithmetic, body(): sample_b = sample.astype(jnp.bfloat16)  1.68 us
    broadcast_in_dim x1, other arithmetic, body(): return ((mean_sum / samples)[None], (scale_sum / samples + 1.0)[None])  1.35 us
  transfers between devices with their start and end apart: 11, of which 4 were waited for; matrix products, arithmetic and copies ran while one was open for 0% of the time, Pallas kernels for 44%

profile of v3, /device:TPU:17, one launch (start us, length us, event | category | flops | bytes accessed | tf_op | source)
XLA Modules:
  0.0 56.0 jit_solution(10962972829826826319)
XLA Ops:
  0.7 1.7 %fusion = (bf16[3,256,256]{2,1,0:T(8,128)(2,1)S(1)}, f32[3,256,256]{2,1,0:T(8,128)S(1)}) fusion(bf16[1,1,3,256,256]{4,3,2,1,0:T(8,128)(2,1)} %param.12, f32[1,3,256,256]{3,2,1,0:T(8,128)} %param.11, f32[1,3,256,256]{3,2,1,0:T(8,128)} %param.10), kind=kLoop, calls=%fused_computation.4 | loop fusion | flops 786432 | bytes 3145728 | tf_op jit(solution)/shard_map/convert_element_type | solution.py:361
  2.4 1.3 %collective-permute-start.1 = (bf16[3,256,256]{2,1,0:T(8,128)(2,1)S(1)}, bf16[3,256,256]{2,1,0:T(8,128)(2,1)S(1)}, u32[]{:S(2)}, u32[]{:S(2)}) collective-permute-start(bf16[3,256,256]{2,1,0:T(8,128)(2,1)S(1)} %get-tuple-element.19.image_ref), channel_id=1, source_target_pairs={{0,4},{8,12},{16,20},{24,28},{4,0},{12,8},{20,16},{28,24},{1,5},{9... | collective-permute-start | bytes 1179656 | tf_op jit(solution)/shard_map/ppermute | solution.py:170
  3.7 1.3 %collective-permute-start.2 = (bf16[3,256,256]{2,1,0:T(8,128)(2,1)S(1)}, bf16[3,256,256]{2,1,0:T(8,128)(2,1)S(1)}, u32[]{:S(2)}, u32[]{:S(2)}) collective-permute-start(bf16[3,256,256]{2,1,0:T(8,128)(2,1)S(1)} %get-tuple-element.19.image_ref), channel_id=1, source_target_pairs={{0,8},{4,12},{16,24},{20,28},{8,0},{12,4},{24,16},{28,20},{1,9},{5... | collective-permute-start | bytes 1179656 | tf_op jit(solution)/shard_map/ppermute | solution.py:170
  5.0 1.9 %collective-permute-start.3 = (bf16[3,256,256]{2,1,0:T(8,128)(2,1)S(1)}, bf16[3,256,256]{2,1,0:T(8,128)(2,1)S(1)}, u32[]{:S(2)}, u32[]{:S(2)}) collective-permute-start(bf16[3,256,256]{2,1,0:T(8,128)(2,1)S(1)} %get-tuple-element.19.image_ref), channel_id=1, source_target_pairs={{8,16},{12,20},{16,8},{20,12},{9,17},{13,21},{17,9},{21,13},{10,18... | collective-permute-start | bytes 1179656 | tf_op jit(solution)/shard_map/ppermute | solution.py:170
  6.9 3.3 %collective-permute-start = (bf16[3,256,256]{2,1,0:T(8,128)(2,1)S(1)}, bf16[3,256,256]{2,1,0:T(8,128)(2,1)S(1)}, u32[]{:S(2)}, u32[]{:S(2)}) collective-permute-start(bf16[3,256,256]{2,1,0:T(8,128)(2,1)S(1)} %get-tuple-element.19.image_ref), channel_id=1, source_target_pairs={{4,8},{12,16},{20,24},{8,4},{16,12},{24,20},{5,9},{13,17},{21,25},... | collective-permute-start | bytes 1179656 | tf_op jit(solution)/shard_map/ppermute | solution.py:170
  10.2 1.9 %collective-permute-start.8 = (bf16[3,256,256]{2,1,0:T(8,128)(2,1)S(1)}, bf16[3,256,256]{2,1,0:T(8,128)(2,1)S(1)}, u32[]{:S(2)}, u32[]{:S(2)}) collective-permute-start(bf16[3,256,256]{2,1,0:T(8,128)(2,1)S(1)} %bitcast.20), channel_id=1, source_target_pairs={{0,1},{1,0},{2,3},{3,2},{4,5},{5,4},{6,7},{7,6},{8,9},{9,8},{10,11... | collective-permute-start | bytes 1179656 | tf_op jit(solution)/shard_map/ppermute | solution.py:29
  12.1 2.4 %prepare.1 = (s32[16,128]{1,0:T(8,128)S(1)}, f32[16,128]{1,0:T(8,128)S(1)}, bf16[16,256,256]{2,1,0:T(8,128)(2,1)S(1)}, bf16[16,256,256]{2,1,0:T(8,128)(2,1)S(1)}) custom-call(s32[6,3,8,9]{3,2,1,0:T(8,128)S(1)} %bitcast.24, s32[8,6]{1,0:T(8,128)S(1)} %copy-done.6, bf16[6,3,8,6]{3,2,1,0:T(8,128)(2,1)S(1)} %bitcast.25, f32[16,25]{1,0:T(8,128)S(1)} %bitcast.26), custom_call_target="tpu_custom_call" | custom-call | flops 805306368 | bytes 1572864 | tf_op jit(solution)/shard_map/prepare/pallas_call | solution.py:381
  14.5 0.0 copy-start.8
  14.5 3.7 %forward_own.1.refs_3_ = f32[3,256,256]{2,1,0:T(8,128)S(1)} custom-call(s32[16,128]{1,0:T(8,128)S(1)} %get-tuple-element.12.slots_ref, f32[16,128]{1,0:T(8,128)S(1)} %get-tuple-element.13.weights_ref, bf16[16,256,256]{2,1,0:T(8,128)(2,1)S(1)} %get-tuple-element.15.basis_ref, bf16[3,256,256]{2,1,0:T(8,128)(2,1)S(1)} %get-tuple-element.19.image_ref), custom_call_target="tpu_custom_call" | custom-call | flops 805306368 | bytes 1572864 | tf_op jit(solution)/shard_map/forward_own/pallas_call | solution.py:381
  18.1 0.1 exponential_bitcast_fusion.refs_0_
  18.3 0.0 copy-start.1
  18.3 0.0 copy-start.2
  18.3 0.0 collective-permute-done.3.refs_2_
  18.3 5.4 %forward_next.1.refs_1_ = f32[3,256,256]{2,1,0:T(8,128)S(1)} custom-call(s32[16,128]{1,0:T(8,128)S(1)} %get-tuple-element.12.slots_ref, f32[16,128]{1,0:T(8,128)S(1)} %get-tuple-element.13.weights_ref, bf16[16,256,256]{2,1,0:T(8,128)(2,1)S(1)} %get-tuple-element.15.basis_ref, ...), custom_call_target="tpu_custom_call", output_to_operand_aliasing={{}: (6, {})} | custom-call | flops 805306368 | bytes 1572864 | tf_op jit(solution)/shard_map/forward_next/pallas_call | solution.py:381
  23.8 0.8 %collective-permute-done.refs_0_ = bf16[3,256,256]{2,1,0:T(8,128)(2,1)S(1)} collective-permute-done((bf16[3,256,256]{2,1,0:T(8,128)(2,1)S(1)}, bf16[3,256,256]{2,1,0:T(8,128)(2,1)S(1)}, u32[]{:S(2)}, u32[]{:S(2)}) %collective-permute-start) | collective-permute-done | bytes 393248 | tf_op jit(solution)/shard_map/ppermute | solution.py:170
  24.6 2.9 %forward_last.1 = (f32[3,256,256]{2,1,0:T(8,128)S(1)}, bf16[3,256,256]{2,1,0:T(8,128)(2,1)S(1)}) custom-call(s32[16,128]{1,0:T(8,128)S(1)} %get-tuple-element.12.slots_ref, f32[16,128]{1,0:T(8,128)S(1)} %get-tuple-element.13.weights_ref, bf16[16,256,256]{2,1,0:T(8,128)(2,1)S(1)} %get-tuple-element.15.basis_ref, ...), custom_call_target="tpu_custom_call", output_to_operand_aliasing={{0}: (4, {})} | custom-call | flops 805306368 | bytes 1572864 | tf_op jit(solution)/shard_map/forward_last/pallas_call | solution.py:381
  27.5 0.1 collective-permute-start.5
  27.6 0.1 collective-permute-start.6
  27.7 2.5 %collective-permute-start.7 = (bf16[3,256,256]{2,1,0:T(8,128)(2,1)S(1)}, bf16[3,256,256]{2,1,0:T(8,128)(2,1)S(1)}, u32[]{:S(2)}, u32[]{:S(2)}) collective-permute-start(bf16[3,256,256]{2,1,0:T(8,128)(2,1)S(1)} %get-tuple-element.16.image_ref), channel_id=1, source_target_pairs={{8,16},{12,20},{16,8},{20,12},{9,17},{13,21},{17,9},{21,13},{10,18... | collective-permute-start | bytes 1179656 | tf_op jit(solution)/shard_map/ppermute | solution.py:170
  30.2 4.2 %backward_own.1 = (f32[3,256,256]{2,1,0:T(8,128)S(1)}, f32[3,256,256]{2,1,0:T(8,128)S(1)}, f32[3,256,256]{2,1,0:T(8,128)S(1)}) custom-call(s32[16,128]{1,0:T(8,128)S(1)} %get-tuple-element.12.slots_ref, f32[16,128]{1,0:T(8,128)S(1)} %get-tuple-element.13.weights_ref, bf16[16,256,256]{2,1,0:T(8,128)(2,1)S(1)} %get-tuple-element.14.basis_ref, ...), custom_call_target="tpu_custom_call" | custom-call | flops 805306368 | bytes 1572864 | tf_op jit(solution)/shard_map/backward_own/pallas_call | solution.py:381
  34.4 0.0 copy-start.7
  34.4 0.1 collective-permute-start.9
  34.5 2.9 %collective-permute-start.4 = (bf16[3,256,256]{2,1,0:T(8,128)(2,1)S(1)}, bf16[3,256,256]{2,1,0:T(8,128)(2,1)S(1)}, u32[]{:S(2)}, u32[]{:S(2)}) collective-permute-start(bf16[3,256,256]{2,1,0:T(8,128)(2,1)S(1)} %get-tuple-element.16.image_ref), channel_id=1, source_target_pairs={{4,8},{12,16},{20,24},{8,4},{16,12},{24,20},{5,9},{13,17},{21,25},... | collective-permute-start | bytes 1179656 | tf_op jit(solution)/shard_map/ppermute | solution.py:170
  37.3 0.0 collective-permute-done.5.refs_0_
  37.4 0.6 %collective-permute-done.7.refs_2_ = bf16[3,256,256]{2,1,0:T(8,128)(2,1)S(1)} collective-permute-done((bf16[3,256,256]{2,1,0:T(8,128)(2,1)S(1)}, bf16[3,256,256]{2,1,0:T(8,128)(2,1)S(1)}, u32[]{:S(2)}, u32[]{:S(2)}) %collective-permute-start.7) | collective-permute-done | bytes 393248 | tf_op jit(solution)/shard_map/ppermute | solution.py:170
  38.0 5.1 %backward_next.1.before_ref = f32[3,256,256]{2,1,0:T(8,128)S(1)} custom-call(s32[16,128]{1,0:T(8,128)S(1)} %get-tuple-element.12.slots_ref, f32[16,128]{1,0:T(8,128)S(1)} %get-tuple-element.13.weights_ref, bf16[16,256,256]{2,1,0:T(8,128)(2,1)S(1)} %get-tuple-element.14.basis_ref, ...), custom_call_target="tpu_custom_call", output_to_operand_aliasing={{}: (6, {})} | custom-call | flops 805306368 | bytes 1572864 | tf_op jit(solution)/shard_map/backward_next/pallas_call | solution.py:381
  43.1 1.0 %backward_prior.1.refs_1_ = f32[3,256,256]{2,1,0:T(8,128)S(1)} custom-call(f32[6,6]{1,0:T(8,128)S(1)} %copy-done.7, f32[3,256,256]{2,1,0:T(8,128)S(1)} %backward_next.1.before_ref, f32[3,256,256]{2,1,0:T(8,128)S(1)} %get-tuple-element.23.sample_ref, bf16[3,256,256]{2,1,0:T(8,128)(2,1)S(1)} %collective-permute-done.9.refs_0_), custom_call_target="tpu_custom_call", output_to_operand_aliasing={{}: (1, {})} | custom-call | flops 805306368 | bytes 1572864 | tf_op jit(solution)/shard_map/backward_prior/pallas_call | solution.py:381
  44.1 4.3 %collective-permute-done.4.refs_0_ = bf16[3,256,256]{2,1,0:T(8,128)(2,1)S(1)} collective-permute-done((bf16[3,256,256]{2,1,0:T(8,128)(2,1)S(1)}, bf16[3,256,256]{2,1,0:T(8,128)(2,1)S(1)}, u32[]{:S(2)}, u32[]{:S(2)}) %collective-permute-start.4) | collective-permute-done | bytes 393248 | tf_op jit(solution)/shard_map/ppermute | solution.py:170
  48.5 2.1 %backward_last.1 = f32[3,256,256]{2,1,0:T(8,128)S(1)} custom-call(s32[16,128]{1,0:T(8,128)S(1)} %get-tuple-element.12.slots_ref, f32[16,128]{1,0:T(8,128)S(1)} %get-tuple-element.13.weights_ref, bf16[16,256,256]{2,1,0:T(8,128)(2,1)S(1)} %get-tuple-element.14.basis_ref, ...), custom_call_target="tpu_custom_call", output_to_operand_aliasing={{}: (4, {})} | custom-call | flops 805306368 | bytes 1572864 | tf_op jit(solution)/shard_map/backward_last/pallas_call | solution.py:381
  50.5 2.2 %collective-permute-start.10 = (f32[3,256,256]{2,1,0:T(8,128)S(1)}, f32[3,256,256]{2,1,0:T(8,128)S(1)}, u32[]{:S(2)}, u32[]{:S(2)}) collective-permute-start(f32[3,256,256]{2,1,0:T(8,128)S(1)} %backward_last.1), channel_id=1, source_target_pairs={{0,1},{1,0},{2,3},{3,2},{4,5},{5,4},{6,7},{7,6},{8,9},{9,8},{10,11... | collective-permute-start | bytes 2359304 | tf_op jit(solution)/shard_map/ppermute | solution.py:29
  52.7 1.9 %collective-permute-done.10 = f32[3,256,256]{2,1,0:T(8,128)S(1)} collective-permute-done((f32[3,256,256]{2,1,0:T(8,128)S(1)}, f32[3,256,256]{2,1,0:T(8,128)S(1)}, u32[]{:S(2)}, u32[]{:S(2)}) %collective-permute-start.10) | collective-permute-done | bytes 786464 | tf_op jit(solution)/shard_map/ppermute | solution.py:29
  54.6 1.3 %add_bitcast_fusion = (f32[1,3,256,256]{3,2,1,0:T(8,128)}, f32[1,3,256,256]{3,2,1,0:T(8,128)}) fusion(f32[3,256,256]{2,1,0:T(8,128)S(1)} %collective-permute-done.10, f32[3,256,256]{2,1,0:T(8,128)S(1)} %get-tuple-element.21, f32[3,256,256]{2,1,0:T(8,128)S(1)} %backward_last.1, f32[3,256,256]{2,1,0:T(8,128)S(1)} %get-tuple-element.20), kind=kLoop, calls=%fused_computation.1 | loop fusion | flops 1376256 | bytes 4718592 | tf_op jit(solution)/shard_map/broadcast_in_dim | solution.py:480
  (19 shorter events, 0.0 us)
Async XLA Ops:
  0.6 9.6 %copy-start = (bf16[1,1,3,256,256]{4,3,2,1,0:T(8,128)(2,1)S(1)}, bf16[1,1,3,256,256]{4,3,2,1,0:T(8,128)(2,1)}, u32[]{:S(2)}) copy-start(bf16[1,1,3,256,256]{4,3,2,1,0:T(8,128)(2,1)} %param.12) | copy-start | bytes 1179652
  0.6 11.4 %copy-start.3 = (s32[8,6,3,9]{3,0,2,1:T(8,128)S(1)}, s32[8,6,3,9]{3,0,2,1:T(8,128)}, u32[]{:S(2)}) copy-start(s32[8,6,3,9]{3,0,2,1:T(8,128)} %param.15) | copy-start | bytes 15556
  0.7 11.4 %copy-start.4 = (bf16[8,6,6,3]{2,0,3,1:T(8,128)(2,1)S(1)}, bf16[8,6,6,3]{2,0,3,1:T(8,128)(2,1)}, u32[]{:S(2)}) copy-start(bf16[8,6,6,3]{2,0,3,1:T(8,128)(2,1)} %param.18) | copy-start | bytes 5188
  0.7 11.4 %copy-start.5 = (f32[8,2,25]{2,1,0:T(2,128)S(1)}, f32[8,2,25]{2,1,0:T(2,128)}, u32[]{:S(2)}) copy-start(f32[8,2,25]{2,1,0:T(2,128)} %param.17) | copy-start | bytes 4804
  0.7 11.4 %copy-start.6 = (s32[8,6]{1,0:T(8,128)S(1)}, s32[8,6]{1,0:T(8,128)}, u32[]{:S(2)}) copy-start(s32[8,6]{1,0:T(8,128)} %counts_ref.1) | copy-start | bytes 580
  2.4 15.9 %collective-permute-start.1 = (bf16[3,256,256]{2,1,0:T(8,128)(2,1)S(1)}, bf16[3,256,256]{2,1,0:T(8,128)(2,1)S(1)}, u32[]{:S(2)}, u32[]{:S(2)}) collective-permute-start(bf16[3,256,256]{2,1,0:T(8,128)(2,1)S(1)} %get-tuple-element.19.image_ref), channel_id=1, source_target_pairs={{0,4},{8,12},{16,20},{24,28},{4,0},{12,8},{20,16},{28,24},{1,5},{9... | collective-permute-start | bytes 1179656 | tf_op jit(solution)/shard_map/ppermute | solution.py:170
  3.7 14.6 %collective-permute-start.2 = (bf16[3,256,256]{2,1,0:T(8,128)(2,1)S(1)}, bf16[3,256,256]{2,1,0:T(8,128)(2,1)S(1)}, u32[]{:S(2)}, u32[]{:S(2)}) collective-permute-start(bf16[3,256,256]{2,1,0:T(8,128)(2,1)S(1)} %get-tuple-element.19.image_ref), channel_id=1, source_target_pairs={{0,8},{4,12},{16,24},{20,28},{8,0},{12,4},{24,16},{28,20},{1,9},{5... | collective-permute-start | bytes 1179656 | tf_op jit(solution)/shard_map/ppermute | solution.py:170
  5.0 13.3 %collective-permute-start.3 = (bf16[3,256,256]{2,1,0:T(8,128)(2,1)S(1)}, bf16[3,256,256]{2,1,0:T(8,128)(2,1)S(1)}, u32[]{:S(2)}, u32[]{:S(2)}) collective-permute-start(bf16[3,256,256]{2,1,0:T(8,128)(2,1)S(1)} %get-tuple-element.19.image_ref), channel_id=1, source_target_pairs={{8,16},{12,20},{16,8},{20,12},{9,17},{13,21},{17,9},{21,13},{10,18... | collective-permute-start | bytes 1179656 | tf_op jit(solution)/shard_map/ppermute | solution.py:170
  6.9 17.7 %collective-permute-start = (bf16[3,256,256]{2,1,0:T(8,128)(2,1)S(1)}, bf16[3,256,256]{2,1,0:T(8,128)(2,1)S(1)}, u32[]{:S(2)}, u32[]{:S(2)}) collective-permute-start(bf16[3,256,256]{2,1,0:T(8,128)(2,1)S(1)} %get-tuple-element.19.image_ref), channel_id=1, source_target_pairs={{4,8},{12,16},{20,24},{8,4},{16,12},{24,20},{5,9},{13,17},{21,25},... | collective-permute-start | bytes 1179656 | tf_op jit(solution)/shard_map/ppermute | solution.py:170
  10.2 20.0 %collective-permute-start.8 = (bf16[3,256,256]{2,1,0:T(8,128)(2,1)S(1)}, bf16[3,256,256]{2,1,0:T(8,128)(2,1)S(1)}, u32[]{:S(2)}, u32[]{:S(2)}) collective-permute-start(bf16[3,256,256]{2,1,0:T(8,128)(2,1)S(1)} %bitcast.20), channel_id=1, source_target_pairs={{0,1},{1,0},{2,3},{3,2},{4,5},{5,4},{6,7},{7,6},{8,9},{9,8},{10,11... | collective-permute-start | bytes 1179656 | tf_op jit(solution)/shard_map/ppermute | solution.py:29
  14.5 3.7 %copy-start.8 = (f32[1,3,256,256]{3,2,1,0:T(8,128)S(1)}, f32[1,3,256,256]{3,2,1,0:T(8,128)}, u32[]{:S(2)}) copy-start(f32[1,3,256,256]{3,2,1,0:T(8,128)} %param.11) | copy-start | bytes 2359300
  18.3 6.3 %copy-start.1 = (bf16[1,3,256,256]{3,2,1,0:T(8,128)(2,1)S(1)}, bf16[1,3,256,256]{3,2,1,0:T(8,128)(2,1)}, u32[]{:S(2)}) copy-start(bf16[1,3,256,256]{3,2,1,0:T(8,128)(2,1)} %param.13) | copy-start | bytes 1179652
  18.3 6.3 %copy-start.2 = (bf16[1,3,256,256]{3,2,1,0:T(8,128)(2,1)S(1)}, bf16[1,3,256,256]{3,2,1,0:T(8,128)(2,1)}, u32[]{:S(2)}) copy-start(bf16[1,3,256,256]{3,2,1,0:T(8,128)(2,1)} %param.14) | copy-start | bytes 1179652
  27.5 9.8 %collective-permute-start.5 = (bf16[3,256,256]{2,1,0:T(8,128)(2,1)S(1)}, bf16[3,256,256]{2,1,0:T(8,128)(2,1)S(1)}, u32[]{:S(2)}, u32[]{:S(2)}) collective-permute-start(bf16[3,256,256]{2,1,0:T(8,128)(2,1)S(1)} %get-tuple-element.16.image_ref), channel_id=1, source_target_pairs={{0,4},{8,12},{16,20},{24,28},{4,0},{12,8},{20,16},{28,24},{1,5},{9... | collective-permute-start | bytes 1179656 | tf_op jit(solution)/shard_map/ppermute | solution.py:170
  27.6 9.8 %collective-permute-start.6 = (bf16[3,256,256]{2,1,0:T(8,128)(2,1)S(1)}, bf16[3,256,256]{2,1,0:T(8,128)(2,1)S(1)}, u32[]{:S(2)}, u32[]{:S(2)}) collective-permute-start(bf16[3,256,256]{2,1,0:T(8,128)(2,1)S(1)} %get-tuple-element.16.image_ref), channel_id=1, source_target_pairs={{0,8},{4,12},{16,24},{20,28},{8,0},{12,4},{24,16},{28,20},{1,9},{5... | collective-permute-start | bytes 1179656 | tf_op jit(solution)/shard_map/ppermute | solution.py:170
  27.7 10.3 %collective-permute-start.7 = (bf16[3,256,256]{2,1,0:T(8,128)(2,1)S(1)}, bf16[3,256,256]{2,1,0:T(8,128)(2,1)S(1)}, u32[]{:S(2)}, u32[]{:S(2)}) collective-permute-start(bf16[3,256,256]{2,1,0:T(8,128)(2,1)S(1)} %get-tuple-element.16.image_ref), channel_id=1, source_target_pairs={{8,16},{12,20},{16,8},{20,12},{9,17},{13,21},{17,9},{21,13},{10,18... | collective-permute-start | bytes 1179656 | tf_op jit(solution)/shard_map/ppermute | solution.py:170
  34.4 8.7 %copy-start.7 = (f32[6,6]{1,0:T(8,128)S(1)}, f32[6,6]{1,0:T(8,128)}, u32[]{:S(2)}) copy-start(f32[6,6]{1,0:T(8,128)} %prec_ref.1) | copy-start | bytes 436
  34.4 8.7 %collective-permute-start.9 = (bf16[3,256,256]{2,1,0:T(8,128)(2,1)S(1)}, bf16[3,256,256]{2,1,0:T(8,128)(2,1)S(1)}, u32[]{:S(2)}, u32[]{:S(2)}) collective-permute-start(bf16[3,256,256]{2,1,0:T(8,128)(2,1)S(1)} %get-tuple-element.19.image_ref), channel_id=1, source_target_pairs={{0,2},{2,0},{1,3},{3,1},{4,6},{6,4},{5,7},{7,5},{8,10},{10,8},{9,1... | collective-permute-start | bytes 1179656 | tf_op jit(solution)/shard_map/ppermute | solution.py:29
  34.5 14.0 %collective-permute-start.4 = (bf16[3,256,256]{2,1,0:T(8,128)(2,1)S(1)}, bf16[3,256,256]{2,1,0:T(8,128)(2,1)S(1)}, u32[]{:S(2)}, u32[]{:S(2)}) collective-permute-start(bf16[3,256,256]{2,1,0:T(8,128)(2,1)S(1)} %get-tuple-element.16.image_ref), channel_id=1, source_target_pairs={{4,8},{12,16},{20,24},{8,4},{16,12},{24,20},{5,9},{13,17},{21,25},... | collective-permute-start | bytes 1179656 | tf_op jit(solution)/shard_map/ppermute | solution.py:170
  50.5 4.1 %collective-permute-start.10 = (f32[3,256,256]{2,1,0:T(8,128)S(1)}, f32[3,256,256]{2,1,0:T(8,128)S(1)}, u32[]{:S(2)}, u32[]{:S(2)}) collective-permute-start(f32[3,256,256]{2,1,0:T(8,128)S(1)} %backward_last.1), channel_id=1, source_target_pairs={{0,1},{1,0},{2,3},{3,2},{4,5},{5,4},{6,7},{7,6},{8,9},{9,8},{10,11... | collective-permute-start | bytes 2359304 | tf_op jit(solution)/shard_map/ppermute | solution.py:29

commit v4 on v3

--- a/solution.py
+++ b/solution.py
@@ -170,17 +170,31 @@
     return lax.ppermute(x, axis, pairs)
 
 
+def relay_onward(near, count):
+    length = lax.axis_size("tile")
+    pairs = [(i, i + 2) for i in range(0, length - 2, 2)]
+    pairs += [(i, i - 2) for i in range(3, length, 2)]
+    return lax.ppermute(near[1, 0][:count], "tile", pairs)
+
+
+def relay_across(near, count):
+    own = lax.axis_index("tile")
+    first = lax.rem(own, 2) == lax.rem(own // 2, 2)
+    image = jnp.where(first, near[2, 0][count:], near[2, 1][count:])
+    return flipped(image, "tile", (1, 0))
+
+
 def gather_live(sizes, moves, backward, slots_ref, images, list_ref, held_ref):
     tiles, filters, local = sizes
     own = lax.axis_index("tile")
     live = jnp.int32(0)
-    for move, image_ref in zip(moves, images):
+    for (move, f_first), image_ref in zip(moves, images):
         far = own if move is None else source_of(own, move)
         inside = jnp.where((far >= 0) & (far < tiles), 1, 0)
         here, there = REACH * local, jnp.clip(far - own + REACH, 0, 2 * REACH) * local
         tile_at, expo_at = (here, there) if backward else (there, here)
         expo = far if backward else own
-        for f in range(local):
+        for f in range(f_first, f_first + image_ref.shape[0]):
             found, base = find_slot(slots_ref, tile_at + f, expo)
             found = found * inside
 
@@ -190,7 +204,7 @@
                 list_ref[1, live] = tile_at + f
                 list_ref[2, live] = base
                 list_ref[3, live] = expo_at + f
-                held_ref[live] = image_ref[f]
+                held_ref[live] = image_ref[f - f_first]
 
             live = live + found
     return live
@@ -271,7 +285,7 @@
 def forward_own(sizes, slots_ref, weights_ref, basis_ref, image_ref, *refs):
     pred_ref, *scratch = refs
     pred_ref[...] = jnp.zeros_like(pred_ref)
-    forward_slots(sizes, [None], slots_ref, weights_ref, basis_ref, [image_ref], pred_ref, scratch)
+    forward_slots(sizes, [(None, 0)], slots_ref, weights_ref, basis_ref, [image_ref], pred_ref, scratch)
 
 
 def forward_next(sizes, moves, slots_ref, weights_ref, basis_ref, *refs):
@@ -315,7 +329,7 @@
         turn_ref[...] = scale_ref[...] * noise_ref[...].astype(jnp.float32)
     grad_ref[...] = jnp.zeros_like(grad_ref)
     backward_slots(
-        sizes, [None], slots_ref, weights_ref, basis_ref, [image_ref], grad_ref, scratch
+        sizes, [(None, 0)], slots_ref, weights_ref, basis_ref, [image_ref], grad_ref, scratch
     )
 
 
@@ -348,9 +362,15 @@
     tiles, filters = counts.shape
     sizes = (tiles, filters, local)
     kinds = kernels.shape[0]
-    started = [(d, parity) for d in range(1, REACH + 1) for parity in (0, 1)]
-    last = (1, 1)
-    early = [move for move in started if move != last]
+    early = [(1, 0), (2, 0), (2, 1)]
+    early_moves = [(move, 0) for move in early]
+    onward = local - local // 3
+    last_moves = [((1, 1), 0)] + ([((1, 1), onward)] if onward < local else [])
+
+    def last_images(near):
+        across = [relay_across(near, onward)] if onward < local else []
+        return [relay_onward(near, onward), *across]
+
     samples = lax.axis_size("mc")
     parts = lax.axis_size("filt")
 
@@ -390,7 +410,7 @@
             name=name,
         )(*smem, *vmem)
 
-    near = {move: flipped(sample_b, "tile", move) for move in started}
+    near = {move: flipped(sample_b, "tile", move) for move in early}
     other_noise = [rotated(noise, "mc", r) for r in range(1, samples)]
     rows = -(-(2 * REACH + 1) * local // 8) * 8
     slots, weights, forth, back = call(
@@ -415,8 +435,10 @@
         (forth, sample_b),
         slot_scratch(1, jnp.bfloat16),
     )
+    near[1, 0], pred = lax.optimization_barrier((near[1, 0], pred))
+    near_last = last_images(near)
     (pred,) = call(
-        functools.partial(forward_next, sizes, early),
+        functools.partial(forward_next, sizes, early_moves),
         "forward_next",
         [image_f32],
         tables,
@@ -425,15 +447,15 @@
         {len(tables) + 1 + len(early): 0},
     )
     _, residual = call(
-        functools.partial(forward_last, sizes, [last]),
+        functools.partial(forward_last, sizes, last_moves),
         "forward_last",
         [image_f32, image_b16],
         tables,
-        (forth, near[last], pred, observed[0], inv_var[0]),
+        (forth, *near_last, pred, observed[0], inv_var[0]),
         slot_scratch(1, jnp.bfloat16),
-        {len(tables) + 2: 0},
-    )
-    near_resid = {move: flipped(residual, "tile", move) for move in started}
+        {len(tables) + 1 + len(near_last): 0},
+    )
+    near_resid = {move: flipped(residual, "tile", move) for move in early}
     grad, turn, *other_turns = call(
         functools.partial(backward_own, sizes, samples),
         "backward_own",
@@ -442,10 +464,11 @@
         (back, residual, scale_map, noise, *other_noise),
         slot_scratch(1, jnp.float32),
     )
-    late_b, grad = lax.optimization_barrier((sample_b, grad))
+    late_b, near_resid[1, 0], grad = lax.optimization_barrier((sample_b, near_resid[1, 0], grad))
+    near_resid_last = last_images(near_resid)
     other_samples = [rotated(late_b, "filt", r) for r in range(1, parts)]
     (grad,) = call(
-        functools.partial(backward_next, sizes, early),
+        functools.partial(backward_next, sizes, early_moves),
         "backward_next",
         [image_f32],
         tables,
@@ -463,13 +486,13 @@
         {1: 0},
     )
     (grad,) = call(
-        functools.partial(backward_next, sizes, [last]),
+        functools.partial(backward_next, sizes, last_moves),
         "backward_last",
         [image_f32],
         tables,
-        (back, near_resid[last], grad),
+        (back, *near_resid_last, grad),
         slot_scratch(1, jnp.float32),
-        {len(tables) + 2: 0},
+        {len(tables) + 1 + len(near_resid_last): 0},
     )
     mean_sum = grad
     scale_sum = grad * turn

time: 56.2 us -> 58.5 us (1.041)
  the two profiles are of different devices: /device:TPU:17 before, /device:TPU:19 now
where the time goes in v4:
time: 58.5 us
  Pallas kernels  20.7 us (35%)
  starting transfers between devices  17.9 us (31%)
  waiting for transfers between devices  15.7 us (27%)
  other arithmetic  3.06 us (5%)
  between operations  0.96 us (2%)
    pallas_call x8, Pallas kernels, call(): pl.pallas_call(kernel, out_shape=outs, in_specs=[SMEM] * len(smem) + [VME...  20.7 us
    ppermute x8, waiting for transfers between devices, flipped(): return lax.ppermute(x, axis, pairs)  10.3 us
    ppermute x8, starting transfers between devices, flipped(): return lax.ppermute(x, axis, pairs)  8.07 us
    ppermute x3, waiting for transfers between devices, rotated(): lax.ppermute(x, axis, [(i, (i + by) % length) for i in range(length)])  5.4 us
    ppermute x2, starting transfers between devices, relay_onward(): return lax.ppermute(near[1, 0][:count], 'tile', pairs)  5.13 us
    ppermute x3, starting transfers between devices, rotated(): lax.ppermute(x, axis, [(i, (i + by) % length) for i in range(length)])  4.67 us
    convert_element_type x1, other arithmetic, body(): sample_b = sample.astype(jnp.bfloat16)  1.68 us
    broadcast_in_dim x1, other arithmetic, body(): return ((mean_sum / samples)[None], (scale_sum / samples + 1.0)[None])  1.35 us
  transfers between devices with their start and end apart: 13, of which 5 were waited for; matrix products, arithmetic and copies ran while one was open for 0% of the time, Pallas kernels for 29%

profile of v4, /device:TPU:19, one launch (start us, length us, event | category | flops | bytes accessed | tf_op | source)
XLA Modules:
  0.0 58.5 jit_solution(8396949130347885837)
XLA Ops:
  0.7 1.7 %fusion = (bf16[3,256,256]{2,1,0:T(8,128)(2,1)S(1)}, f32[3,256,256]{2,1,0:T(8,128)S(1)}) fusion(bf16[1,1,3,256,256]{4,3,2,1,0:T(8,128)(2,1)} %param.12, f32[1,3,256,256]{3,2,1,0:T(8,128)} %param.11, f32[1,3,256,256]{3,2,1,0:T(8,128)} %param.10), kind=kLoop, calls=%fused_computation.6 | loop fusion | flops 786432 | bytes 3145728 | tf_op jit(solution)/shard_map/convert_element_type | solution.py:381
  2.4 1.3 %collective-permute-start = (bf16[3,256,256]{2,1,0:T(8,128)(2,1)S(1)}, bf16[3,256,256]{2,1,0:T(8,128)(2,1)S(1)}, u32[]{:S(2)}, u32[]{:S(2)}) collective-permute-start(bf16[3,256,256]{2,1,0:T(8,128)(2,1)S(1)} %get-tuple-element.25.image_ref), channel_id=1, source_target_pairs={{0,4},{8,12},{16,20},{24,28},{4,0},{12,8},{20,16},{28,24},{1,5},{9... | collective-permute-start | bytes 1179656 | tf_op jit(solution)/shard_map/ppermute | solution.py:170
  3.7 1.3 %collective-permute-start.2 = (bf16[3,256,256]{2,1,0:T(8,128)(2,1)S(1)}, bf16[3,256,256]{2,1,0:T(8,128)(2,1)S(1)}, u32[]{:S(2)}, u32[]{:S(2)}) collective-permute-start(bf16[3,256,256]{2,1,0:T(8,128)(2,1)S(1)} %get-tuple-element.25.image_ref), channel_id=1, source_target_pairs={{0,8},{4,12},{16,24},{20,28},{8,0},{12,4},{24,16},{28,20},{1,9},{5... | collective-permute-start | bytes 1179656 | tf_op jit(solution)/shard_map/ppermute | solution.py:170
  5.0 1.9 %collective-permute-start.3 = (bf16[3,256,256]{2,1,0:T(8,128)(2,1)S(1)}, bf16[3,256,256]{2,1,0:T(8,128)(2,1)S(1)}, u32[]{:S(2)}, u32[]{:S(2)}) collective-permute-start(bf16[3,256,256]{2,1,0:T(8,128)(2,1)S(1)} %get-tuple-element.25.image_ref), channel_id=1, source_target_pairs={{8,16},{12,20},{16,8},{20,12},{9,17},{13,21},{17,9},{21,13},{10,18... | collective-permute-start | bytes 1179656 | tf_op jit(solution)/shard_map/ppermute | solution.py:170
  6.9 2.4 %prepare.1 = (s32[16,128]{1,0:T(8,128)S(1)}, f32[16,128]{1,0:T(8,128)S(1)}, bf16[16,256,256]{2,1,0:T(8,128)(2,1)S(1)}, bf16[16,256,256]{2,1,0:T(8,128)(2,1)S(1)}) custom-call(s32[6,3,8,9]{3,2,1,0:T(8,128)S(1)} %bitcast.24, s32[8,6]{1,0:T(8,128)S(1)} %copy-done.6, bf16[6,3,8,6]{3,2,1,0:T(8,128)(2,1)S(1)} %bitcast.25, f32[16,25]{1,0:T(8,128)S(1)} %bitcast.26), custom_call_target="tpu_custom_call" | custom-call | flops 805306368 | bytes 1572864 | tf_op jit(solution)/shard_map/prepare/pallas_call | solution.py:401
  9.3 0.0 copy-start
  9.3 0.9 %forward_own.1.refs_3_ = f32[3,256,256]{2,1,0:T(8,128)S(1)} custom-call(s32[16,128]{1,0:T(8,128)S(1)} %get-tuple-element.15.slots_ref, f32[16,128]{1,0:T(8,128)S(1)} %get-tuple-element.16.weights_ref, bf16[16,256,256]{2,1,0:T(8,128)(2,1)S(1)} %get-tuple-element.18.basis_ref, bf16[3,256,256]{2,1,0:T(8,128)(2,1)S(1)} %get-tuple-element.25.image_ref), custom_call_target="tpu_custom_call" | custom-call | flops 805306368 | bytes 1572864 | tf_op jit(solution)/shard_map/forward_own/pallas_call | solution.py:401
  10.2 2.2 %collective-permute-done.refs_0_ = bf16[3,256,256]{2,1,0:T(8,128)(2,1)S(1)} collective-permute-done((bf16[3,256,256]{2,1,0:T(8,128)(2,1)S(1)}, bf16[3,256,256]{2,1,0:T(8,128)(2,1)S(1)}, u32[]{:S(2)}, u32[]{:S(2)}) %collective-permute-start) | collective-permute-done | bytes 393248 | tf_op jit(solution)/shard_map/ppermute | solution.py:170
  12.4 3.2 %collective-permute-start.1 = (bf16[2,256,256]{2,1,0:T(8,128)(2,1)S(1)}, bf16[2,256,256]{2,1,0:T(8,128)(2,1)S(1)}, u32[]{:S(2)}, u32[]{:S(2)}) collective-permute-start(bf16[2,256,256]{2,1,0:T(8,128)(2,1)S(1)} %slice.18), channel_id=1, source_target_pairs={{0,8},{8,16},{16,24},{12,4},{20,12},{28,20},{1,9},{9,17},{17,25},{... | collective-permute-start | bytes 786440 | tf_op jit(solution)/shard_map/ppermute | solution.py:177
  15.6 0.6 collective-permute-done.3.refs_2_
  16.2 0.3 collective-permute-start.4
  16.5 2.9 %collective-permute-start.6 = (bf16[3,256,256]{2,1,0:T(8,128)(2,1)S(1)}, bf16[3,256,256]{2,1,0:T(8,128)(2,1)S(1)}, u32[]{:S(2)}, u32[]{:S(2)}) collective-permute-start(bf16[3,256,256]{2,1,0:T(8,128)(2,1)S(1)} %bitcast.20), channel_id=1, source_target_pairs={{0,1},{1,0},{2,3},{3,2},{4,5},{5,4},{6,7},{7,6},{8,9},{9,8},{10,11... | collective-permute-start | bytes 1179656 | tf_op jit(solution)/shard_map/ppermute | solution.py:29
  19.4 6.3 %forward_next.1.refs_2_ = f32[3,256,256]{2,1,0:T(8,128)S(1)} custom-call(s32[16,128]{1,0:T(8,128)S(1)} %get-tuple-element.15.slots_ref, f32[16,128]{1,0:T(8,128)S(1)} %get-tuple-element.16.weights_ref, bf16[16,256,256]{2,1,0:T(8,128)(2,1)S(1)} %get-tuple-element.18.basis_ref, ...), custom_call_target="tpu_custom_call", output_to_operand_aliasing={{}: (6, {})} | custom-call | flops 805306368 | bytes 1572864 | tf_op jit(solution)/shard_map/forward_next/pallas_call | solution.py:401
  25.7 0.0 copy-start.8
  25.8 2.1 %forward_last.1 = (f32[3,256,256]{2,1,0:T(8,128)S(1)}, bf16[3,256,256]{2,1,0:T(8,128)(2,1)S(1)}) custom-call(s32[16,128]{1,0:T(8,128)S(1)} %get-tuple-element.15.slots_ref, f32[16,128]{1,0:T(8,128)S(1)} %get-tuple-element.16.weights_ref, bf16[16,256,256]{2,1,0:T(8,128)(2,1)S(1)} %get-tuple-element.18.basis_ref, ...), custom_call_target="tpu_custom_call", output_to_operand_aliasing={{0}: (5, {})} | custom-call | flops 805306368 | bytes 1572864 | tf_op jit(solution)/shard_map/forward_last/pallas_call | solution.py:401
  27.9 0.1 collective-permute-start.5
  27.9 0.1 collective-permute-start.8
  28.0 1.9 %collective-permute-start.9 = (bf16[3,256,256]{2,1,0:T(8,128)(2,1)S(1)}, bf16[3,256,256]{2,1,0:T(8,128)(2,1)S(1)}, u32[]{:S(2)}, u32[]{:S(2)}) collective-permute-start(bf16[3,256,256]{2,1,0:T(8,128)(2,1)S(1)} %get-tuple-element.21.image_ref), channel_id=1, source_target_pairs={{8,16},{12,20},{16,8},{20,12},{9,17},{13,21},{17,9},{21,13},{10,18... | collective-permute-start | bytes 1179656 | tf_op jit(solution)/shard_map/ppermute | solution.py:170
  30.0 0.1 exponential_bitcast_fusion.refs_0_
  30.1 1.0 %backward_own.1 = (f32[3,256,256]{2,1,0:T(8,128)S(1)}, f32[3,256,256]{2,1,0:T(8,128)S(1)}, f32[3,256,256]{2,1,0:T(8,128)S(1)}) custom-call(s32[16,128]{1,0:T(8,128)S(1)} %get-tuple-element.15.slots_ref, f32[16,128]{1,0:T(8,128)S(1)} %get-tuple-element.16.weights_ref, bf16[16,256,256]{2,1,0:T(8,128)(2,1)S(1)} %get-tuple-element.17.basis_ref, ...), custom_call_target="tpu_custom_call" | custom-call | flops 805306368 | bytes 1572864 | tf_op jit(solution)/shard_map/backward_own/pallas_call | solution.py:401
  31.1 7.6 %collective-permute-done.5.refs_0_ = bf16[3,256,256]{2,1,0:T(8,128)(2,1)S(1)} collective-permute-done((bf16[3,256,256]{2,1,0:T(8,128)(2,1)S(1)}, bf16[3,256,256]{2,1,0:T(8,128)(2,1)S(1)}, u32[]{:S(2)}, u32[]{:S(2)}) %collective-permute-start.5) | collective-permute-done | bytes 393248 | tf_op jit(solution)/shard_map/ppermute | solution.py:170
  38.7 1.9 %collective-permute-start.7 = (bf16[2,256,256]{2,1,0:T(8,128)(2,1)S(1)}, bf16[2,256,256]{2,1,0:T(8,128)(2,1)S(1)}, u32[]{:S(2)}, u32[]{:S(2)}) collective-permute-start(bf16[2,256,256]{2,1,0:T(8,128)(2,1)S(1)} %slice.21), channel_id=1, source_target_pairs={{0,8},{8,16},{16,24},{12,4},{20,12},{28,20},{1,9},{9,17},{17,25},{... | collective-permute-start | bytes 786440 | tf_op jit(solution)/shard_map/ppermute | solution.py:177
  40.6 0.0 collective-permute-done.9.refs_2_
  40.7 0.0 copy-start.7
  40.7 1.2 %collective-permute-start.10 = (bf16[1,256,256]{2,1,0:T(8,128)(2,1)S(1)}, bf16[1,256,256]{2,1,0:T(8,128)(2,1)S(1)}, u32[]{:S(2)}, u32[]{:S(2)}) collective-permute-start(bf16[1,256,256]{2,1,0:T(8,128)(2,1)S(1)} %slice_select_fusion), channel_id=1, source_target_pairs={{0,4},{8,12},{16,20},{24,28},{4,0},{12,8},{20,16},{28,24},{1,5},{9... | collective-permute-start | bytes 393224 | tf_op jit(solution)/shard_map/ppermute | solution.py:170
  41.9 3.1 %backward_next.1.before_ref = f32[3,256,256]{2,1,0:T(8,128)S(1)} custom-call(s32[16,128]{1,0:T(8,128)S(1)} %get-tuple-element.15.slots_ref, f32[16,128]{1,0:T(8,128)S(1)} %get-tuple-element.16.weights_ref, bf16[16,256,256]{2,1,0:T(8,128)(2,1)S(1)} %get-tuple-element.17.basis_ref, ...), custom_call_target="tpu_custom_call", output_to_operand_aliasing={{}: (6, {})} | custom-call | flops 805306368 | bytes 1572864 | tf_op jit(solution)/shard_map/backward_next/pallas_call | solution.py:401
  45.0 3.5 %collective-permute-done.11.refs_0_ = bf16[3,256,256]{2,1,0:T(8,128)(2,1)S(1)} collective-permute-done((bf16[3,256,256]{2,1,0:T(8,128)(2,1)S(1)}, bf16[3,256,256]{2,1,0:T(8,128)(2,1)S(1)}, u32[]{:S(2)}, u32[]{:S(2)}) %collective-permute-start.11) | collective-permute-done | bytes 393248 | tf_op jit(solution)/shard_map/ppermute | solution.py:29
  48.5 1.0 %backward_prior.1.refs_2_ = f32[3,256,256]{2,1,0:T(8,128)S(1)} custom-call(f32[6,6]{1,0:T(8,128)S(1)} %copy-done.7, f32[3,256,256]{2,1,0:T(8,128)S(1)} %backward_next.1.before_ref, f32[3,256,256]{2,1,0:T(8,128)S(1)} %get-tuple-element.29.sample_ref, bf16[3,256,256]{2,1,0:T(8,128)(2,1)S(1)} %collective-permute-done.11.refs_0_), custom_call_target="tpu_custom_call", output_to_operand_aliasing={{}: (1, {})} | custom-call | flops 805306368 | bytes 1572864 | tf_op jit(solution)/shard_map/backward_prior/pallas_call | solution.py:401
  49.5 4.0 %backward_last.1 = f32[3,256,256]{2,1,0:T(8,128)S(1)} custom-call(s32[16,128]{1,0:T(8,128)S(1)} %get-tuple-element.15.slots_ref, f32[16,128]{1,0:T(8,128)S(1)} %get-tuple-element.16.weights_ref, bf16[16,256,256]{2,1,0:T(8,128)(2,1)S(1)} %get-tuple-element.17.basis_ref, ...), custom_call_target="tpu_custom_call", output_to_operand_aliasing={{}: (5, {})} | custom-call | flops 805306368 | bytes 1572864 | tf_op jit(solution)/shard_map/backward_last/pallas_call | solution.py:401
  53.5 1.7 %collective-permute-start.12 = (f32[3,256,256]{2,1,0:T(8,128)S(1)}, f32[3,256,256]{2,1,0:T(8,128)S(1)}, u32[]{:S(2)}, u32[]{:S(2)}) collective-permute-start(f32[3,256,256]{2,1,0:T(8,128)S(1)} %backward_last.1), channel_id=1, source_target_pairs={{0,1},{1,0},{2,3},{3,2},{4,5},{5,4},{6,7},{7,6},{8,9},{9,8},{10,11... | collective-permute-start | bytes 2359304 | tf_op jit(solution)/shard_map/ppermute | solution.py:29
  55.3 1.9 %collective-permute-done.12 = f32[3,256,256]{2,1,0:T(8,128)S(1)} collective-permute-done((f32[3,256,256]{2,1,0:T(8,128)S(1)}, f32[3,256,256]{2,1,0:T(8,128)S(1)}, u32[]{:S(2)}, u32[]{:S(2)}) %collective-permute-start.12) | collective-permute-done | bytes 786464 | tf_op jit(solution)/shard_map/ppermute | solution.py:29
  57.2 1.3 %add_bitcast_fusion = (f32[1,3,256,256]{3,2,1,0:T(8,128)}, f32[1,3,256,256]{3,2,1,0:T(8,128)}) fusion(f32[3,256,256]{2,1,0:T(8,128)S(1)} %collective-permute-done.12, f32[3,256,256]{2,1,0:T(8,128)S(1)} %get-tuple-element.27, f32[3,256,256]{2,1,0:T(8,128)S(1)} %backward_last.1, f32[3,256,256]{2,1,0:T(8,128)S(1)} %get-tuple-element.26), kind=kLoop, calls=%fused_computation.1 | loop fusion | flops 1376256 | bytes 4718592 | tf_op jit(solution)/shard_map/broadcast_in_dim | solution.py:503
  (27 shorter events, 0.1 us)
Async XLA Ops:
  0.6 6.3 %copy-start.3 = (s32[8,6,3,9]{3,0,2,1:T(8,128)S(1)}, s32[8,6,3,9]{3,0,2,1:T(8,128)}, u32[]{:S(2)}) copy-start(s32[8,6,3,9]{3,0,2,1:T(8,128)} %param.15) | copy-start | bytes 15556
  0.6 6.3 %copy-start.4 = (bf16[8,6,6,3]{2,0,3,1:T(8,128)(2,1)S(1)}, bf16[8,6,6,3]{2,0,3,1:T(8,128)(2,1)}, u32[]{:S(2)}) copy-start(bf16[8,6,6,3]{2,0,3,1:T(8,128)(2,1)} %param.18) | copy-start | bytes 5188
  0.7 6.3 %copy-start.5 = (f32[8,2,25]{2,1,0:T(2,128)S(1)}, f32[8,2,25]{2,1,0:T(2,128)}, u32[]{:S(2)}) copy-start(f32[8,2,25]{2,1,0:T(2,128)} %param.17) | copy-start | bytes 4804
  0.7 6.3 %copy-start.6 = (s32[8,6]{1,0:T(8,128)S(1)}, s32[8,6]{1,0:T(8,128)}, u32[]{:S(2)}) copy-start(s32[8,6]{1,0:T(8,128)} %counts_ref.1) | copy-start | bytes 580
  2.4 10.0 %collective-permute-start = (bf16[3,256,256]{2,1,0:T(8,128)(2,1)S(1)}, bf16[3,256,256]{2,1,0:T(8,128)(2,1)S(1)}, u32[]{:S(2)}, u32[]{:S(2)}) collective-permute-start(bf16[3,256,256]{2,1,0:T(8,128)(2,1)S(1)} %get-tuple-element.25.image_ref), channel_id=1, source_target_pairs={{0,4},{8,12},{16,20},{24,28},{4,0},{12,8},{20,16},{28,24},{1,5},{9... | collective-permute-start | bytes 1179656 | tf_op jit(solution)/shard_map/ppermute | solution.py:170
  3.7 12.0 %collective-permute-start.2 = (bf16[3,256,256]{2,1,0:T(8,128)(2,1)S(1)}, bf16[3,256,256]{2,1,0:T(8,128)(2,1)S(1)}, u32[]{:S(2)}, u32[]{:S(2)}) collective-permute-start(bf16[3,256,256]{2,1,0:T(8,128)(2,1)S(1)} %get-tuple-element.25.image_ref), channel_id=1, source_target_pairs={{0,8},{4,12},{16,24},{20,28},{8,0},{12,4},{24,16},{28,20},{1,9},{5... | collective-permute-start | bytes 1179656 | tf_op jit(solution)/shard_map/ppermute | solution.py:170
  5.0 11.3 %collective-permute-start.3 = (bf16[3,256,256]{2,1,0:T(8,128)(2,1)S(1)}, bf16[3,256,256]{2,1,0:T(8,128)(2,1)S(1)}, u32[]{:S(2)}, u32[]{:S(2)}) collective-permute-start(bf16[3,256,256]{2,1,0:T(8,128)(2,1)S(1)} %get-tuple-element.25.image_ref), channel_id=1, source_target_pairs={{8,16},{12,20},{16,8},{20,12},{9,17},{13,21},{17,9},{21,13},{10,18... | collective-permute-start | bytes 1179656 | tf_op jit(solution)/shard_map/ppermute | solution.py:170
  9.3 7.2 %copy-start = (bf16[1,1,3,256,256]{4,3,2,1,0:T(8,128)(2,1)S(1)}, bf16[1,1,3,256,256]{4,3,2,1,0:T(8,128)(2,1)}, u32[]{:S(2)}) copy-start(bf16[1,1,3,256,256]{4,3,2,1,0:T(8,128)(2,1)} %param.12) | copy-start | bytes 1179652
  12.4 13.3 %collective-permute-start.1 = (bf16[2,256,256]{2,1,0:T(8,128)(2,1)S(1)}, bf16[2,256,256]{2,1,0:T(8,128)(2,1)S(1)}, u32[]{:S(2)}, u32[]{:S(2)}) collective-permute-start(bf16[2,256,256]{2,1,0:T(8,128)(2,1)S(1)} %slice.18), channel_id=1, source_target_pairs={{0,8},{8,16},{16,24},{12,4},{20,12},{28,20},{1,9},{9,17},{17,25},{... | collective-permute-start | bytes 786440 | tf_op jit(solution)/shard_map/ppermute | solution.py:177
  16.2 9.5 %collective-permute-start.4 = (bf16[1,256,256]{2,1,0:T(8,128)(2,1)S(1)}, bf16[1,256,256]{2,1,0:T(8,128)(2,1)S(1)}, u32[]{:S(2)}, u32[]{:S(2)}) collective-permute-start(bf16[1,256,256]{2,1,0:T(8,128)(2,1)S(1)} %slice_select_fusion.1), channel_id=1, source_target_pairs={{0,4},{8,12},{16,20},{24,28},{4,0},{12,8},{20,16},{28,24},{1,5},{9... | collective-permute-start | bytes 393224 | tf_op jit(solution)/shard_map/ppermute | solution.py:170
  16.5 9.2 %copy-start.1 = (bf16[1,3,256,256]{3,2,1,0:T(8,128)(2,1)S(1)}, bf16[1,3,256,256]{3,2,1,0:T(8,128)(2,1)}, u32[]{:S(2)}) copy-start(bf16[1,3,256,256]{3,2,1,0:T(8,128)(2,1)} %param.13) | copy-start | bytes 1179652
  16.5 9.2 %copy-start.2 = (bf16[1,3,256,256]{3,2,1,0:T(8,128)(2,1)S(1)}, bf16[1,3,256,256]{3,2,1,0:T(8,128)(2,1)}, u32[]{:S(2)}) copy-start(bf16[1,3,256,256]{3,2,1,0:T(8,128)(2,1)} %param.14) | copy-start | bytes 1179652
  16.5 13.6 %collective-permute-start.6 = (bf16[3,256,256]{2,1,0:T(8,128)(2,1)S(1)}, bf16[3,256,256]{2,1,0:T(8,128)(2,1)S(1)}, u32[]{:S(2)}, u32[]{:S(2)}) collective-permute-start(bf16[3,256,256]{2,1,0:T(8,128)(2,1)S(1)} %bitcast.20), channel_id=1, source_target_pairs={{0,1},{1,0},{2,3},{3,2},{4,5},{5,4},{6,7},{7,6},{8,9},{9,8},{10,11... | collective-permute-start | bytes 1179656 | tf_op jit(solution)/shard_map/ppermute | solution.py:29
  25.7 4.2 %copy-start.8 = (f32[1,3,256,256]{3,2,1,0:T(8,128)S(1)}, f32[1,3,256,256]{3,2,1,0:T(8,128)}, u32[]{:S(2)}) copy-start(f32[1,3,256,256]{3,2,1,0:T(8,128)} %param.11) | copy-start | bytes 2359300
  27.9 10.8 %collective-permute-start.5 = (bf16[3,256,256]{2,1,0:T(8,128)(2,1)S(1)}, bf16[3,256,256]{2,1,0:T(8,128)(2,1)S(1)}, u32[]{:S(2)}, u32[]{:S(2)}) collective-permute-start(bf16[3,256,256]{2,1,0:T(8,128)(2,1)S(1)} %get-tuple-element.21.image_ref), channel_id=1, source_target_pairs={{0,4},{8,12},{16,20},{24,28},{4,0},{12,8},{20,16},{28,24},{1,5},{9... | collective-permute-start | bytes 1179656 | tf_op jit(solution)/shard_map/ppermute | solution.py:170
  27.9 12.7 %collective-permute-start.8 = (bf16[3,256,256]{2,1,0:T(8,128)(2,1)S(1)}, bf16[3,256,256]{2,1,0:T(8,128)(2,1)S(1)}, u32[]{:S(2)}, u32[]{:S(2)}) collective-permute-start(bf16[3,256,256]{2,1,0:T(8,128)(2,1)S(1)} %get-tuple-element.21.image_ref), channel_id=1, source_target_pairs={{0,8},{4,12},{16,24},{20,28},{8,0},{12,4},{24,16},{28,20},{1,9},{5... | collective-permute-start | bytes 1179656 | tf_op jit(solution)/shard_map/ppermute | solution.py:170
  28.0 12.6 %collective-permute-start.9 = (bf16[3,256,256]{2,1,0:T(8,128)(2,1)S(1)}, bf16[3,256,256]{2,1,0:T(8,128)(2,1)S(1)}, u32[]{:S(2)}, u32[]{:S(2)}) collective-permute-start(bf16[3,256,256]{2,1,0:T(8,128)(2,1)S(1)} %get-tuple-element.21.image_ref), channel_id=1, source_target_pairs={{8,16},{12,20},{16,8},{20,12},{9,17},{13,21},{17,9},{21,13},{10,18... | collective-permute-start | bytes 1179656 | tf_op jit(solution)/shard_map/ppermute | solution.py:170
  38.7 9.8 %collective-permute-start.11 = (bf16[3,256,256]{2,1,0:T(8,128)(2,1)S(1)}, bf16[3,256,256]{2,1,0:T(8,128)(2,1)S(1)}, u32[]{:S(2)}, u32[]{:S(2)}) collective-permute-start(bf16[3,256,256]{2,1,0:T(8,128)(2,1)S(1)} %get-tuple-element.25.image_ref), channel_id=1, source_target_pairs={{0,2},{2,0},{1,3},{3,1},{4,6},{6,4},{5,7},{7,5},{8,10},{10,8},{9,1... | collective-permute-start | bytes 1179656 | tf_op jit(solution)/shard_map/ppermute | solution.py:29
  38.7 10.8 %collective-permute-start.7 = (bf16[2,256,256]{2,1,0:T(8,128)(2,1)S(1)}, bf16[2,256,256]{2,1,0:T(8,128)(2,1)S(1)}, u32[]{:S(2)}, u32[]{:S(2)}) collective-permute-start(bf16[2,256,256]{2,1,0:T(8,128)(2,1)S(1)} %slice.21), channel_id=1, source_target_pairs={{0,8},{8,16},{16,24},{12,4},{20,12},{28,20},{1,9},{9,17},{17,25},{... | collective-permute-start | bytes 786440 | tf_op jit(solution)/shard_map/ppermute | solution.py:177
  40.7 7.8 %copy-start.7 = (f32[6,6]{1,0:T(8,128)S(1)}, f32[6,6]{1,0:T(8,128)}, u32[]{:S(2)}) copy-start(f32[6,6]{1,0:T(8,128)} %prec_ref.1) | copy-start | bytes 436
  40.7 8.8 %collective-permute-start.10 = (bf16[1,256,256]{2,1,0:T(8,128)(2,1)S(1)}, bf16[1,256,256]{2,1,0:T(8,128)(2,1)S(1)}, u32[]{:S(2)}, u32[]{:S(2)}) collective-permute-start(bf16[1,256,256]{2,1,0:T(8,128)(2,1)S(1)} %slice_select_fusion), channel_id=1, source_target_pairs={{0,4},{8,12},{16,20},{24,28},{4,0},{12,8},{20,16},{28,24},{1,5},{9... | collective-permute-start | bytes 393224 | tf_op jit(solution)/shard_map/ppermute | solution.py:170
  53.5 3.7 %collective-permute-start.12 = (f32[3,256,256]{2,1,0:T(8,128)S(1)}, f32[3,256,256]{2,1,0:T(8,128)S(1)}, u32[]{:S(2)}, u32[]{:S(2)}) collective-permute-start(f32[3,256,256]{2,1,0:T(8,128)S(1)} %backward_last.1), channel_id=1, source_target_pairs={{0,1},{1,0},{2,3},{3,2},{4,5},{5,4},{6,7},{7,6},{8,9},{9,8},{10,11... | collective-permute-start | bytes 2359304 | tf_op jit(solution)/shard_map/ppermute | solution.py:29

commit v5 on v4

--- a/solution.py
+++ b/solution.py
@@ -333,15 +333,18 @@
     )
 
 
-def backward_prior(sizes, prec_ref, before_ref, sample_ref, *refs):
-    others, (grad_ref,) = refs[:-1], refs[-1:]
-    del before_ref
-    subtract_prior(sizes, prec_ref, sample_ref, others, grad_ref)
-
-
 def backward_next(sizes, moves, slots_ref, weights_ref, basis_ref, *refs):
     images, (before_ref, grad_ref, *scratch) = refs[: len(moves)], refs[len(moves) :]
     del before_ref
+    backward_slots(sizes, moves, slots_ref, weights_ref, basis_ref, images, grad_ref, scratch)
+
+
+def backward_last(sizes, moves, slots_ref, weights_ref, prec_ref, basis_ref, *refs):
+    parts = sizes[1] // sizes[2]
+    images, (before_ref, sample_ref, *refs) = refs[: len(moves)], refs[len(moves) :]
+    others, (grad_ref, *scratch) = refs[: parts - 1], refs[parts - 1 :]
+    del before_ref
+    subtract_prior(sizes, prec_ref, sample_ref, others, grad_ref)
     backward_slots(sizes, moves, slots_ref, weights_ref, basis_ref, images, grad_ref, scratch)
 
 
@@ -362,10 +365,10 @@
     tiles, filters = counts.shape
     sizes = (tiles, filters, local)
     kinds = kernels.shape[0]
-    early = [(1, 0), (2, 0), (2, 1)]
+    early, far_odd = [(1, 0), (2, 0), (2, 1)], (1, 1)
     early_moves = [(move, 0) for move in early]
     onward = local - local // 3
-    last_moves = [((1, 1), 0)] + ([((1, 1), onward)] if onward < local else [])
+    last_moves = [(far_odd, 0)] + ([(far_odd, onward)] if onward < local else [])
 
     def last_images(near):
         across = [relay_across(near, onward)] if onward < local else []
@@ -387,7 +390,6 @@
     cost = pl.CostEstimate(
         flops=2 * NB * 4 * side**3, bytes_accessed=8 * local * side * side, transcendentals=0
     )
-
     lines = pltpu.VMEM((2, 2 * kinds, side), jnp.float32)
 
     def slot_scratch(groups, ready):
@@ -455,7 +457,9 @@
         slot_scratch(1, jnp.bfloat16),
         {len(tables) + 1 + len(near_last): 0},
     )
-    near_resid = {move: flipped(residual, "tile", move) for move in early}
+    near_resid = {move: flipped(residual, "tile", move) for move in [*early, far_odd]}
+    late_b, residual = lax.optimization_barrier((sample_b, residual))
+    other_samples = [rotated(late_b, "filt", r) for r in range(1, parts)]
     grad, turn, *other_turns = call(
         functools.partial(backward_own, sizes, samples),
         "backward_own",
@@ -464,9 +468,6 @@
         (back, residual, scale_map, noise, *other_noise),
         slot_scratch(1, jnp.float32),
     )
-    late_b, near_resid[1, 0], grad = lax.optimization_barrier((sample_b, near_resid[1, 0], grad))
-    near_resid_last = last_images(near_resid)
-    other_samples = [rotated(late_b, "filt", r) for r in range(1, parts)]
     (grad,) = call(
         functools.partial(backward_next, sizes, early_moves),
         "backward_next",
@@ -477,22 +478,13 @@
         {len(tables) + 1 + len(early): 0},
     )
     (grad,) = call(
-        functools.partial(backward_prior, sizes),
-        "backward_prior",
-        [image_f32],
-        (prior_prec,),
-        (grad, sample, *other_samples),
-        [],
-        {1: 0},
-    )
-    (grad,) = call(
-        functools.partial(backward_next, sizes, last_moves),
+        functools.partial(backward_last, sizes, [(far_odd, 0)]),
         "backward_last",
         [image_f32],
-        tables,
-        (back, *near_resid_last, grad),
+        tables + (prior_prec,),
+        (back, near_resid[far_odd], grad, sample, *other_samples),
         slot_scratch(1, jnp.float32),
-        {len(tables) + 1 + len(near_resid_last): 0},
+        {len(tables) + 3: 0},
     )
     mean_sum = grad
     scale_sum = grad * turn

time: 58.5 us -> 57.2 us (0.978)
  the two profiles are of different devices: /device:TPU:19 before, /device:TPU:13 now
where the time goes in v5:
time: 57.2 us; the launch traced here: 56.7 us
  starting transfers between devices  23.7 us (41%)
  Pallas kernels  18.5 us (32%)
  waiting for transfers between devices  10.4 us (18%)
  other arithmetic  3.09 us (5%)
  between operations  0.87 us (2%)
    pallas_call x7, Pallas kernels, call(): pl.pallas_call(kernel, out_shape=outs, in_specs=[SMEM] * len(smem) + [VME...  18.5 us
    ppermute x8, starting transfers between devices, flipped(): return lax.ppermute(x, axis, pairs)  17.1 us
    ppermute x8, waiting for transfers between devices, flipped(): return lax.ppermute(x, axis, pairs)  8.47 us
    ppermute x3, starting transfers between devices, rotated(): lax.ppermute(x, axis, [(i, (i + by) % length) for i in range(length)])  4.52 us
    ppermute x1, starting transfers between devices, relay_onward(): return lax.ppermute(near[1, 0][:count], 'tile', pairs)  2.08 us
    ppermute x3, waiting for transfers between devices, rotated(): lax.ppermute(x, axis, [(i, (i + by) % length) for i in range(length)])  1.92 us
    convert_element_type x1, other arithmetic, body(): sample_b = sample.astype(jnp.bfloat16)  1.68 us
    broadcast_in_dim x1, other arithmetic, body(): return ((mean_sum / samples)[None], (scale_sum / samples + 1.0)[None])  1.39 us
  transfers between devices with their start and end apart: 12, of which 7 were waited for; matrix products, arithmetic and copies ran while one was open for 0% of the time, Pallas kernels for 25%

profile of v5, /device:TPU:13, one launch (start us, length us, event | category | flops | bytes accessed | tf_op | source)
XLA Modules:
  0.0 56.7 jit_solution(8638237934266708740)
XLA Ops:
  0.7 1.7 %fusion = (bf16[3,256,256]{2,1,0:T(8,128)(2,1)S(1)}, f32[3,256,256]{2,1,0:T(8,128)S(1)}) fusion(bf16[1,1,3,256,256]{4,3,2,1,0:T(8,128)(2,1)} %param.12, f32[1,3,256,256]{3,2,1,0:T(8,128)} %param.11, f32[1,3,256,256]{3,2,1,0:T(8,128)} %param.10), kind=kLoop, calls=%fused_computation.5 | loop fusion | flops 786432 | bytes 3145728 | tf_op jit(solution)/shard_map/convert_element_type | solution.py:384
  2.4 0.3 collective-permute-start
  2.7 0.0 collective-permute-start.2
  2.7 4.5 %collective-permute-start.3 = (bf16[3,256,256]{2,1,0:T(8,128)(2,1)S(1)}, bf16[3,256,256]{2,1,0:T(8,128)(2,1)S(1)}, u32[]{:S(2)}, u32[]{:S(2)}) collective-permute-start(bf16[3,256,256]{2,1,0:T(8,128)(2,1)S(1)} %get-tuple-element.23.image_ref), channel_id=1, source_target_pairs={{8,16},{12,20},{16,8},{20,12},{9,17},{13,21},{17,9},{21,13},{10,18... | collective-permute-start | bytes 1179656 | tf_op jit(solution)/shard_map/ppermute | solution.py:170
  7.2 1.6 %collective-permute-start.9 = (bf16[3,256,256]{2,1,0:T(8,128)(2,1)S(1)}, bf16[3,256,256]{2,1,0:T(8,128)(2,1)S(1)}, u32[]{:S(2)}, u32[]{:S(2)}) collective-permute-start(bf16[3,256,256]{2,1,0:T(8,128)(2,1)S(1)} %bitcast.20), channel_id=1, source_target_pairs={{0,1},{1,0},{2,3},{3,2},{4,5},{5,4},{6,7},{7,6},{8,9},{9,8},{10,11... | collective-permute-start | bytes 1179656 | tf_op jit(solution)/shard_map/ppermute | solution.py:29
  8.8 2.4 %prepare.1 = (s32[16,128]{1,0:T(8,128)S(1)}, f32[16,128]{1,0:T(8,128)S(1)}, bf16[16,256,256]{2,1,0:T(8,128)(2,1)S(1)}, bf16[16,256,256]{2,1,0:T(8,128)(2,1)S(1)}) custom-call(s32[6,3,8,9]{3,2,1,0:T(8,128)S(1)} %bitcast.24, s32[8,6]{1,0:T(8,128)S(1)} %copy-done.7, bf16[6,3,8,6]{3,2,1,0:T(8,128)(2,1)S(1)} %bitcast.25, f32[16,25]{1,0:T(8,128)S(1)} %bitcast.26), custom_call_target="tpu_custom_call" | custom-call | flops 805306368 | bytes 1572864 | tf_op jit(solution)/shard_map/prepare/pallas_call | solution.py:403
  11.1 0.9 %forward_own.1.refs_3_ = f32[3,256,256]{2,1,0:T(8,128)S(1)} custom-call(s32[16,128]{1,0:T(8,128)S(1)} %get-tuple-element.14.slots_ref, f32[16,128]{1,0:T(8,128)S(1)} %get-tuple-element.15.weights_ref, bf16[16,256,256]{2,1,0:T(8,128)(2,1)S(1)} %get-tuple-element.17.basis_ref, bf16[3,256,256]{2,1,0:T(8,128)(2,1)S(1)} %get-tuple-element.23.image_ref), custom_call_target="tpu_custom_call" | custom-call | flops 805306368 | bytes 1572864 | tf_op jit(solution)/shard_map/forward_own/pallas_call | solution.py:403
  12.0 0.4 collective-permute-done.refs_0_
  12.4 2.1 %collective-permute-start.1 = (bf16[2,256,256]{2,1,0:T(8,128)(2,1)S(1)}, bf16[2,256,256]{2,1,0:T(8,128)(2,1)S(1)}, u32[]{:S(2)}, u32[]{:S(2)}) collective-permute-start(bf16[2,256,256]{2,1,0:T(8,128)(2,1)S(1)} %slice.9), channel_id=1, source_target_pairs={{0,8},{8,16},{16,24},{12,4},{20,12},{28,20},{1,9},{9,17},{17,25},{... | collective-permute-start | bytes 786440 | tf_op jit(solution)/shard_map/ppermute | solution.py:177
  14.5 0.0 collective-permute-done.2.refs_1_
  14.5 0.8 %collective-permute-done.3.refs_2_ = bf16[3,256,256]{2,1,0:T(8,128)(2,1)S(1)} collective-permute-done((bf16[3,256,256]{2,1,0:T(8,128)(2,1)S(1)}, bf16[3,256,256]{2,1,0:T(8,128)(2,1)S(1)}, u32[]{:S(2)}, u32[]{:S(2)}) %collective-permute-start.3) | collective-permute-done | bytes 393248 | tf_op jit(solution)/shard_map/ppermute | solution.py:170
  15.4 0.0 copy-start.1
  15.4 0.0 copy-start.2
  15.4 1.9 %collective-permute-start.4 = (bf16[1,256,256]{2,1,0:T(8,128)(2,1)S(1)}, bf16[1,256,256]{2,1,0:T(8,128)(2,1)S(1)}, u32[]{:S(2)}, u32[]{:S(2)}) collective-permute-start(bf16[1,256,256]{2,1,0:T(8,128)(2,1)S(1)} %slice_select_fusion), channel_id=1, source_target_pairs={{0,4},{8,12},{16,20},{24,28},{4,0},{12,8},{20,16},{28,24},{1,5},{9... | collective-permute-start | bytes 393224 | tf_op jit(solution)/shard_map/ppermute | solution.py:170
  17.3 3.7 %forward_next.1.refs_2_ = f32[3,256,256]{2,1,0:T(8,128)S(1)} custom-call(s32[16,128]{1,0:T(8,128)S(1)} %get-tuple-element.14.slots_ref, f32[16,128]{1,0:T(8,128)S(1)} %get-tuple-element.15.weights_ref, bf16[16,256,256]{2,1,0:T(8,128)(2,1)S(1)} %get-tuple-element.17.basis_ref, ...), custom_call_target="tpu_custom_call", output_to_operand_aliasing={{}: (6, {})} | custom-call | flops 805306368 | bytes 1572864 | tf_op jit(solution)/shard_map/forward_next/pallas_call | solution.py:403
  21.1 0.0 copy-start.8
  21.1 1.0 %forward_last.1 = (f32[3,256,256]{2,1,0:T(8,128)S(1)}, bf16[3,256,256]{2,1,0:T(8,128)(2,1)S(1)}) custom-call(s32[16,128]{1,0:T(8,128)S(1)} %get-tuple-element.14.slots_ref, f32[16,128]{1,0:T(8,128)S(1)} %get-tuple-element.15.weights_ref, bf16[16,256,256]{2,1,0:T(8,128)(2,1)S(1)} %get-tuple-element.17.basis_ref, ...), custom_call_target="tpu_custom_call", output_to_operand_aliasing={{0}: (5, {})} | custom-call | flops 805306368 | bytes 1572864 | tf_op jit(solution)/shard_map/forward_last/pallas_call | solution.py:403
  22.1 5.1 %collective-permute-start.6 = (bf16[3,256,256]{2,1,0:T(8,128)(2,1)S(1)}, bf16[3,256,256]{2,1,0:T(8,128)(2,1)S(1)}, u32[]{:S(2)}, u32[]{:S(2)}) collective-permute-start(bf16[3,256,256]{2,1,0:T(8,128)(2,1)S(1)} %get-tuple-element.21.image_ref), channel_id=1, source_target_pairs={{0,4},{8,12},{16,20},{24,28},{4,0},{12,8},{20,16},{28,24},{1,5},{9... | collective-permute-start | bytes 1179656 | tf_op jit(solution)/shard_map/ppermute | solution.py:170
  27.2 3.4 %collective-permute-start.8 = (bf16[3,256,256]{2,1,0:T(8,128)(2,1)S(1)}, bf16[3,256,256]{2,1,0:T(8,128)(2,1)S(1)}, u32[]{:S(2)}, u32[]{:S(2)}) collective-permute-start(bf16[3,256,256]{2,1,0:T(8,128)(2,1)S(1)} %get-tuple-element.21.image_ref), channel_id=1, source_target_pairs={{8,16},{12,20},{16,8},{20,12},{9,17},{13,21},{17,9},{21,13},{10,18... | collective-permute-start | bytes 1179656 | tf_op jit(solution)/shard_map/ppermute | solution.py:170
  30.6 1.9 %collective-permute-start.5 = (bf16[3,256,256]{2,1,0:T(8,128)(2,1)S(1)}, bf16[3,256,256]{2,1,0:T(8,128)(2,1)S(1)}, u32[]{:S(2)}, u32[]{:S(2)}) collective-permute-start(bf16[3,256,256]{2,1,0:T(8,128)(2,1)S(1)} %get-tuple-element.21.image_ref), channel_id=1, source_target_pairs={{4,8},{12,16},{20,24},{8,4},{16,12},{24,20},{5,9},{13,17},{21,25},... | collective-permute-start | bytes 1179656 | tf_op jit(solution)/shard_map/ppermute | solution.py:170
  32.5 1.1 %collective-permute-start.10 = (bf16[3,256,256]{2,1,0:T(8,128)(2,1)S(1)}, bf16[3,256,256]{2,1,0:T(8,128)(2,1)S(1)}, u32[]{:S(2)}, u32[]{:S(2)}) collective-permute-start(bf16[3,256,256]{2,1,0:T(8,128)(2,1)S(1)} %get-tuple-element.23.image_ref), channel_id=1, source_target_pairs={{0,2},{2,0},{1,3},{3,1},{4,6},{6,4},{5,7},{7,5},{8,10},{10,8},{9,1... | collective-permute-start | bytes 1179656 | tf_op jit(solution)/shard_map/ppermute | solution.py:29
  33.6 0.1 exponential_bitcast_fusion.refs_0_
  33.7 1.0 %backward_own.1 = (f32[3,256,256]{2,1,0:T(8,128)S(1)}, f32[3,256,256]{2,1,0:T(8,128)S(1)}, f32[3,256,256]{2,1,0:T(8,128)S(1)}) custom-call(s32[16,128]{1,0:T(8,128)S(1)} %get-tuple-element.14.slots_ref, f32[16,128]{1,0:T(8,128)S(1)} %get-tuple-element.15.weights_ref, bf16[16,256,256]{2,1,0:T(8,128)(2,1)S(1)} %get-tuple-element.16.basis_ref, ...), custom_call_target="tpu_custom_call" | custom-call | flops 805306368 | bytes 1572864 | tf_op jit(solution)/shard_map/backward_own/pallas_call | solution.py:403
  34.7 1.1 %collective-permute-done.6.refs_0_ = bf16[3,256,256]{2,1,0:T(8,128)(2,1)S(1)} collective-permute-done((bf16[3,256,256]{2,1,0:T(8,128)(2,1)S(1)}, bf16[3,256,256]{2,1,0:T(8,128)(2,1)S(1)}, u32[]{:S(2)}, u32[]{:S(2)}) %collective-permute-start.6) | collective-permute-done | bytes 393248 | tf_op jit(solution)/shard_map/ppermute | solution.py:170
  35.8 0.8 %collective-permute-done.7.refs_1_ = bf16[3,256,256]{2,1,0:T(8,128)(2,1)S(1)} collective-permute-done((bf16[3,256,256]{2,1,0:T(8,128)(2,1)S(1)}, bf16[3,256,256]{2,1,0:T(8,128)(2,1)S(1)}, u32[]{:S(2)}, u32[]{:S(2)}) %collective-permute-start.7) | collective-permute-done | bytes 393248 | tf_op jit(solution)/shard_map/ppermute | solution.py:170
  36.7 1.9 %collective-permute-done.8.refs_2_ = bf16[3,256,256]{2,1,0:T(8,128)(2,1)S(1)} collective-permute-done((bf16[3,256,256]{2,1,0:T(8,128)(2,1)S(1)}, bf16[3,256,256]{2,1,0:T(8,128)(2,1)S(1)}, u32[]{:S(2)}, u32[]{:S(2)}) %collective-permute-start.8) | collective-permute-done | bytes 393248 | tf_op jit(solution)/shard_map/ppermute | solution.py:170
  38.6 5.1 %backward_next.1.refs_1_ = f32[3,256,256]{2,1,0:T(8,128)S(1)} custom-call(s32[16,128]{1,0:T(8,128)S(1)} %get-tuple-element.14.slots_ref, f32[16,128]{1,0:T(8,128)S(1)} %get-tuple-element.15.weights_ref, bf16[16,256,256]{2,1,0:T(8,128)(2,1)S(1)} %get-tuple-element.16.basis_ref, ...), custom_call_target="tpu_custom_call", output_to_operand_aliasing={{}: (6, {})} | custom-call | flops 805306368 | bytes 1572864 | tf_op jit(solution)/shard_map/backward_next/pallas_call | solution.py:403
  43.7 3.4 %collective-permute-done.5.refs_0_ = bf16[3,256,256]{2,1,0:T(8,128)(2,1)S(1)} collective-permute-done((bf16[3,256,256]{2,1,0:T(8,128)(2,1)S(1)}, bf16[3,256,256]{2,1,0:T(8,128)(2,1)S(1)}, u32[]{:S(2)}, u32[]{:S(2)}) %collective-permute-start.5) | collective-permute-done | bytes 393248 | tf_op jit(solution)/shard_map/ppermute | solution.py:170
  47.0 4.4 %backward_last.1 = f32[3,256,256]{2,1,0:T(8,128)S(1)} custom-call(s32[16,128]{1,0:T(8,128)S(1)} %get-tuple-element.14.slots_ref, f32[16,128]{1,0:T(8,128)S(1)} %get-tuple-element.15.weights_ref, f32[6,6]{1,0:T(8,128)S(1)} %copy-done.3, bf16[16,256,256]{2,1,0:T(8,128)(2,1)S(1)} %get-tuple-element.16.basis_ref, ...), custom_call_target="tpu_custom_call", output_to_operand_aliasing={{}: (5, {})} | custom-call | flops 805306368 | bytes 1572864 | tf_op jit(solution)/shard_map/backward_last/pallas_call | solution.py:403
  51.5 1.9 %collective-permute-start.11 = (f32[3,256,256]{2,1,0:T(8,128)S(1)}, f32[3,256,256]{2,1,0:T(8,128)S(1)}, u32[]{:S(2)}, u32[]{:S(2)}) collective-permute-start(f32[3,256,256]{2,1,0:T(8,128)S(1)} %backward_last.1), channel_id=1, source_target_pairs={{0,1},{1,0},{2,3},{3,2},{4,5},{5,4},{6,7},{7,6},{8,9},{9,8},{10,11... | collective-permute-start | bytes 2359304 | tf_op jit(solution)/shard_map/ppermute | solution.py:29
  53.4 1.9 %collective-permute-done.11 = f32[3,256,256]{2,1,0:T(8,128)S(1)} collective-permute-done((f32[3,256,256]{2,1,0:T(8,128)S(1)}, f32[3,256,256]{2,1,0:T(8,128)S(1)}, u32[]{:S(2)}, u32[]{:S(2)}) %collective-permute-start.11) | collective-permute-done | bytes 786464 | tf_op jit(solution)/shard_map/ppermute | solution.py:29
  55.3 1.4 %add_bitcast_fusion = (f32[1,3,256,256]{3,2,1,0:T(8,128)}, f32[1,3,256,256]{3,2,1,0:T(8,128)}) fusion(f32[3,256,256]{2,1,0:T(8,128)S(1)} %collective-permute-done.11, f32[3,256,256]{2,1,0:T(8,128)S(1)} %get-tuple-element.25, f32[3,256,256]{2,1,0:T(8,128)S(1)} %backward_last.1, f32[3,256,256]{2,1,0:T(8,128)S(1)} %get-tuple-element.24), kind=kLoop, calls=%fused_computation.1 | loop fusion | flops 1376256 | bytes 4718592 | tf_op jit(solution)/shard_map/broadcast_in_dim | solution.py:495
  (22 shorter events, 0.1 us)
Async XLA Ops:
  0.6 6.5 %copy-start = (bf16[1,1,3,256,256]{4,3,2,1,0:T(8,128)(2,1)S(1)}, bf16[1,1,3,256,256]{4,3,2,1,0:T(8,128)(2,1)}, u32[]{:S(2)}) copy-start(bf16[1,1,3,256,256]{4,3,2,1,0:T(8,128)(2,1)} %param.12) | copy-start | bytes 1179652
  0.6 8.1 %copy-start.4 = (s32[8,6,3,9]{3,0,2,1:T(8,128)S(1)}, s32[8,6,3,9]{3,0,2,1:T(8,128)}, u32[]{:S(2)}) copy-start(s32[8,6,3,9]{3,0,2,1:T(8,128)} %param.15) | copy-start | bytes 15556
  0.7 8.1 %copy-start.5 = (bf16[8,6,6,3]{2,0,3,1:T(8,128)(2,1)S(1)}, bf16[8,6,6,3]{2,0,3,1:T(8,128)(2,1)}, u32[]{:S(2)}) copy-start(bf16[8,6,6,3]{2,0,3,1:T(8,128)(2,1)} %param.18) | copy-start | bytes 5188
  0.7 8.1 %copy-start.6 = (f32[8,2,25]{2,1,0:T(2,128)S(1)}, f32[8,2,25]{2,1,0:T(2,128)}, u32[]{:S(2)}) copy-start(f32[8,2,25]{2,1,0:T(2,128)} %param.17) | copy-start | bytes 4804
  0.7 8.1 %copy-start.7 = (s32[8,6]{1,0:T(8,128)S(1)}, s32[8,6]{1,0:T(8,128)}, u32[]{:S(2)}) copy-start(s32[8,6]{1,0:T(8,128)} %counts_ref.1) | copy-start | bytes 580
  2.4 10.0 %collective-permute-start = (bf16[3,256,256]{2,1,0:T(8,128)(2,1)S(1)}, bf16[3,256,256]{2,1,0:T(8,128)(2,1)S(1)}, u32[]{:S(2)}, u32[]{:S(2)}) collective-permute-start(bf16[3,256,256]{2,1,0:T(8,128)(2,1)S(1)} %get-tuple-element.23.image_ref), channel_id=1, source_target_pairs={{0,4},{8,12},{16,20},{24,28},{4,0},{12,8},{20,16},{28,24},{1,5},{9... | collective-permute-start | bytes 1179656 | tf_op jit(solution)/shard_map/ppermute | solution.py:170
  2.7 11.9 %collective-permute-start.2 = (bf16[3,256,256]{2,1,0:T(8,128)(2,1)S(1)}, bf16[3,256,256]{2,1,0:T(8,128)(2,1)S(1)}, u32[]{:S(2)}, u32[]{:S(2)}) collective-permute-start(bf16[3,256,256]{2,1,0:T(8,128)(2,1)S(1)} %get-tuple-element.23.image_ref), channel_id=1, source_target_pairs={{0,8},{4,12},{16,24},{20,28},{8,0},{12,4},{24,16},{28,20},{1,9},{5... | collective-permute-start | bytes 1179656 | tf_op jit(solution)/shard_map/ppermute | solution.py:170
  2.7 12.7 %collective-permute-start.3 = (bf16[3,256,256]{2,1,0:T(8,128)(2,1)S(1)}, bf16[3,256,256]{2,1,0:T(8,128)(2,1)S(1)}, u32[]{:S(2)}, u32[]{:S(2)}) collective-permute-start(bf16[3,256,256]{2,1,0:T(8,128)(2,1)S(1)} %get-tuple-element.23.image_ref), channel_id=1, source_target_pairs={{8,16},{12,20},{16,8},{20,12},{9,17},{13,21},{17,9},{21,13},{10,18... | collective-permute-start | bytes 1179656 | tf_op jit(solution)/shard_map/ppermute | solution.py:170
  7.2 25.3 %collective-permute-start.9 = (bf16[3,256,256]{2,1,0:T(8,128)(2,1)S(1)}, bf16[3,256,256]{2,1,0:T(8,128)(2,1)S(1)}, u32[]{:S(2)}, u32[]{:S(2)}) collective-permute-start(bf16[3,256,256]{2,1,0:T(8,128)(2,1)S(1)} %bitcast.20), channel_id=1, source_target_pairs={{0,1},{1,0},{2,3},{3,2},{4,5},{5,4},{6,7},{7,6},{8,9},{9,8},{10,11... | collective-permute-start | bytes 1179656 | tf_op jit(solution)/shard_map/ppermute | solution.py:29
  12.4 8.7 %collective-permute-start.1 = (bf16[2,256,256]{2,1,0:T(8,128)(2,1)S(1)}, bf16[2,256,256]{2,1,0:T(8,128)(2,1)S(1)}, u32[]{:S(2)}, u32[]{:S(2)}) collective-permute-start(bf16[2,256,256]{2,1,0:T(8,128)(2,1)S(1)} %slice.9), channel_id=1, source_target_pairs={{0,8},{8,16},{16,24},{12,4},{20,12},{28,20},{1,9},{9,17},{17,25},{... | collective-permute-start | bytes 786440 | tf_op jit(solution)/shard_map/ppermute | solution.py:177
  15.4 5.7 %copy-start.1 = (bf16[1,3,256,256]{3,2,1,0:T(8,128)(2,1)S(1)}, bf16[1,3,256,256]{3,2,1,0:T(8,128)(2,1)}, u32[]{:S(2)}) copy-start(bf16[1,3,256,256]{3,2,1,0:T(8,128)(2,1)} %param.13) | copy-start | bytes 1179652
  15.4 5.7 %copy-start.2 = (bf16[1,3,256,256]{3,2,1,0:T(8,128)(2,1)S(1)}, bf16[1,3,256,256]{3,2,1,0:T(8,128)(2,1)}, u32[]{:S(2)}) copy-start(bf16[1,3,256,256]{3,2,1,0:T(8,128)(2,1)} %param.14) | copy-start | bytes 1179652
  15.4 5.7 %collective-permute-start.4 = (bf16[1,256,256]{2,1,0:T(8,128)(2,1)S(1)}, bf16[1,256,256]{2,1,0:T(8,128)(2,1)S(1)}, u32[]{:S(2)}, u32[]{:S(2)}) collective-permute-start(bf16[1,256,256]{2,1,0:T(8,128)(2,1)S(1)} %slice_select_fusion), channel_id=1, source_target_pairs={{0,4},{8,12},{16,20},{24,28},{4,0},{12,8},{20,16},{28,24},{1,5},{9... | collective-permute-start | bytes 393224 | tf_op jit(solution)/shard_map/ppermute | solution.py:170
  21.1 12.5 %copy-start.8 = (f32[1,3,256,256]{3,2,1,0:T(8,128)S(1)}, f32[1,3,256,256]{3,2,1,0:T(8,128)}, u32[]{:S(2)}) copy-start(f32[1,3,256,256]{3,2,1,0:T(8,128)} %param.11) | copy-start | bytes 2359300
  22.1 13.7 %collective-permute-start.6 = (bf16[3,256,256]{2,1,0:T(8,128)(2,1)S(1)}, bf16[3,256,256]{2,1,0:T(8,128)(2,1)S(1)}, u32[]{:S(2)}, u32[]{:S(2)}) collective-permute-start(bf16[3,256,256]{2,1,0:T(8,128)(2,1)S(1)} %get-tuple-element.21.image_ref), channel_id=1, source_target_pairs={{0,4},{8,12},{16,20},{24,28},{4,0},{12,8},{20,16},{28,24},{1,5},{9... | collective-permute-start | bytes 1179656 | tf_op jit(solution)/shard_map/ppermute | solution.py:170
  27.2 9.5 %collective-permute-start.7 = (bf16[3,256,256]{2,1,0:T(8,128)(2,1)S(1)}, bf16[3,256,256]{2,1,0:T(8,128)(2,1)S(1)}, u32[]{:S(2)}, u32[]{:S(2)}) collective-permute-start(bf16[3,256,256]{2,1,0:T(8,128)(2,1)S(1)} %get-tuple-element.21.image_ref), channel_id=1, source_target_pairs={{0,8},{4,12},{16,24},{20,28},{8,0},{12,4},{24,16},{28,20},{1,9},{5... | collective-permute-start | bytes 1179656 | tf_op jit(solution)/shard_map/ppermute | solution.py:170
  27.2 11.4 %collective-permute-start.8 = (bf16[3,256,256]{2,1,0:T(8,128)(2,1)S(1)}, bf16[3,256,256]{2,1,0:T(8,128)(2,1)S(1)}, u32[]{:S(2)}, u32[]{:S(2)}) collective-permute-start(bf16[3,256,256]{2,1,0:T(8,128)(2,1)S(1)} %get-tuple-element.21.image_ref), channel_id=1, source_target_pairs={{8,16},{12,20},{16,8},{20,12},{9,17},{13,21},{17,9},{21,13},{10,18... | collective-permute-start | bytes 1179656 | tf_op jit(solution)/shard_map/ppermute | solution.py:170
  30.6 16.5 %collective-permute-start.5 = (bf16[3,256,256]{2,1,0:T(8,128)(2,1)S(1)}, bf16[3,256,256]{2,1,0:T(8,128)(2,1)S(1)}, u32[]{:S(2)}, u32[]{:S(2)}) collective-permute-start(bf16[3,256,256]{2,1,0:T(8,128)(2,1)S(1)} %get-tuple-element.21.image_ref), channel_id=1, source_target_pairs={{4,8},{12,16},{20,24},{8,4},{16,12},{24,20},{5,9},{13,17},{21,25},... | collective-permute-start | bytes 1179656 | tf_op jit(solution)/shard_map/ppermute | solution.py:170
  32.5 11.2 %collective-permute-start.10 = (bf16[3,256,256]{2,1,0:T(8,128)(2,1)S(1)}, bf16[3,256,256]{2,1,0:T(8,128)(2,1)S(1)}, u32[]{:S(2)}, u32[]{:S(2)}) collective-permute-start(bf16[3,256,256]{2,1,0:T(8,128)(2,1)S(1)} %get-tuple-element.23.image_ref), channel_id=1, source_target_pairs={{0,2},{2,0},{1,3},{3,1},{4,6},{6,4},{5,7},{7,5},{8,10},{10,8},{9,1... | collective-permute-start | bytes 1179656 | tf_op jit(solution)/shard_map/ppermute | solution.py:29
  38.6 8.5 %copy-start.3 = (f32[6,6]{1,0:T(8,128)S(1)}, f32[6,6]{1,0:T(8,128)}, u32[]{:S(2)}) copy-start(f32[6,6]{1,0:T(8,128)} %prec_ref.1) | copy-start | bytes 436
  51.5 3.8 %collective-permute-start.11 = (f32[3,256,256]{2,1,0:T(8,128)S(1)}, f32[3,256,256]{2,1,0:T(8,128)S(1)}, u32[]{:S(2)}, u32[]{:S(2)}) collective-permute-start(f32[3,256,256]{2,1,0:T(8,128)S(1)} %backward_last.1), channel_id=1, source_target_pairs={{0,1},{1,0},{2,3},{3,2},{4,5},{5,4},{6,7},{7,6},{8,9},{9,8},{10,11... | collective-permute-start | bytes 2359304 | tf_op jit(solution)/shard_map/ppermute | solution.py:29
